TPU v7x, 128 devices: a whole 4x4x4 slice. The times are simulated.
128 devices in a mesh: seq: 32 (over y, x_hi, z), head: 4 (over x_lo, core).
Axes of the slice: x: 4 (x_hi: 2, x_lo: 2; x = x_hi * 2 + x_lo), y: 4, z: 4, core: 2. Of those that a mesh axis runs over, the one named last changes fastest.
Arguments:
- hidden_in: bfloat16 [16384, 2048], P('seq'), may hold values from -6 to 6
- norm_gain_attn: bfloat16 [2048], P('seq'), may hold values from 0.099609375 to 1.8984375
- w_query: bfloat16 [2048, 2048], P('seq', 'head'), may hold values from -0.25 to 0.25
- w_key: bfloat16 [2048, 2048], P('seq', 'head'), may hold values from -0.125 to 0.125
- w_value: bfloat16 [2048, 2048], P('seq', 'head'), may hold values from -0.125 to 0.125
- w_out: bfloat16 [2048, 2048], P('head', 'seq'), may hold values from -0.5 to 0.5
- norm_gain_mlp: bfloat16 [2048], P('seq'), may hold values from 0.099609375 to 1.8984375
- w_gate: bfloat16 [2048, 5504], P('seq', 'head'), may hold values from -0.125 to 0.125
- w_up: bfloat16 [2048, 5504], P('seq', 'head'), may hold values from -0.125 to 0.125
- w_down: bfloat16 [5504, 2048], P('head', 'seq'), may hold values from -0.078125 to 0.078125
- lengths: int32 [3], replicated, may hold values from 1 to 15872, as said below
- cotangent: bfloat16 [16384, 2048], P('seq'), may hold values from -6 to 6
Outputs:
- output: bfloat16 [16384, 2048], P('seq')
- input_grad: bfloat16 [16384, 2048], P('seq')
- grad_gain_attn: float32 [2048], P('seq')
- grad_query: float32 [2048, 2048], P('seq', 'head')
- grad_key: float32 [2048, 2048], P('seq', 'head')
- grad_value: float32 [2048, 2048], P('seq', 'head')
- grad_out: float32 [2048, 2048], P('head', 'seq')
- grad_gain_mlp: float32 [2048], P('seq')
- grad_gate: float32 [2048, 5504], P('seq', 'head')
- grad_up: float32 [2048, 5504], P('seq', 'head')
- grad_down: float32 [5504, 2048], P('head', 'seq')
Inputs may be any that keep to these rules, and one draw needn't show every extreme that they name: The lengths sum to 16384; the middle one is 15872 and the outer two add up to 512.
All inputs are finite; a program needn't handle non-finite values.
Results may differ from a plain program's by a relative error of at most 0.029.
Values may be sent and summed in bfloat16 or wider, within the bound.
A program may use at most 192 MiB of HBM per device.

v0:
```python
import jax
import jax.numpy as jnp
from jax import lax
from jax.sharding import PartitionSpec as P

HEAD_DIM = 128
WINDOW = 64


epsilon = 1e-05
masked_score = -1e30


def shifted(value, axis, steps):
    count = lax.axis_size(axis)
    leading, last = (max(0, -steps), min(count, count - steps))
    return lax.ppermute(value, axis, [(source, source + steps) for source in range(leading, last)])


def rms_scale(values, gain):
    return values * lax.rsqrt(jnp.mean(values * values, axis=-1, keepdims=True) + epsilon) * gain


def dot_plain(left, right):
    return jnp.dot(left, right, preferred_element_type=jnp.float32)


def dot_right_turned(left, right):
    return lax.dot_general(
        left, right, (((1,), (1,)), ((), ())), preferred_element_type=jnp.float32
    )


def dot_left_turned(left, right):
    return lax.dot_general(
        left, right, (((0,), (0,)), ((), ())), preferred_element_type=jnp.float32
    )


def band_blocks(array):
    shaped = array.reshape((array.shape[0] // WINDOW, WINDOW) + array.shape[1:])
    return jnp.concatenate([shaped[:-1], shaped[1:]], axis=1)


def fold_blocks(blocks):
    lower = jnp.pad(blocks[:, :WINDOW], ((0, 1), (0, 0), (0, 0), (0, 0)))
    upper = jnp.pad(blocks[:, WINDOW:], ((1, 0), (0, 0), (0, 0), (0, 0)))
    total = lower + upper
    return total.reshape(total.shape[0] * WINDOW, total.shape[2] * total.shape[3])


def visibility(start, count, lengths):
    positions = start - WINDOW + jnp.arange((count + 1) * WINDOW, dtype=jnp.int32)
    ends = jnp.cumsum(lengths)
    segment = jnp.sum((positions[None, :] >= ends[:, None]).astype(jnp.int32), axis=0)
    key_pos = band_blocks(positions)
    key_seg = band_blocks(segment)
    query_pos = positions[WINDOW:].reshape(count, WINDOW)
    query_seg = segment[WINDOW:].reshape(count, WINDOW)
    visible = (key_pos[:, None, :] <= query_pos[:, :, None]) & (
        key_pos[:, None, :] > query_pos[:, :, None] - WINDOW
    )
    return visible & (key_pos[:, None, :] >= 0) & (key_seg[:, None, :] == query_seg[:, :, None])


def score_blocks(query_blocks, key_blocks, visible):
    scores = jnp.einsum(
        "bqhd,bkhd->bhqk", query_blocks, key_blocks, preferred_element_type=jnp.float32
    ) * HEAD_DIM ** (-0.5)
    return jnp.where(visible[:, None], scores, masked_score)


def attend(query_blocks, key_blocks, value_blocks, visible):
    scores = score_blocks(query_blocks, key_blocks, visible)
    highest = jnp.max(scores, axis=-1, keepdims=True)
    expo = jnp.exp(scores - highest)
    total = jnp.sum(expo, axis=-1, keepdims=True)
    probs = (expo / total).astype(jnp.bfloat16)
    mixed = jnp.einsum("bhqk,bkhd->bqhd", probs, value_blocks, preferred_element_type=jnp.float32)
    rows_here = mixed.shape[0] * mixed.shape[1]
    return (mixed.reshape(rows_here, -1).astype(jnp.bfloat16), highest + jnp.log(total))


def attend_back(query_blocks, key_blocks, value_blocks, visible, log_total, grad_mixed):
    scores = score_blocks(query_blocks, key_blocks, visible)
    probs = jnp.exp(scores - log_total)
    probs_low = probs.astype(jnp.bfloat16)
    grad_blocks = grad_mixed.reshape(query_blocks.shape)
    grad_probs = jnp.einsum(
        "bqhd,bkhd->bhqk", grad_blocks, value_blocks, preferred_element_type=jnp.float32
    )
    inner = jnp.sum(probs * grad_probs, axis=-1, keepdims=True)
    grad_scores = (probs * (grad_probs - inner)).astype(jnp.bfloat16)
    scale = HEAD_DIM ** (-0.5)
    grad_queries = (
        jnp.einsum("bhqk,bkhd->bqhd", grad_scores, key_blocks, preferred_element_type=jnp.float32)
        * scale
    )
    grad_keys = (
        jnp.einsum("bhqk,bqhd->bkhd", grad_scores, query_blocks, preferred_element_type=jnp.float32)
        * scale
    )
    grad_values = jnp.einsum(
        "bhqk,bqhd->bkhd", probs_low, grad_blocks, preferred_element_type=jnp.float32
    )
    rows_here = grad_queries.shape[0] * grad_queries.shape[1]
    return (grad_queries.reshape(rows_here, -1), fold_blocks(grad_keys), fold_blocks(grad_values))


def swiglu(gate_in, up_in):
    return jax.nn.silu(gate_in) * up_in


def per_device(
    hidden_in,
    norm_gain_attn,
    w_query,
    w_key,
    w_value,
    w_out,
    norm_gain_mlp,
    w_gate,
    w_up,
    w_down,
    lengths,
    cotangent,
):
    tokens_here = hidden_in.shape[0]
    count = tokens_here // WINDOW
    start = lax.axis_index("seq") * tokens_here
    visible = visibility(start, count, lengths)
    gain_attn, query_w, key_w, value_w, gain_mlp, gate_w, up_w = (
        lax.all_gather(norm_gain_attn, "seq", axis=0, tiled=True),
        lax.all_gather(w_query, "seq", axis=0, tiled=True),
        lax.all_gather(w_key, "seq", axis=0, tiled=True),
        lax.all_gather(w_value, "seq", axis=0, tiled=True),
        lax.all_gather(norm_gain_mlp, "seq", axis=0, tiled=True),
        lax.all_gather(w_gate, "seq", axis=0, tiled=True),
        lax.all_gather(w_up, "seq", axis=0, tiled=True),
    )
    out_w, down_w = (
        lax.all_gather(w_out, "seq", axis=1, tiled=True),
        lax.all_gather(w_down, "seq", axis=1, tiled=True),
    )
    heads_here = query_w.shape[1] // HEAD_DIM
    gain_attn_f = gain_attn.astype(jnp.float32)
    gain_mlp_f = gain_mlp.astype(jnp.float32)
    hidden = hidden_in.astype(jnp.float32)
    normed_attn = rms_scale(hidden, gain_attn_f).astype(jnp.bfloat16)
    queries = dot_plain(normed_attn, query_w).astype(jnp.bfloat16)
    keys = dot_plain(normed_attn, key_w).astype(jnp.bfloat16)
    values = dot_plain(normed_attn, value_w).astype(jnp.bfloat16)
    tails = shifted(jnp.stack([keys[-WINDOW:], values[-WINDOW:]]), "seq", 1)
    keys_ext = jnp.concatenate([tails[0], keys])
    values_ext = jnp.concatenate([tails[1], values])
    query_blocks = queries.reshape(count, WINDOW, heads_here, HEAD_DIM)
    key_blocks = band_blocks(keys_ext).reshape(count, 2 * WINDOW, heads_here, HEAD_DIM)
    value_blocks = band_blocks(values_ext).reshape(count, 2 * WINDOW, heads_here, HEAD_DIM)
    mixed, log_total = attend(query_blocks, key_blocks, value_blocks, visible)
    branch_terms = dot_plain(mixed, out_w)
    resid = hidden + lax.psum(branch_terms, "head")
    normed_mlp = rms_scale(resid, gain_mlp_f).astype(jnp.bfloat16)
    gate = dot_plain(normed_mlp, gate_w)
    up = dot_plain(normed_mlp, up_w)
    activated = swiglu(gate, up).astype(jnp.bfloat16)
    result = resid + lax.psum(dot_plain(activated, down_w).astype(jnp.bfloat16), "head").astype(
        jnp.float32
    )
    grad_down = dot_left_turned(activated, cotangent)
    grad_act = dot_right_turned(cotangent, down_w)
    unused_act, swiglu_back = jax.vjp(swiglu, gate, up)
    grad_gate_f, grad_up_f = swiglu_back(grad_act)
    grad_gate_act = grad_gate_f.astype(jnp.bfloat16)
    grad_up_act = grad_up_f.astype(jnp.bfloat16)
    grad_gate = dot_left_turned(normed_mlp, grad_gate_act)
    grad_up = dot_left_turned(normed_mlp, grad_up_act)
    grad_normed_terms = dot_right_turned(grad_gate_act, gate_w) + dot_right_turned(
        grad_up_act, up_w
    )
    grad_normed_mlp = lax.psum(grad_normed_terms, "head")
    unused_mlp, norm_mlp_back = jax.vjp(rms_scale, resid, gain_mlp_f)
    grad_resid_norm, grad_gain_mlp = norm_mlp_back(grad_normed_mlp)
    grad_resid = cotangent.astype(jnp.float32) + grad_resid_norm
    grad_branch = grad_resid.astype(jnp.bfloat16)
    grad_out = dot_left_turned(mixed, grad_branch)
    grad_mixed = dot_right_turned(grad_branch, out_w).astype(jnp.bfloat16)
    grad_queries, grad_keys_ext, grad_values_ext = attend_back(
        query_blocks, key_blocks, value_blocks, visible, log_total, grad_mixed
    )
    returned = shifted(
        jnp.stack([grad_keys_ext[:WINDOW], grad_values_ext[:WINDOW]]).astype(jnp.bfloat16),
        "seq",
        -1,
    ).astype(jnp.float32)
    grad_keys = grad_keys_ext[WINDOW:]
    grad_values = grad_values_ext[WINDOW:]
    grad_keys = jnp.concatenate([grad_keys[:-WINDOW], grad_keys[-WINDOW:] + returned[0]])
    grad_values = jnp.concatenate([grad_values[:-WINDOW], grad_values[-WINDOW:] + returned[1]])
    grad_queries_low = grad_queries.astype(jnp.bfloat16)
    grad_keys_low = grad_keys.astype(jnp.bfloat16)
    grad_values_low = grad_values.astype(jnp.bfloat16)
    grad_query = dot_left_turned(normed_attn, grad_queries_low)
    grad_key = dot_left_turned(normed_attn, grad_keys_low)
    grad_value = dot_left_turned(normed_attn, grad_values_low)
    grad_attn_terms = (
        dot_right_turned(grad_queries_low, query_w)
        + dot_right_turned(grad_keys_low, key_w)
        + dot_right_turned(grad_values_low, value_w)
    )
    grad_normed_attn = lax.psum(grad_attn_terms.astype(jnp.bfloat16), "head").astype(jnp.float32)
    unused_attn, norm_attn_back = jax.vjp(rms_scale, hidden, gain_attn_f)
    grad_hidden_norm, grad_gain_attn = norm_attn_back(grad_normed_attn)
    grad_hidden = grad_resid + grad_hidden_norm
    summed_rows = (
        lax.psum_scatter(
            grad_gain_attn.astype(jnp.bfloat16), "seq", scatter_dimension=0, tiled=True
        ).astype(jnp.float32),
        lax.psum_scatter(
            grad_query.astype(jnp.bfloat16), "seq", scatter_dimension=0, tiled=True
        ).astype(jnp.float32),
        lax.psum_scatter(
            grad_key.astype(jnp.bfloat16), "seq", scatter_dimension=0, tiled=True
        ).astype(jnp.float32),
        lax.psum_scatter(
            grad_value.astype(jnp.bfloat16), "seq", scatter_dimension=0, tiled=True
        ).astype(jnp.float32),
        lax.psum_scatter(
            grad_gain_mlp.astype(jnp.bfloat16), "seq", scatter_dimension=0, tiled=True
        ).astype(jnp.float32),
        lax.psum_scatter(
            grad_gate.astype(jnp.bfloat16), "seq", scatter_dimension=0, tiled=True
        ).astype(jnp.float32),
        lax.psum_scatter(
            grad_up.astype(jnp.bfloat16), "seq", scatter_dimension=0, tiled=True
        ).astype(jnp.float32),
    )
    summed_cols = (
        lax.psum_scatter(
            grad_out.astype(jnp.bfloat16), "seq", scatter_dimension=1, tiled=True
        ).astype(jnp.float32),
        lax.psum_scatter(
            grad_down.astype(jnp.bfloat16), "seq", scatter_dimension=1, tiled=True
        ).astype(jnp.float32),
    )
    return (
        result.astype(jnp.bfloat16),
        grad_hidden.astype(jnp.bfloat16),
        summed_rows[0],
        summed_rows[1],
        summed_rows[2],
        summed_rows[3],
        summed_cols[0],
        summed_rows[4],
        summed_rows[5],
        summed_rows[6],
        summed_cols[1],
    )


def solution(mesh):
    placed = (
        P("seq", None),
        P("seq"),
        P("seq", "head"),
        P("seq", "head"),
        P("seq", "head"),
        P("head", "seq"),
        P("seq"),
        P("seq", "head"),
        P("seq", "head"),
        P("head", "seq"),
        P(),
        P("seq", None),
    )
    return jax.shard_map(
        per_device,
        mesh=mesh,
        in_specs=placed,
        out_specs=(
            P("seq", None),
            P("seq", None),
            P("seq"),
            P("seq", "head"),
            P("seq", "head"),
            P("seq", "head"),
            P("head", "seq"),
            P("seq"),
            P("seq", "head"),
            P("seq", "head"),
            P("head", "seq"),
        ),
        check_vma=False,
    )
```

profile of v0, /device:TPU:1, one launch (start us, length us, event | category | flops | bytes accessed | tf_op | source)
XLA Modules:
  0.0 2199.4 jit_solution(8396333241906915756)
XLA Ops:
  17.4 86.6 %all-reduce.9 = (bf16[2048]{0:T(1024)(128)(2,1)S(1)}, bf16[2048]{0:T(1024)(128)(2,1)}) all-reduce(bf16[2048]{0:T(1024)(128)(2,1)S(1)} %dynamic-update-slice, bf16[2048]{0:T(1024)(128)(2,1)S(1)} %dynamic-update-slice.1), channel_id=1, replica_groups=mesh['seq'=32,'head'=4] {'seq'}, use_global_device_ids=true, to_apply=%add.4 | all-reduce | flops 4096 | bytes 16384
  107.7 48.1 %all-gather.8.cloned.1.call-done = bf16[2048,512]{1,0:T(8,128)(2,1)} async-done(((bf16[64,512]{1,0:T(8,128)(2,1)}), bf16[2048,512]{1,0:T(8,128)(2,1)}) %all-gather.8.cloned.1.call-update) | async-done | bytes 2097168 | tf_op jit(solution)/shard_map/all_gather | solution.py:135
  161.4 66.5 %all-gather.12.cloned.1.call-done = bf16[2048,512]{1,0:T(8,128)(2,1)} async-done(((bf16[64,512]{1,0:T(8,128)(2,1)}), bf16[2048,512]{1,0:T(8,128)(2,1)}) %all-gather.12.cloned.1.call-update) | async-done | bytes 2097168 | tf_op jit(solution)/shard_map/all_gather | solution.py:134
  245.5 54.2 %all-gather.14.cloned.1.call-done = bf16[512,2048]{0,1:T(8,128)(2,1)} async-done(((bf16[512,64]{0,1:T(8,128)(2,1)}), bf16[512,2048]{0,1:T(8,128)(2,1)}) %all-gather.14.cloned.1.call-update) | async-done | bytes 2097168 | tf_op jit(solution)/shard_map/all_gather | solution.py:142
  307.2 89.2 %all-reduce.15.cloned.1.call-done = f32[512,2048]{1,0:T(8,128)} async-done(((f32[512,2048]{1,0:T(8,128)}), f32[512,2048]{1,0:T(8,128)}) %all-reduce.15.cloned.1.call-update) | async-done | bytes 4194320 | tf_op jit(solution)/shard_map/psum | solution.py:161
  403.0 86.3 %all-gather.18.cloned.1.call-done = bf16[2048,1376]{1,0:T(8,128)(2,1)} async-done(((bf16[64,1376]{1,0:T(8,128)(2,1)}), bf16[2048,1376]{1,0:T(8,128)(2,1)}) %all-gather.18.cloned.1.call-update) | async-done | bytes 5636112 | tf_op jit(solution)/shard_map/all_gather | solution.py:139
  489.3 7.9 fusion.66
  497.2 82.8 %all-gather.16.cloned.1.call-done = bf16[2048,1376]{1,0:T(8,128)(2,1)} async-done(((bf16[64,1376]{1,0:T(8,128)(2,1)}), bf16[2048,1376]{1,0:T(8,128)(2,1)}) %all-gather.16.cloned.1.call-update) | async-done | bytes 5636112 | tf_op jit(solution)/shard_map/all_gather | solution.py:138
  580.0 8.0 fusion.65
  588.1 82.7 %all-gather.20.cloned.1.call-done = bf16[1376,2048]{0,1:T(8,128)(2,1)} async-done(((bf16[1376,64]{0,1:T(8,128)(2,1)}), bf16[1376,2048]{0,1:T(8,128)(2,1)}) %all-gather.20.cloned.1.call-update) | async-done | bytes 5636112 | tf_op jit(solution)/shard_map/all_gather | solution.py:143
  670.7 10.5 multiply_convert_fusion.1
  693.1 90.2 %all-reduce.17.cloned.1.call-done = f32[512,2048]{1,0:T(8,128)} async-done(((f32[512,2048]{1,0:T(8,128)}), f32[512,2048]{1,0:T(8,128)}) %all-reduce.17.cloned.1.call-update) | async-done | bytes 4194320 | tf_op jit(solution)/shard_map/psum | solution.py:180
  830.3 8.0 convolution_convert_fusion.7
  844.3 8.0 convolution_convert_fusion
  852.6 8.0 convolution_convert_fusion.1
  869.2 91.6 %reduce-scatter.14.cloned.1.call-done = bf16[512,64]{0,1:T(8,128)(2,1)} async-done(((bf16[512,2048]{0,1:T(8,128)(2,1)}), bf16[512,64]{0,1:T(8,128)(2,1)}) %reduce-scatter.14.cloned.1.call-update) | async-done | bytes 65552 | tf_op jit(solution)/shard_map/reduce_scatter | solution.py:238
  962.3 182.1 %reduce-scatter.8.cloned.1.call-done = bf16[64,512]{1,0:T(8,128)(2,1)} async-done(((bf16[2048,512]{1,0:T(8,128)(2,1)}), bf16[64,512]{1,0:T(8,128)(2,1)}) %reduce-scatter.8.cloned.1.call-update) | async-done | bytes 65552 | tf_op jit(solution)/shard_map/reduce_scatter | solution.py:218
  1145.9 182.6 %reduce-scatter.12.cloned.1.call-done = bf16[64,512]{1,0:T(8,128)(2,1)} async-done(((bf16[2048,512]{1,0:T(8,128)(2,1)}), bf16[64,512]{1,0:T(8,128)(2,1)}) %reduce-scatter.12.cloned.1.call-update) | async-done | bytes 65552 | tf_op jit(solution)/shard_map/reduce_scatter | solution.py:224
  1330.0 183.0 %reduce-scatter.10.cloned.1.call-done = bf16[64,512]{1,0:T(8,128)(2,1)} async-done(((bf16[2048,512]{1,0:T(8,128)(2,1)}), bf16[64,512]{1,0:T(8,128)(2,1)}) %reduce-scatter.10.cloned.1.call-update) | async-done | bytes 65552 | tf_op jit(solution)/shard_map/reduce_scatter | solution.py:221
  1514.5 112.9 %all-reduce.19.cloned.1.call-done = (bf16[512,2048]{1,0:T(8,128)(2,1)}, bf16[512,2048]{1,0:T(8,128)(2,1)}) async-done(((bf16[512,2048]{1,0:T(8,128)(2,1)}, bf16[512,2048]{1,0:T(8,128)(2,1)}), (bf16[512,2048]{1,0:T(8,128)(2,1)}, bf16[512,2048]{1,0:T(8,128)(2,1)})) %all-reduce.19.cloned.1.call-update) | async-done | bytes 4194320 | tf_op jit(solution)/shard_map/psum | solution.py:166
  1630.7 86.2 %all-reduce.8 = (bf16[2048]{0:T(1024)(128)(2,1)S(1)}, bf16[2048]{0:T(1024)(128)(2,1)S(1)}) all-reduce(bf16[2048]{0:T(1024)(128)(2,1)S(1)} %get-tuple-element.13, bf16[2048]{0:T(1024)(128)(2,1)S(1)} %get-tuple-element.11), channel_id=2, replica_groups=mesh['seq'=32,'head'=4] {'seq'}, use_global_device_ids=true, to_apply=%region_14.15.clone | all-reduce | flops 4096 | bytes 16384
  1725.7 78.2 %reduce-scatter.20.cloned.1.call-done = bf16[1376,64]{0,1:T(8,128)(2,1)} async-done(((bf16[1376,2048]{0,1:T(8,128)(2,1)}), bf16[1376,64]{0,1:T(8,128)(2,1)}) %reduce-scatter.20.cloned.1.call-update) | async-done | bytes 176144 | tf_op jit(solution)/shard_map/reduce_scatter | solution.py:241
  1805.6 191.9 %reduce-scatter.18.cloned.1.call-done = bf16[64,1376]{1,0:T(8,128)(2,1)} async-done(((bf16[2048,1376]{1,0:T(8,128)(2,1)}), bf16[64,1376]{1,0:T(8,128)(2,1)}) %reduce-scatter.18.cloned.1.call-update) | async-done | bytes 176144 | tf_op jit(solution)/shard_map/reduce_scatter | solution.py:233
  1999.2 191.6 %reduce-scatter.16.cloned.1.call-done = bf16[64,1376]{1,0:T(8,128)(2,1)} async-done(((bf16[2048,1376]{1,0:T(8,128)(2,1)}), bf16[64,1376]{1,0:T(8,128)(2,1)}) %reduce-scatter.16.cloned.1.call-update) | async-done | bytes 176144 | tf_op jit(solution)/shard_map/reduce_scatter | solution.py:230
  (191 shorter events, 146.0 us)
Async XLA Ops:
  7.2 96.8 %all-gather.10.cloned.1.call-start = ((), (), s32[]{:S(2)}) async-start(), calls=%async_computation.8 | async-start | bytes 2162688 | tf_op jit(solution)/shard_map/all_gather | solution.py:136
  7.9 147.9 %all-gather.8.cloned.1.call-start = ((), (), s32[]{:S(2)}) async-start(), calls=%async_computation.7 | async-start | bytes 2162688 | tf_op jit(solution)/shard_map/all_gather | solution.py:135
  8.7 219.2 %all-gather.12.cloned.1.call-start = ((), (), s32[]{:S(2)}) async-start(), calls=%async_computation.9 | async-start | bytes 2162688 | tf_op jit(solution)/shard_map/all_gather | solution.py:134
  9.4 290.3 %all-gather.14.cloned.1.call-start = ((), (), s32[]{:S(2)}) async-start(), calls=%async_computation.10 | async-start | bytes 2162688 | tf_op jit(solution)/shard_map/all_gather | solution.py:142
  10.0 386.5 %all-reduce.15.cloned.1.call-start = ((), (), s32[]{:S(2)}) async-start(), calls=%async_computation.11 | async-start | bytes 8388608 | tf_op jit(solution)/shard_map/psum | solution.py:161
  104.0 51.8 %copy-start.4 = (bf16[512,2048]{1,0:T(8,128)(2,1)S(1)}, bf16[512,2048]{1,0:T(8,128)(2,1)}, u32[]{:S(2)}) copy-start(bf16[512,2048]{1,0:T(8,128)(2,1)} %param.12) | copy-start | bytes 6291460
  158.7 76.6 %collective-permute-start = (bf16[2,64,512]{2,1,0:T(8,128)(2,1)S(1)}, bf16[2,64,512]{2,1,0:T(8,128)(2,1)S(1)}, u32[]{:S(2)}, u32[]{:S(2)}) collective-permute-start(bf16[2,64,512]{2,1,0:T(8,128)(2,1)S(1)} %pad_maximum_fusion.8), channel_id=1, source_target_pairs={{0,4},{4,8},{8,12},{12,16},{16,20},{20,24},{24,28},{28,32},{32,36}... | collective-permute-start | bytes 393224 | tf_op jit(solution)/shard_map/ppermute | solution.py:17
  304.9 184.4 %all-gather.18.cloned.1.call-start = ((), (), s32[]{:S(2)}) async-start(), calls=%async_computation.13 | async-start | bytes 5947392 | tf_op jit(solution)/shard_map/all_gather | solution.py:139
  305.5 274.5 %all-gather.16.cloned.1.call-start = ((), (), s32[]{:S(2)}) async-start(), calls=%async_computation.12 | async-start | bytes 5947392 | tf_op jit(solution)/shard_map/all_gather | solution.py:138
  306.2 364.5 %all-gather.20.cloned.1.call-start = ((), (), s32[]{:S(2)}) async-start(), calls=%async_computation.14 | async-start | bytes 5947392 | tf_op jit(solution)/shard_map/all_gather | solution.py:143
  307.0 476.4 %all-reduce.17.cloned.1.call-start = ((), (), s32[]{:S(2)}) async-start(), calls=%async_computation.15 | async-start | bytes 8388608 | tf_op jit(solution)/shard_map/psum | solution.py:180
  670.7 10.5 copy-start.22
  693.0 267.8 %reduce-scatter.14.cloned.1.call-start = ((), (), s32[]{:S(2)}) async-start(), calls=%async_computation.19 | async-start | bytes 2162688 | tf_op jit(solution)/shard_map/reduce_scatter | solution.py:238
  783.3 5.9 copy-start.5
  796.7 347.7 %reduce-scatter.8.cloned.1.call-start = ((), (), s32[]{:S(2)}) async-start(), calls=%async_computation.16 | async-start | bytes 2162688 | tf_op jit(solution)/shard_map/reduce_scatter | solution.py:218
  811.9 516.6 %reduce-scatter.12.cloned.1.call-start = ((), (), s32[]{:S(2)}) async-start(), calls=%async_computation.18 | async-start | bytes 2162688 | tf_op jit(solution)/shard_map/reduce_scatter | solution.py:224
  816.2 7.7 collective-permute-start.1
  826.8 686.2 %reduce-scatter.10.cloned.1.call-start = ((), (), s32[]{:S(2)}) async-start(), calls=%async_computation.17 | async-start | bytes 2162688 | tf_op jit(solution)/shard_map/reduce_scatter | solution.py:221
  830.0 797.3 %all-reduce.19.cloned.1.call-start = ((), (), s32[]{:S(2)}) async-start(), calls=%async_computation.23 | async-start | bytes 8388608 | tf_op jit(solution)/shard_map/psum | solution.py:166
  830.3 8.0 copy-start.14
  830.3 8.0 copy-start.20
  844.2 959.7 %reduce-scatter.20.cloned.1.call-start = ((), (), s32[]{:S(2)}) async-start(), calls=%async_computation.22 | async-start | bytes 5947392 | tf_op jit(solution)/shard_map/reduce_scatter | solution.py:241
  852.3 1145.2 %reduce-scatter.18.cloned.1.call-start = ((), (), s32[]{:S(2)}) async-start(), calls=%async_computation.21 | async-start | bytes 5947392 | tf_op jit(solution)/shard_map/reduce_scatter | solution.py:233
  860.6 1330.2 %reduce-scatter.16.cloned.1.call-start = ((), (), s32[]{:S(2)}) async-start(), calls=%async_computation.20 | async-start | bytes 5947392 | tf_op jit(solution)/shard_map/reduce_scatter | solution.py:230
  (21 other events, 58.4 us)
Sparse Core Ops, SparseCore 0:
  11.1 72.9 all-gather.9
  87.1 68.6 all-gather.7
  158.9 68.9 all-gather.11
  230.8 68.9 all-gather.13
  305.0 91.4 all-reduce.14
  399.8 89.4 all-gather.17
  492.8 87.1 all-gather.15
  583.5 87.1 all-gather.19
  693.1 90.1 all-reduce.16
  796.8 163.9 reduce-scatter.13
  963.3 181.0 reduce-scatter.7
  1146.6 181.8 reduce-scatter.11
  1331.0 181.9 reduce-scatter.9
  1516.0 111.3 all-reduce.18
  1629.8 174.1 reduce-scatter.19
  1806.3 191.1 reduce-scatter.17
  1999.9 190.8 reduce-scatter.15
where the time goes:
time: 2230 us; the launch traced here: 2200 us
  waiting for transfers between devices  1820 us (82%)
  blocking collectives  173 us (8%)
  matrix products  115 us (5%)
  other arithmetic  41.5 us (2%)
  local copies, waits for them, and re-layouts  23.9 us (1%)
    reduce_scatter x1, waiting for transfers between devices, per_device(): lax.psum_scatter(grad_up.astype(jnp.bfloat16), 'seq', scatter_dimension=0...  192 us
    reduce_scatter x1, waiting for transfers between devices, per_device(): lax.psum_scatter(grad_gate.astype(jnp.bfloat16), 'seq', scatter_dimension...  192 us
    reduce_scatter x1, waiting for transfers between devices, per_device(): lax.psum_scatter(grad_key.astype(jnp.bfloat16), 'seq', scatter_dimension=...  183 us
    reduce_scatter x1, waiting for transfers between devices, per_device(): lax.psum_scatter(grad_value.astype(jnp.bfloat16), 'seq', scatter_dimensio...  183 us
    reduce_scatter x1, waiting for transfers between devices, per_device(): lax.psum_scatter(grad_query.astype(jnp.bfloat16), 'seq', scatter_dimensio...  182 us
    unnamed x2, blocking collectives  173 us
    psum x1, waiting for transfers between devices, per_device(): lax.psum(dot_plain(activated, down_w).astype(jnp.bfloat16), 'head')  113 us
    reduce_scatter x1, waiting for transfers between devices, per_device(): lax.psum_scatter(grad_out.astype(jnp.bfloat16), 'seq', scatter_dimension=...  91.6 us
  transfers between devices with their start and end apart: 19, of which 17 were waited for; matrix products, arithmetic and copies ran while one was open for 6% of the time, Pallas kernels for 0%

commit v1 on v0

v1 whole, which is shorter than its diff:
```python
import jax
import jax.numpy as jnp
from jax import lax
from jax.sharding import Mesh, PartitionSpec as P

HEAD_DIM = 128
WINDOW = 64
BLOCK = 512
OWNED = 128
AXES = ("y", "xh", "z", "xl", "c")
RING = ("xh", "xl")

epsilon = 1e-05
masked_score = -1e30
f32 = jnp.float32
bf16 = jnp.bfloat16


def shift(value, axis, steps):
    return lax.ppermute(value, axis, [(i, (i + steps) % 4) for i in range(4)])


def flip(value, axis):
    return lax.ppermute(value, axis, [(0, 1), (1, 0)])


def dot_plain(left, right):
    return jnp.dot(left, right, preferred_element_type=f32)


def dot_right_turned(left, right):
    return lax.dot_general(left, right, (((1,), (1,)), ((), ())), preferred_element_type=f32)


def dot_left_turned(left, right):
    return lax.dot_general(left, right, (((0,), (0,)), ((), ())), preferred_element_type=f32)


def rms_scale(values, gain):
    return values * lax.rsqrt(jnp.mean(values * values, axis=-1, keepdims=True) + epsilon) * gain


def in_order(flag, mine, other, axis):
    return jnp.where(
        flag == 0,
        jnp.concatenate([mine, other], axis=axis),
        jnp.concatenate([other, mine], axis=axis),
    )


def pick(array, axis, index):
    return lax.dynamic_slice_in_dim(array, index, 1, axis)


def place(pieces, axis, index):
    shape = list(pieces[0].shape)
    shape[axis] = 4
    total = jnp.zeros(shape, pieces[0].dtype)
    for k, piece in enumerate(pieces):
        total = lax.dynamic_update_slice_in_dim(total, piece, (index + k) % 4, axis)
    return total


def gather4(block, mesh_axis, axis, split):
    index = lax.axis_index(mesh_axis)
    before = shift(block, mesh_axis, 1)
    after = shift(block, mesh_axis, -1)
    half = block.shape[split] // 2
    far = jnp.concatenate(
        [
            shift(lax.slice_in_dim(before, 0, half, axis=split), mesh_axis, 1),
            shift(lax.slice_in_dim(after, half, 2 * half, axis=split), mesh_axis, -1),
        ],
        axis=split,
    )
    return place([block, after, far, before], axis, index)


def reduce4(total, mesh_axis, axis, split):
    index = lax.axis_index(mesh_axis)
    half = total.shape[split] // 2
    own, nxt, far, prev = [pick(total, axis, (index + k) % 4) for k in range(4)]
    low = lambda a: lax.slice_in_dim(a, 0, half, axis=split)
    high = lambda a: lax.slice_in_dim(a, half, 2 * half, axis=split)
    add = lambda a, b: (a.astype(f32) + b.astype(f32)).astype(bf16)
    from_prev = shift(low(far), mesh_axis, 1)
    from_next = shift(high(far), mesh_axis, -1)
    from_prev_own = shift(high(nxt), mesh_axis, 1)
    from_next_own = shift(low(prev), mesh_axis, -1)
    from_prev_sum = shift(add(low(nxt), from_prev), mesh_axis, 1)
    from_next_sum = shift(add(high(prev), from_next), mesh_axis, -1)
    got_prev = jnp.concatenate([from_prev_sum, from_prev_own], axis=split)
    got_next = jnp.concatenate([from_next_own, from_next_sum], axis=split)
    return (own.astype(f32) + got_prev.astype(f32) + got_next.astype(f32)).astype(bf16)


def gather_weights(pack):
    cols = pack.shape[2]
    cut = cols // 256 * 128
    a = pack[None, :, None, :, :cut]
    b = pack[None, :, None, :, cut:]
    a = gather4(gather4(a, "z", 2, 3), "y", 0, 3)
    b = gather4(gather4(b, "y", 0, 3), "z", 2, 3)
    return a.reshape(2048, cut), b.reshape(2048, cols - cut)


def reduce_weights(a, b):
    a = a.reshape(4, 2, 4, 64, a.shape[1])
    b = b.reshape(4, 2, 4, 64, b.shape[1])
    a = reduce4(reduce4(a, "y", 0, 3), "z", 2, 3)
    b = reduce4(reduce4(b, "z", 2, 3), "y", 0, 3)
    return jnp.concatenate([a[0, :, 0], b[0, :, 0]], axis=2)


def gather_block(value):
    c = lax.axis_index("c")
    part = lax.dynamic_slice_in_dim(value, c * 256, 256, 0)
    got = lax.ppermute(part, RING, [(i, 3 - i) for i in range(4)])
    other = in_order(c, got, flip(got, "c"), 0)
    return in_order(lax.axis_index("xh"), value, other, 0)


def reduce_group(total):
    c = lax.axis_index("c")
    x = lax.axis_index(RING)
    parts = total.reshape(4, 2, OWNED, 2048)
    mine = pick(parts, 1, c)[:, 0]
    theirs = pick(parts, 1, 1 - c)[:, 0].astype(bf16)
    mine = mine + flip(theirs, "c").astype(f32)
    low = mine.astype(bf16)
    result = pick(mine, 0, x)[0]
    for k in (1, 3, 2):
        result = result + shift(pick(low, 0, (x + k) % 4)[0], RING, k).astype(f32)
    return result


def gather_group(owned):
    c = lax.axis_index("c")
    x = lax.axis_index(RING)
    mine = owned[None]
    pieces = [mine, shift(mine, RING, -1), shift(mine, RING, 2), shift(mine, RING, 1)]
    half = place(pieces, 0, x)[:, None]
    return in_order(c, half, flip(half, "c"), 1).reshape(1024, 2048)


def gather_owned(owned):
    pair = in_order(lax.axis_index("xl"), owned[None], flip(owned, "xl")[None], 0)[:, None]
    return in_order(lax.axis_index("c"), pair, flip(pair, "c"), 1).reshape(BLOCK, 2048)


def band_blocks(array):
    shaped = array.reshape((2, 9, WINDOW) + array.shape[2:])
    both = jnp.concatenate([shaped[:, :-1], shaped[:, 1:]], axis=2)
    return both.reshape((16, 2 * WINDOW) + array.shape[2:])


def fold_blocks(blocks):
    shaped = blocks.reshape(2, 8, 2, WINDOW, -1)
    edge = jnp.zeros((2, 1, WINDOW, shaped.shape[-1]), f32)
    total = jnp.concatenate([shaped[:, :, 0], edge], axis=1) + jnp.concatenate(
        [edge, shaped[:, :, 1]], axis=1
    )
    return total.reshape(2, 576, -1)


def visibility(lengths):
    y, z = lax.axis_index("y"), lax.axis_index("z")
    starts = (y * 8 + z + 4 * jnp.arange(2, dtype=jnp.int32)) * BLOCK
    positions = starts[:, None] - WINDOW + jnp.arange(BLOCK + WINDOW, dtype=jnp.int32)
    ends = jnp.cumsum(lengths)
    segment = jnp.sum((positions[..., None] >= ends).astype(jnp.int32), axis=-1)
    key_pos = band_blocks(positions)
    key_seg = band_blocks(segment)
    query_pos = positions[:, WINDOW:].reshape(16, WINDOW)
    query_seg = segment[:, WINDOW:].reshape(16, WINDOW)
    visible = (key_pos[:, None, :] <= query_pos[:, :, None]) & (
        key_pos[:, None, :] > query_pos[:, :, None] - WINDOW
    )
    return visible & (key_pos[:, None, :] >= 0) & (key_seg[:, None, :] == query_seg[:, :, None])


YZ = ("y", "z")


def tails_forward(tails):
    z = lax.axis_index("z")
    ring = shift(tails, "z", 1)
    step = lax.ppermute(tails[1], YZ, [(4 * y + 3, 4 * y + 4) for y in range(3)])
    return jnp.where(z == 0, jnp.stack([step, ring[0]]), ring)


def tails_back(heads):
    z = lax.axis_index("z")
    ring = shift(heads, "z", -1)
    step = lax.ppermute(heads[0], YZ, [(4 * y + 4, 4 * y + 3) for y in range(3)])
    return jnp.where(z == 3, jnp.stack([ring[1], step]), ring)


def score_blocks(query_blocks, key_blocks, visible):
    scores = jnp.einsum(
        "bqhd,bkhd->bhqk", query_blocks, key_blocks, preferred_element_type=f32
    ) * HEAD_DIM ** (-0.5)
    return jnp.where(visible[:, None], scores, masked_score)


def per_device(
    hidden_in,
    norm_gain_attn,
    w_query,
    w_key,
    w_value,
    w_out,
    norm_gain_mlp,
    w_gate,
    w_up,
    w_down,
    lengths,
    cotangent,
):
    xh, xl, c = lax.axis_index("xh"), lax.axis_index("xl"), lax.axis_index("c")

    def halves(w):
        n = w.shape[1] // 2
        return jnp.where(xh == 0, w[:, :n], w[:, n:]), jnp.where(xh == 0, w[:, n:], w[:, :n])

    def swap(pairs):
        mine = jnp.concatenate([p[0] for p in pairs], axis=1)
        theirs = jnp.concatenate([p[1] for p in pairs], axis=1)
        return in_order(xh, mine[None], flip(theirs, "xh")[None], 0)

    gains = jnp.stack([norm_gain_attn, norm_gain_mlp], axis=1)
    gains = jnp.pad(gains, ((0, 0), (0, 126)))
    attn_pack = swap([halves(w) for w in (w_query, w_key, w_value, w_out.T)] + [(gains, gains)])
    ff_pack = swap([halves(w) for w in (w_gate, w_up, w_down.T)])
    attn_a, attn_b = gather_weights(attn_pack)
    attn = jnp.concatenate([attn_a, attn_b], axis=1)
    qkv_w = attn[:, :768]
    out_w = attn[:, 768:1024]
    gain_attn = attn[:, 1024].astype(f32)
    gain_mlp = attn[:, 1025].astype(f32)

    hidden = gather_block(hidden_in)
    cot = gather_block(cotangent)
    q = xl * 2 + c
    owned_rows = lambda a: lax.dynamic_slice_in_dim(a, q * OWNED, OWNED, 0)
    hidden_owned = owned_rows(hidden_in).astype(f32)
    cot_owned = owned_rows(cotangent).astype(f32)

    ff_a, ff_b = gather_weights(ff_pack)
    ff = jnp.concatenate([ff_a, ff_b], axis=1)
    gate_w, up_w, down_w = ff[:, :688], ff[:, 688:1376], ff[:, 1376:]

    visible = visibility(lengths)
    normed_attn = rms_scale(hidden.astype(f32), gain_attn).astype(bf16)
    qkv = dot_plain(normed_attn, qkv_w).astype(bf16)
    queries = qkv[:, :256].reshape(16, WINDOW, 2, HEAD_DIM)
    kv = qkv[:, 256:].reshape(2, BLOCK, 512)
    kv_ext = jnp.concatenate([tails_forward(kv[:, -WINDOW:]), kv], axis=1)
    key_blocks = band_blocks(kv_ext[..., :256]).reshape(16, 2 * WINDOW, 2, HEAD_DIM)
    value_blocks = band_blocks(kv_ext[..., 256:]).reshape(16, 2 * WINDOW, 2, HEAD_DIM)
    scores = score_blocks(queries, key_blocks, visible)
    highest = jnp.max(scores, axis=-1, keepdims=True)
    expo = jnp.exp(scores - highest)
    probs = expo / jnp.sum(expo, axis=-1, keepdims=True)
    probs_low = probs.astype(bf16)
    mixed = jnp.einsum("bhqk,bkhd->bqhd", probs_low, value_blocks, preferred_element_type=f32)
    mixed = mixed.reshape(1024, 256).astype(bf16)
    resid = hidden_owned + reduce_group(dot_right_turned(mixed, out_w))
    normed_mlp = gather_group(rms_scale(resid, gain_mlp).astype(bf16))

    gate = dot_plain(normed_mlp, gate_w)
    up = dot_plain(normed_mlp, up_w)
    sig = 1 / (1 + jnp.exp(-gate))
    silu = gate * sig
    activated = (silu * up).astype(bf16)
    result = resid + reduce_group(dot_right_turned(activated, down_w))
    result = gather_owned(result.astype(bf16))

    grad_act = dot_plain(cot, down_w)
    grad_gate_act = (grad_act * up * sig * (1 + gate * (1 - sig))).astype(bf16)
    grad_up_act = (grad_act * silu).astype(bf16)
    grad_normed_mlp = reduce_group(
        dot_right_turned(grad_gate_act, gate_w) + dot_right_turned(grad_up_act, up_w)
    )
    grad_down = dot_left_turned(cot, activated).astype(bf16)
    grad_gate = dot_left_turned(normed_mlp, grad_gate_act).astype(bf16)
    grad_up = dot_left_turned(normed_mlp, grad_up_act).astype(bf16)
    grad_ff = jnp.concatenate([grad_gate, grad_up, grad_down], axis=1)
    grad_ff = reduce_weights(grad_ff[:, :1024], grad_ff[:, 1024:])

    def norm_back(grad, values, gain):
        r = lax.rsqrt(jnp.mean(values * values, axis=-1, keepdims=True) + epsilon)
        e = grad * gain
        back = r * e - values * r**3 * jnp.mean(e * values, axis=-1, keepdims=True)
        return back, jnp.sum(grad * values * r, axis=0)

    back, grad_gain_mlp = norm_back(grad_normed_mlp, resid, gain_mlp)
    grad_resid = cot_owned + back
    grad_branch = gather_group(grad_resid.astype(bf16))
    grad_out = dot_left_turned(grad_branch, mixed).astype(bf16)
    grad_mixed = dot_plain(grad_branch, out_w).astype(bf16).reshape(16, WINDOW, 2, HEAD_DIM)
    grad_probs = jnp.einsum("bqhd,bkhd->bhqk", grad_mixed, value_blocks, preferred_element_type=f32)
    inner = jnp.sum(probs * grad_probs, axis=-1, keepdims=True)
    grad_scores = (probs * (grad_probs - inner)).astype(bf16)
    scale = HEAD_DIM ** (-0.5)
    grad_queries = (
        jnp.einsum("bhqk,bkhd->bqhd", grad_scores, key_blocks, preferred_element_type=f32) * scale
    )
    grad_keys = (
        jnp.einsum("bhqk,bqhd->bkhd", grad_scores, queries, preferred_element_type=f32) * scale
    )
    grad_values = jnp.einsum("bhqk,bqhd->bkhd", probs_low, grad_mixed, preferred_element_type=f32)
    grad_kv = jnp.concatenate([fold_blocks(grad_keys), fold_blocks(grad_values)], axis=-1)
    returned = tails_back(grad_kv[:, :WINDOW].astype(bf16)).astype(f32)
    grad_kv = jnp.concatenate(
        [grad_kv[:, WINDOW:BLOCK], grad_kv[:, BLOCK:] + returned], axis=1
    ).reshape(1024, 512)
    grad_qkv_act = jnp.concatenate([grad_queries.reshape(1024, 256), grad_kv], axis=1).astype(bf16)
    grad_normed_attn = reduce_group(dot_right_turned(grad_qkv_act, qkv_w))
    grad_qkv = dot_left_turned(normed_attn, grad_qkv_act).astype(bf16)
    back, grad_gain_attn = norm_back(grad_normed_attn, hidden_owned, gain_attn)
    input_grad = gather_owned((grad_resid + back).astype(bf16))

    grad_gains = jnp.stack([grad_gain_attn, grad_gain_mlp], axis=1)
    grad_gains = jnp.pad(grad_gains, ((0, 0), (0, 126))).astype(bf16)
    grad_attn = jnp.concatenate([grad_qkv, grad_out, grad_gains], axis=1)
    grad_attn = reduce_weights(grad_attn[:, :512], grad_attn[:, 512:])

    def unswap(pack):
        mine = pick(pack, 0, xh)[0]
        return mine, flip(pick(pack, 0, 1 - xh)[0], "xh")

    mine_a, other_a = unswap(grad_attn)
    mine_f, other_f = unswap(grad_ff)

    def whole(mine, other, start, width):
        return in_order(xh, mine[:, start : start + width], other[:, start : start + width], 1).astype(f32)

    grads_gain = mine_a[:, 1024:1026].astype(f32) + other_a[:, 1024:1026].astype(f32)
    grads_gain = grads_gain + flip(grads_gain, "xl")
    grads_gain = grads_gain + flip(grads_gain, "c")
    return (
        result,
        input_grad,
        grads_gain[:, 0],
        whole(mine_a, other_a, 0, 256),
        whole(mine_a, other_a, 256, 256),
        whole(mine_a, other_a, 512, 256),
        whole(mine_a, other_a, 768, 256).T,
        grads_gain[:, 1],
        whole(mine_f, other_f, 0, 688),
        whole(mine_f, other_f, 688, 688),
        whole(mine_f, other_f, 1376, 688).T,
    )


def solution(mesh):
    mesh = Mesh(mesh.devices.reshape(4, 2, 4, 2, 2), AXES)
    seq, head = ("y", "xh", "z"), ("xl", "c")
    rows, cols, flat, turned = P(seq, None), P(seq, head), P(seq), P(head, seq)
    return jax.shard_map(
        per_device,
        mesh=mesh,
        in_specs=(rows, flat, cols, cols, cols, turned, flat, cols, cols, turned, P(), rows),
        out_specs=(rows, rows, flat, cols, cols, cols, turned, flat, cols, cols, turned),
        check_vma=False,
    )
```

time: 2230 us -> 672 us (0.30)
  waiting for transfers between devices: 1820 us -> 189 us
  starting transfers between devices: 5.43 us -> 187 us
  blocking collectives: 173 us -> 0 us
  local copies, waits for them, and re-layouts: 23.9 us -> 112 us
  other arithmetic: 41.5 us -> 78.1 us
    reduce_scatter x7 -> x0, waiting for transfers between devices: 1100 us -> none  [the longest x1 192 us: per_device(): lax.psum_scatter(grad_up.astype(jnp.bfloat16), 'seq', scatter_dimension=0...]
    all_gather x7 -> x0, waiting for transfers between devices: 421 us -> none  [the longest x1 86.3 us: per_device(): lax.all_gather(w_up, 'seq', axis=0, tiled=True)]
    psum x3 -> x0, waiting for transfers between devices: 292 us -> none  [the longest x1 113 us: per_device(): lax.psum(dot_plain(activated, down_w).astype(jnp.bfloat16), 'head')]
    ppermute x2 -> x122, starting transfers between devices: 3.9 us -> 187 us  [the longest x100 127 us: shift(): return lax.ppermute(value, axis, [(i, (i + steps) % 4) for i in range(4)])]
    ppermute x2 -> x122, waiting for transfers between devices: 5.73 us -> 189 us  [the longest x100 175 us: shift(): return lax.ppermute(value, axis, [(i, (i + steps) % 4) for i in range(4)])]
    unnamed x2 -> x0, blocking collectives: 173 us -> none
    slice x11 -> x46, local copies, waits for them, and re-layouts: 1.66 us -> 33.5 us  [the longest x2 12.9 us: per_device(): grad_ff = reduce_weights(grad_ff[:, :1024], grad_ff[:, 1024:])]
    select_n x0 -> x14, other arithmetic: none -> 27.3 us  [the longest x10 24.1 us: in_order(): jnp.where(flag == 0, jnp.concatenate([mine, other], axis=axis), jnp.conca...]
  transfers between devices with their start and end apart: 19 -> 122, of which waited for: 17 -> 37; matrix products, arithmetic and copies ran while one was open for 6% -> 32% of each run, Pallas kernels for 0% -> 0%
where the time goes in v1:
time: 672 us; the launch traced here: 663 us
  waiting for transfers between devices  189 us (28%)
  starting transfers between devices  187 us (28%)
  local copies, waits for them, and re-layouts  112 us (17%)
  matrix products  94.5 us (14%)
  other arithmetic  78.1 us (12%)
    ppermute x100, waiting for transfers between devices, shift(): return lax.ppermute(value, axis, [(i, (i + steps) % 4) for i in range(4)])  175 us
    ppermute x100, starting transfers between devices, shift(): return lax.ppermute(value, axis, [(i, (i + steps) % 4) for i in range(4)])  127 us
    ppermute x18, starting transfers between devices, flip(): return lax.ppermute(value, axis, [(0, 1), (1, 0)])  56.3 us
    dot_general x5, matrix products, dot_plain(): return jnp.dot(left, right, preferred_element_type=f32)  28.8 us
    dot_general x5, matrix products, dot_right_turned(): lax.dot_general(left, right, (((1,), (1,)), ((), ())), preferred_element_...  25.4 us
    select_n x10, other arithmetic, in_order(): jnp.where(flag == 0, jnp.concatenate([mine, other], axis=axis), jnp.conca...  24.1 us
    dot_general x5, matrix products, dot_left_turned(): lax.dot_general(left, right, (((0,), (0,)), ((), ())), preferred_element_...  20.3 us
    dynamic_update_slice x30, local copies, waits for them, and re-layouts, place(): total = lax.dynamic_update_slice_in_dim(total, piece, (index + k) % 4, axis)  18.7 us
  transfers between devices with their start and end apart: 122, of which 37 were waited for; matrix products, arithmetic and copies ran while one was open for 32% of the time, Pallas kernels for 0%

profile of v1, /device:TPU:1, one launch (start us, length us, event | category | flops | bytes accessed | tf_op | source)
XLA Modules:
  0.0 663.5 jit_solution(12914054044333092473)
XLA Ops:
  93.2 5.5 fusion.24
  136.2 9.7 %collective-permute-done.24 = bf16[128,2048]{1,0:T(8,128)(2,1)S(1)} collective-permute-done((bf16[128,2048]{1,0:T(8,128)(2,1)S(1)}, bf16[128,2048]{1,0:T(8,128)(2,1)S(1)}, u32[]{:S(2)}, u32[]{:S(2)}) %collective-permute-start.24) | collective-permute-done | bytes 524320 | tf_op jit(solution)/shard_map/ppermute | solution.py:20
  152.3 37.2 %collective-permute-done.25 = bf16[1,128,2048]{2,1,0:T(8,128)(2,1)S(1)} collective-permute-done((bf16[1,128,2048]{2,1,0:T(8,128)(2,1)S(1)}, bf16[1,128,2048]{2,1,0:T(8,128)(2,1)S(1)}, u32[]{:S(2)}, u32[]{:S(2)}) %collective-permute-start.25) | collective-permute-done | bytes 524320 | tf_op jit(solution)/shard_map/ppermute | solution.py:20
  235.4 5.7 maximum_select_fusion.1
  251.2 12.4 %multiply_convert_fusion.1 = (bf16[1024,688]{0,1:T(8,128)(2,1)}, bf16[1024,688]{0,1:T(8,128)(2,1)}, bf16[1024,688]{0,1:T(8,128)(2,1)}) fusion(f32[1024,688]{0,1:T(8,128)} %fusion.11, f32[1024,688]{0,1:T(8,128)} %fusion.91, bf16[2048,1040]{1,0:T(8,128)(2,1)S(1)} %bitcast.293, bf16[512,2048]{1,0:T(8,128)(2,1)} %maximum_select_fusion.6, ...), kind=kOutput, calls=%fused_computation.30 | convolution fusion | flops 2915123200 | bytes 17203200 | tf_op jit(solution)/shard_map/dot_general | solution.py:28
  268.9 7.5 %fusion.92 = f32[1024,2048]{1,0:T(8,128)} fusion(bf16[1024,688]{0,1:T(8,128)(2,1)S(1)} %copy-done.74, bf16[2048,1040]{1,0:T(8,128)(2,1)S(1)} %bitcast.294, bf16[2048,1024]{1,0:T(8,128)(2,1)S(1)} %bitcast.314), kind=kOutput, calls=%fused_computation.348 | convolution fusion | flops 2891317248 | bytes 18251776 | tf_op jit(solution)/shard_map/dot_general | solution.py:32
  282.1 6.4 copy.200
  302.7 6.5 copy.201
  312.4 7.3 %convolution_add_fusion = f32[1024,2048]{1,0:T(8,128)S(1)} fusion(f32[1024,2048]{1,0:T(8,128)} %fusion.92, bf16[1024,688]{0,1:T(8,128)(2,1)} %get-tuple-element.35, bf16[2048,1024]{1,0:T(8,128)(2,1)S(1)} %bitcast.315), kind=kOutput, calls=%fused_computation.22 | convolution fusion | flops 2887778304 | bytes 21331968 | tf_op jit(solution)/shard_map/dot_general | solution.py:32
  329.2 7.7 %collective-permute-start.54 = (bf16[4,128,2048]{2,1,0:T(8,128)(2,1)}, bf16[4,128,2048]{2,1,0:T(8,128)(2,1)}, u32[]{:S(2)}, u32[]{:S(2)}) collective-permute-start(bf16[4,128,2048]{2,1,0:T(8,128)(2,1)} %fusion.17), channel_id=1, source_target_pairs={{0,1},{1,0},{2,3},{3,2},{4,5},{5,4},{6,7},{7,6},{8,9},{9,8},{10,11... | collective-permute-start | bytes 6291464 | tf_op jit(solution)/shard_map/ppermute | solution.py:24
  344.9 11.6 %collective-permute-done.111 = bf16[4,2,1,32,1040]{4,3,2,1,0:T(8,128)(2,1)S(1)} collective-permute-done((bf16[4,2,1,32,1040]{4,3,2,1,0:T(8,128)(2,1)S(1)}, bf16[4,2,1,32,1040]{4,3,2,1,0:T(8,128)(2,1)S(1)}, u32[]{:S(2)}, u32[]{:S(2)}) %collective-permute-start.111) | collective-permute-done | bytes 532512 | tf_op jit(solution)/shard_map/ppermute | solution.py:20
  362.2 8.4 %collective-permute-done.112 = bf16[4,2,1,32,1040]{4,3,2,1,0:T(8,128)(2,1)S(1)} collective-permute-done((bf16[4,2,1,32,1040]{4,3,2,1,0:T(8,128)(2,1)S(1)}, bf16[4,2,1,32,1040]{4,3,2,1,0:T(8,128)(2,1)S(1)}, u32[]{:S(2)}, u32[]{:S(2)}) %collective-permute-start.112) | collective-permute-done | bytes 532512 | tf_op jit(solution)/shard_map/ppermute | solution.py:20
  373.5 9.8 %collective-permute-done.114 = bf16[4,2,1,32,1040]{4,3,2,1,0:T(8,128)(2,1)S(1)} collective-permute-done((bf16[4,2,1,32,1040]{4,3,2,1,0:T(8,128)(2,1)S(1)}, bf16[4,2,1,32,1040]{4,3,2,1,0:T(8,128)(2,1)S(1)}, u32[]{:S(2)}, u32[]{:S(2)}) %collective-permute-start.114) | collective-permute-done | bytes 532512 | tf_op jit(solution)/shard_map/ppermute | solution.py:20
  401.9 8.8 %collective-permute-done.57 = bf16[128,2048]{1,0:T(8,128)(2,1)S(1)} collective-permute-done((bf16[128,2048]{1,0:T(8,128)(2,1)S(1)}, bf16[128,2048]{1,0:T(8,128)(2,1)S(1)}, u32[]{:S(2)}, u32[]{:S(2)}) %collective-permute-start.57) | collective-permute-done | bytes 524320 | tf_op jit(solution)/shard_map/ppermute | solution.py:20
  411.7 10.4 %collective-permute-done.47 = bf16[128,2048]{1,0:T(8,128)(2,1)S(1)} collective-permute-done((bf16[128,2048]{1,0:T(8,128)(2,1)S(1)}, bf16[128,2048]{1,0:T(8,128)(2,1)S(1)}, u32[]{:S(2)}, u32[]{:S(2)}) %collective-permute-start.47) | collective-permute-done | bytes 524320 | tf_op jit(solution)/shard_map/ppermute | solution.py:20
  424.8 6.9 %collective-permute-done.49 = bf16[128,2048]{1,0:T(8,128)(2,1)S(1)} collective-permute-done((bf16[128,2048]{1,0:T(8,128)(2,1)S(1)}, bf16[128,2048]{1,0:T(8,128)(2,1)S(1)}, u32[]{:S(2)}, u32[]{:S(2)}) %collective-permute-start.49) | collective-permute-done | bytes 524320 | tf_op jit(solution)/shard_map/ppermute | solution.py:20
  440.6 5.6 collective-permute-done.58
  450.7 10.8 %collective-permute-done.60 = bf16[1,128,2048]{2,1,0:T(8,128)(2,1)S(1)} collective-permute-done((bf16[1,128,2048]{2,1,0:T(8,128)(2,1)S(1)}, bf16[1,128,2048]{2,1,0:T(8,128)(2,1)S(1)}, u32[]{:S(2)}, u32[]{:S(2)}) %collective-permute-start.60) | collective-permute-done | bytes 524320 | tf_op jit(solution)/shard_map/ppermute | solution.py:20
  465.0 9.5 %collective-permute-start.61 = (bf16[4,1,128,2048]{3,2,1,0:T(8,128)(2,1)}, bf16[4,1,128,2048]{3,2,1,0:T(8,128)(2,1)}, u32[]{:S(2)}, u32[]{:S(2)}) collective-permute-start(bf16[4,1,128,2048]{3,2,1,0:T(8,128)(2,1)} %bitcast_dynamic-update-slice_fusion), channel_id=1, source_target_pairs={{0,1},{1,0},{2,3},{3,2},{4,5},{5,4},{6,7},{7,6},{8,9},{9,8},{10,11... | collective-permute-start | bytes 6291464 | tf_op jit(solution)/shard_map/ppermute | solution.py:24
  488.5 7.4 %collective-permute-done.121 = bf16[64,2064]{1,0:T(8,128)(2,1)S(1)} collective-permute-done((bf16[64,2064]{1,0:T(8,128)(2,1)S(1)}, bf16[64,2064]{1,0:T(8,128)(2,1)S(1)}, u32[]{:S(2)}, u32[]{:S(2)}) %collective-permute-start.121) | collective-permute-done | bytes 264224 | tf_op jit(solution)/shard_map/ppermute | solution.py:24
  508.2 7.1 %convolution_bitcast_fusion = f32[16,128,2,128]{1,3,2,0:T(8,128)} fusion(bf16[16,64,2,128]{3,2,1,0:T(2,128)(2,1)} %reshape.882, f32[16,2,64]{2,1,0:T(2,128)S(1)} %get-tuple-element.152, f32[16,2,64,128]{3,2,1,0:T(8,128)} %copy-done.24), kind=kOutput, calls=%fused_computation.65 | convolution fusion | flops 67897472 | bytes 3678208 | tf_op jit(solution)/shard_map/bhqk,bqhd->bkhd/dot_general | solution.py:312
  591.8 9.3 %collective-permute-done.67 = bf16[128,2048]{1,0:T(8,128)(2,1)S(1)} collective-permute-done((bf16[128,2048]{1,0:T(8,128)(2,1)S(1)}, bf16[128,2048]{1,0:T(8,128)(2,1)S(1)}, u32[]{:S(2)}, u32[]{:S(2)}) %collective-permute-start.67) | collective-permute-done | bytes 524320 | tf_op jit(solution)/shard_map/ppermute | solution.py:20
  620.0 5.6 collective-permute-done.83
  639.7 7.1 %collective-permute-start.69 = (bf16[2,1,128,2048]{3,2,1,0:T(8,128)(2,1)S(1)}, bf16[2,1,128,2048]{3,2,1,0:T(8,128)(2,1)S(1)}, u32[]{:S(2)}, u32[]{:S(2)}) collective-permute-start(bf16[2,1,128,2048]{3,2,1,0:T(8,128)(2,1)S(1)} %maximum_select_fusion.9), channel_id=1, source_target_pairs={{0,1},{1,0},{2,3},{3,2},{4,5},{5,4},{6,7},{7,6},{8,9},{9,8},{10,11... | collective-permute-start | bytes 3145736 | tf_op jit(solution)/shard_map/ppermute | solution.py:24
  (631 shorter events, 436.3 us)
Async XLA Ops:
  10.7 31.4 %collective-permute-start = (bf16[256,2048]{1,0:T(8,128)(2,1)}, bf16[256,2048]{1,0:T(8,128)(2,1)}, u32[]{:S(2)}, u32[]{:S(2)}) collective-permute-start(bf16[256,2048]{1,0:T(8,128)(2,1)} %constant_dynamic-slice_fusion.36), channel_id=1, source_target_pairs={{0,18},{2,16},{16,2},{18,0},{1,19},{3,17},{17,3},{19,1},{4,22},{6,... | collective-permute-start | bytes 3145736 | tf_op jit(solution)/shard_map/ppermute | solution.py:118
  56.0 48.7 %collective-permute-start.29 = (bf16[64,2064]{1,0:T(8,128)(2,1)}, bf16[64,2064]{1,0:T(8,128)(2,1)}, u32[]{:S(2)}, u32[]{:S(2)}) collective-permute-start(bf16[64,2064]{1,0:T(8,128)(2,1)} %concatenate.443), channel_id=1, source_target_pairs={{0,16},{16,0},{1,17},{17,1},{2,18},{18,2},{3,19},{19,3},{4,20},{20... | collective-permute-start | bytes 792584 | tf_op jit(solution)/shard_map/ppermute | solution.py:24
  132.7 60.9 %collective-permute-start.52 = (bf16[256,2048]{1,0:T(8,128)(2,1)S(1)}, bf16[256,2048]{1,0:T(8,128)(2,1)}, u32[]{:S(2)}, u32[]{:S(2)}) collective-permute-start(bf16[256,2048]{1,0:T(8,128)(2,1)S(1)} %constant_dynamic-slice_fusion.35), channel_id=1, source_target_pairs={{0,18},{2,16},{16,2},{18,0},{1,19},{3,17},{17,3},{19,1},{4,22},{6,... | collective-permute-start | bytes 3145736 | tf_op jit(solution)/shard_map/ppermute | solution.py:118
  133.3 78.3 %collective-permute-start.34 = (bf16[1,2,4,64,1024]{4,3,2,1,0:T(8,128)(2,1)}, bf16[1,2,4,64,1024]{4,3,2,1,0:T(8,128)(2,1)}, u32[]{:S(2)}, u32[]{:S(2)}) collective-permute-start(bf16[1,2,4,64,1024]{4,3,2,1,0:T(8,128)(2,1)} %constant_dynamic-update-slice_fusion.6), channel_id=1, source_target_pairs={{0,96},{32,0},{64,32},{96,64},{1,97},{33,1},{65,33},{97,65},{2,98}... | collective-permute-start | bytes 3145736 | tf_op jit(solution)/shard_map/ppermute | solution.py:20
  136.2 70.4 %collective-permute-start.35 = (bf16[1,2,4,64,1024]{4,3,2,1,0:T(8,128)(2,1)}, bf16[1,2,4,64,1024]{4,3,2,1,0:T(8,128)(2,1)}, u32[]{:S(2)}, u32[]{:S(2)}) collective-permute-start(bf16[1,2,4,64,1024]{4,3,2,1,0:T(8,128)(2,1)} %constant_dynamic-update-slice_fusion.6), channel_id=1, source_target_pairs={{0,32},{32,64},{64,96},{96,0},{1,33},{33,65},{65,97},{97,1},{2,34}... | collective-permute-start | bytes 3145736 | tf_op jit(solution)/shard_map/ppermute | solution.py:20
  146.6 42.9 %collective-permute-start.25 = (bf16[1,128,2048]{2,1,0:T(8,128)(2,1)S(1)}, bf16[1,128,2048]{2,1,0:T(8,128)(2,1)S(1)}, u32[]{:S(2)}, u32[]{:S(2)}) collective-permute-start(bf16[1,128,2048]{2,1,0:T(8,128)(2,1)S(1)} %fusion.90), channel_id=1, source_target_pairs={{0,18},{2,0},{16,2},{18,16},{1,19},{3,1},{17,3},{19,17},{4,22},{6,... | collective-permute-start | bytes 1572872 | tf_op jit(solution)/shard_map/ppermute | solution.py:20
  148.3 44.3 %collective-permute-start.26 = (bf16[1,128,2048]{2,1,0:T(8,128)(2,1)S(1)}, bf16[1,128,2048]{2,1,0:T(8,128)(2,1)S(1)}, u32[]{:S(2)}, u32[]{:S(2)}) collective-permute-start(bf16[1,128,2048]{2,1,0:T(8,128)(2,1)S(1)} %fusion.90), channel_id=1, source_target_pairs={{0,16},{2,18},{16,0},{18,2},{1,17},{3,19},{17,1},{19,3},{4,20},{6,... | collective-permute-start | bytes 1572872 | tf_op jit(solution)/shard_map/ppermute | solution.py:20
  192.6 28.3 %collective-permute-start.42 = (bf16[4,2,1,64,1040]{4,3,2,1,0:T(8,128)(2,1)}, bf16[4,2,1,64,1040]{4,3,2,1,0:T(8,128)(2,1)}, u32[]{:S(2)}, u32[]{:S(2)}) collective-permute-start(bf16[4,2,1,64,1040]{4,3,2,1,0:T(8,128)(2,1)} %bitcast_dynamic-update-slice_fusion.9), channel_id=1, source_target_pairs={{0,12},{4,0},{8,4},{12,8},{1,13},{5,1},{9,5},{13,9},{2,14},{6,2},{... | collective-permute-start | bytes 3194888 | tf_op jit(solution)/shard_map/ppermute | solution.py:20
  206.5 28.9 %collective-permute-start.28 = (bf16[4,1,128,2048]{3,2,1,0:T(8,128)(2,1)}, bf16[4,1,128,2048]{3,2,1,0:T(8,128)(2,1)}, u32[]{:S(2)}, u32[]{:S(2)}) collective-permute-start(bf16[4,1,128,2048]{3,2,1,0:T(8,128)(2,1)} %bitcast_dynamic-update-slice_fusion.4), channel_id=1, source_target_pairs={{0,1},{1,0},{2,3},{3,2},{4,5},{5,4},{6,7},{7,6},{8,9},{9,8},{10,11... | collective-permute-start | bytes 6291464 | tf_op jit(solution)/shard_map/ppermute | solution.py:24
  291.5 34.6 %collective-permute-start.101 = (bf16[1,2,4,32,1024]{4,3,2,1,0:T(8,128)(2,1)}, bf16[1,2,4,32,1024]{4,3,2,1,0:T(8,128)(2,1)}, u32[]{:S(2)}, u32[]{:S(2)}) collective-permute-start(bf16[1,2,4,32,1024]{4,3,2,1,0:T(8,128)(2,1)} %get-tuple-element.46), channel_id=1, source_target_pairs={{0,96},{32,0},{64,32},{96,64},{1,97},{33,1},{65,33},{97,65},{2,98}... | collective-permute-start | bytes 1572872 | tf_op jit(solution)/shard_map/ppermute | solution.py:20
  292.7 36.5 %collective-permute-start.97 = (bf16[1,2,4,32,1024]{4,3,2,1,0:T(8,128)(2,1)}, bf16[1,2,4,32,1024]{4,3,2,1,0:T(8,128)(2,1)}, u32[]{:S(2)}, u32[]{:S(2)}) collective-permute-start(bf16[1,2,4,32,1024]{4,3,2,1,0:T(8,128)(2,1)} %get-tuple-element.45), channel_id=1, source_target_pairs={{0,32},{32,64},{64,96},{96,0},{1,33},{33,65},{65,97},{97,1},{2,34}... | collective-permute-start | bytes 1572872 | tf_op jit(solution)/shard_map/ppermute | solution.py:20
  293.0 47.3 %collective-permute-start.100 = (bf16[1,2,4,32,1024]{4,3,2,1,0:T(8,128)(2,1)}, bf16[1,2,4,32,1024]{4,3,2,1,0:T(8,128)(2,1)}, u32[]{:S(2)}, u32[]{:S(2)}) collective-permute-start(bf16[1,2,4,32,1024]{4,3,2,1,0:T(8,128)(2,1)} %get-tuple-element.44), channel_id=1, source_target_pairs={{0,96},{32,0},{64,32},{96,64},{1,97},{33,1},{65,33},{97,65},{2,98}... | collective-permute-start | bytes 1572872 | tf_op jit(solution)/shard_map/ppermute | solution.py:20
  295.4 45.0 %collective-permute-start.99 = (bf16[1,2,4,32,1024]{4,3,2,1,0:T(8,128)(2,1)}, bf16[1,2,4,32,1024]{4,3,2,1,0:T(8,128)(2,1)}, u32[]{:S(2)}, u32[]{:S(2)}) collective-permute-start(bf16[1,2,4,32,1024]{4,3,2,1,0:T(8,128)(2,1)} %get-tuple-element.47), channel_id=1, source_target_pairs={{0,32},{32,64},{64,96},{96,0},{1,33},{33,65},{65,97},{97,1},{2,34}... | collective-permute-start | bytes 1572872 | tf_op jit(solution)/shard_map/ppermute | solution.py:20
  312.4 28.1 %collective-permute-start.109 = (bf16[4,2,1,32,1040]{4,3,2,1,0:T(8,128)(2,1)}, bf16[4,2,1,32,1040]{4,3,2,1,0:T(8,128)(2,1)}, u32[]{:S(2)}, u32[]{:S(2)}) collective-permute-start(bf16[4,2,1,32,1040]{4,3,2,1,0:T(8,128)(2,1)} %get-tuple-element.39), channel_id=1, source_target_pairs={{0,4},{4,8},{8,12},{12,0},{1,5},{5,9},{9,13},{13,1},{2,6},{6,10},{... | collective-permute-start | bytes 1597448 | tf_op jit(solution)/shard_map/ppermute | solution.py:20
  329.2 55.4 %collective-permute-start.54 = (bf16[4,128,2048]{2,1,0:T(8,128)(2,1)}, bf16[4,128,2048]{2,1,0:T(8,128)(2,1)}, u32[]{:S(2)}, u32[]{:S(2)}) collective-permute-start(bf16[4,128,2048]{2,1,0:T(8,128)(2,1)} %fusion.17), channel_id=1, source_target_pairs={{0,1},{1,0},{2,3},{3,2},{4,5},{5,4},{6,7},{7,6},{8,9},{9,8},{10,11... | collective-permute-start | bytes 6291464 | tf_op jit(solution)/shard_map/ppermute | solution.py:24
  340.4 49.9 %collective-permute-start.46 = (bf16[4,128,2048]{2,1,0:T(8,128)(2,1)}, bf16[4,128,2048]{2,1,0:T(8,128)(2,1)S(1)}, u32[]{:S(2)}, u32[]{:S(2)}) collective-permute-start(bf16[4,128,2048]{2,1,0:T(8,128)(2,1)} %fusion.16), channel_id=1, source_target_pairs={{0,1},{1,0},{2,3},{3,2},{4,5},{5,4},{6,7},{7,6},{8,9},{9,8},{10,11... | collective-permute-start | bytes 6291464 | tf_op jit(solution)/shard_map/ppermute | solution.py:24
  370.6 63.9 %collective-permute-start.103 = (bf16[1,2,1,32,1024]{4,3,2,1,0:T(8,128)(2,1)}, bf16[1,2,1,32,1024]{4,3,2,1,0:T(8,128)(2,1)}, u32[]{:S(2)}, u32[]{:S(2)}) collective-permute-start(bf16[1,2,1,32,1024]{4,3,2,1,0:T(8,128)(2,1)} %get-tuple-element.88), channel_id=1, source_target_pairs={{0,4},{4,8},{8,12},{12,0},{1,5},{5,9},{9,13},{13,1},{2,6},{6,10},{... | collective-permute-start | bytes 393224 | tf_op jit(solution)/shard_map/ppermute | solution.py:20
  371.9 64.3 %collective-permute-start.107 = (bf16[1,2,1,32,1024]{4,3,2,1,0:T(8,128)(2,1)}, bf16[1,2,1,32,1024]{4,3,2,1,0:T(8,128)(2,1)}, u32[]{:S(2)}, u32[]{:S(2)}) collective-permute-start(bf16[1,2,1,32,1024]{4,3,2,1,0:T(8,128)(2,1)} %get-tuple-element.89), channel_id=1, source_target_pairs={{0,12},{4,0},{8,4},{12,8},{1,13},{5,1},{9,5},{13,9},{2,14},{6,2},{... | collective-permute-start | bytes 393224 | tf_op jit(solution)/shard_map/ppermute | solution.py:20
  422.1 52.4 %collective-permute-start.105 = (bf16[1,2,1,32,1024]{4,3,2,1,0:T(8,128)(2,1)S(1)}, bf16[1,2,1,32,1024]{4,3,2,1,0:T(8,128)(2,1)S(1)}, u32[]{:S(2)}, u32[]{:S(2)}) collective-permute-start(bf16[1,2,1,32,1024]{4,3,2,1,0:T(8,128)(2,1)S(1)} %copy-done.51), channel_id=1, source_target_pairs={{0,4},{4,8},{8,12},{12,0},{1,5},{5,9},{9,13},{13,1},{2,6},{6,10},{... | collective-permute-start | bytes 393224 | tf_op jit(solution)/shard_map/ppermute | solution.py:20
  422.2 53.4 %collective-permute-start.106 = (bf16[1,2,1,32,1024]{4,3,2,1,0:T(8,128)(2,1)S(1)}, bf16[1,2,1,32,1024]{4,3,2,1,0:T(8,128)(2,1)S(1)}, u32[]{:S(2)}, u32[]{:S(2)}) collective-permute-start(bf16[1,2,1,32,1024]{4,3,2,1,0:T(8,128)(2,1)S(1)} %copy-done.50), channel_id=1, source_target_pairs={{0,12},{4,0},{8,4},{12,8},{1,13},{5,1},{9,5},{13,9},{2,14},{6,2},{... | collective-permute-start | bytes 393224 | tf_op jit(solution)/shard_map/ppermute | solution.py:20
  431.7 30.6 %collective-permute-start.115 = (bf16[1,2,1,32,1040]{4,3,2,1,0:T(8,128)(2,1)S(1)}, bf16[1,2,1,32,1040]{4,3,2,1,0:T(8,128)(2,1)S(1)}, u32[]{:S(2)}, u32[]{:S(2)}) collective-permute-start(bf16[1,2,1,32,1040]{4,3,2,1,0:T(8,128)(2,1)S(1)} %copy-done.49), channel_id=1, source_target_pairs={{0,32},{32,64},{64,96},{96,0},{1,33},{33,65},{65,97},{97,1},{2,34}... | collective-permute-start | bytes 399368 | tf_op jit(solution)/shard_map/ppermute | solution.py:20
  465.0 33.4 %collective-permute-start.61 = (bf16[4,1,128,2048]{3,2,1,0:T(8,128)(2,1)}, bf16[4,1,128,2048]{3,2,1,0:T(8,128)(2,1)}, u32[]{:S(2)}, u32[]{:S(2)}) collective-permute-start(bf16[4,1,128,2048]{3,2,1,0:T(8,128)(2,1)} %bitcast_dynamic-update-slice_fusion), channel_id=1, source_target_pairs={{0,1},{1,0},{2,3},{3,2},{4,5},{5,4},{6,7},{7,6},{8,9},{9,8},{10,11... | collective-permute-start | bytes 6291464 | tf_op jit(solution)/shard_map/ppermute | solution.py:24
  498.4 55.5 %collective-permute-start.50 = (bf16[128,2048]{1,0:T(8,128)(2,1)}, bf16[128,2048]{1,0:T(8,128)(2,1)}, u32[]{:S(2)}, u32[]{:S(2)}) collective-permute-start(bf16[128,2048]{1,0:T(8,128)(2,1)} %get-tuple-element.93), channel_id=1, source_target_pairs={{0,2},{2,0},{1,3},{3,1},{4,6},{6,4},{5,7},{7,5},{8,10},{10,8},{9,1... | collective-permute-start | bytes 1572872 | tf_op jit(solution)/shard_map/ppermute | solution.py:24
  589.9 41.0 %collective-permute-start.78 = (bf16[1,2,1,32,512]{4,3,1,2,0:T(8,128)(2,1)S(1)}, bf16[1,2,1,32,512]{4,3,1,2,0:T(8,128)(2,1)S(1)}, u32[]{:S(2)}, u32[]{:S(2)}) collective-permute-start(bf16[1,2,1,32,512]{4,3,1,2,0:T(8,128)(2,1)S(1)} %get-tuple-element.109), channel_id=1, source_target_pairs={{0,4},{4,8},{8,12},{12,0},{1,5},{5,9},{9,13},{13,1},{2,6},{6,10},{... | collective-permute-start | bytes 196616 | tf_op jit(solution)/shard_map/ppermute | solution.py:20
  (180 other events, 2112.0 us)

commit v2 on v1

--- a/solution.py
+++ b/solution.py
@@ -1,6 +1,10 @@
+import functools
+
 import jax
 import jax.numpy as jnp
 from jax import lax
+from jax.experimental import pallas as pl
+from jax.experimental.pallas import tpu as pltpu
 from jax.sharding import Mesh, PartitionSpec as P
 
 HEAD_DIM = 128
@@ -203,6 +207,440 @@
     return jnp.where(visible[:, None], scores, masked_score)
 
 
+MESH = pl.DeviceIdType.MESH
+SCALE = HEAD_DIM ** (-0.5)
+ANY = pl.BlockSpec(memory_space=pl.ANY)
+TURNED = (((1,), (1,)), ((), ()))
+LEFT_TURNED = (((0,), (0,)), ((), ()))
+
+
+class Place:
+    def __init__(self):
+        self.y, self.z, self.c = lax.axis_index("y"), lax.axis_index("z"), lax.axis_index("c")
+        self.xh, self.xl = lax.axis_index("xh"), lax.axis_index("xl")
+        self.x = self.xh * 2 + self.xl
+        self.q = self.xl * 2 + self.c
+
+    def at(self, y=None, x=None, z=None, c=None):
+        y = self.y if y is None else y
+        x = self.x if x is None else x
+        z = self.z if z is None else z
+        c = self.c if c is None else c
+        return (y, x // 2, z, x % 2, c)
+
+
+class Links:
+    def __init__(self, send_sems, recv_sems, local_sems):
+        self.send_sems, self.recv_sems, self.local_sems = send_sems, recv_sems, local_sems
+        self.count, self.local_count, self.started = 0, 0, []
+
+    def send(self, src, dst, device):
+        copy = pltpu.make_async_remote_copy(
+            src_ref=src,
+            dst_ref=dst,
+            send_sem=self.send_sems.at[self.count],
+            recv_sem=self.recv_sems.at[self.count],
+            device_id=device,
+            device_id_type=MESH,
+        )
+        self.count += 1
+        copy.start()
+        self.started.append(copy)
+        return copy
+
+    def local(self, src, dst):
+        copy = pltpu.make_async_copy(src, dst, self.local_sems.at[self.local_count])
+        self.local_count += 1
+        copy.start()
+        return copy
+
+    def finish(self):
+        for copy in self.started:
+            copy.wait_send()
+
+
+class WeightGather:
+    def __init__(self, links, place, pack, whole, cut):
+        self.links, self.place, self.whole = links, place, whole
+        cols = whole.shape[-1]
+        self.parts = (pl.ds(0, cut), pl.ds(cut, cols - cut))
+        self.swap = links.send(
+            pack.at[1 - place.xh], whole.at[place.y, place.xh, place.z], place.at(x=(place.x + 2) % 4)
+        )
+        self.mine = links.local(pack.at[place.xh], whole.at[place.y, place.xh, place.z])
+
+    def send(self, ref, device):
+        return self.links.send(ref, ref, device)
+
+    def near(self, view_z, view_y):
+        p = self.place
+        first, second = self.parts
+        zs = (p.at(z=(p.z + 1) % 4), p.at(z=(p.z + 3) % 4))
+        ys = (p.at(y=(p.y + 1) % 4), p.at(y=(p.y + 3) % 4))
+        (ref_z, axis_z), (ref_y, axis_y) = view_z, view_y
+        to = {"z": zs, "y": ys}
+        self.got = [
+            self.send(ref_z, to[axis_z][0]),
+            self.send(ref_y, to[axis_y][0]),
+            self.send(ref_z, to[axis_z][1]),
+            self.send(ref_y, to[axis_y][1]),
+        ]
+
+    def wait(self):
+        for copy in self.got:
+            copy.wait_recv()
+
+    def start0(self):
+        p, w = self.place, self.whole
+        first, second = self.parts
+        self.swap.wait_recv()
+        self.mine.wait()
+        self.near(
+            (w.at[p.y, :, p.z, :, first], "z"),
+            (w.at[p.y, :, p.z, :, second], "y"),
+        )
+
+    def start1(self):
+        p, w = self.place, self.whole
+        first, second = self.parts
+        self.wait()
+        zn, zp, yn, yp = (p.z + 1) % 4, (p.z + 3) % 4, (p.y + 1) % 4, (p.y + 3) % 4
+        self.got = [
+            self.send(w.at[p.y, 0, zp, :, first], p.at(z=zn)),
+            self.send(w.at[yp, 0, p.z, :, second], p.at(y=yn)),
+            self.send(w.at[p.y, 1, zn, :, first], p.at(z=zp)),
+            self.send(w.at[yn, 1, p.z, :, second], p.at(y=yp)),
+        ]
+
+    def start2(self):
+        p, w = self.place, self.whole
+        first, second = self.parts
+        self.wait()
+        self.near(
+            (w.at[:, :, p.z, :, second], "z"),
+            (w.at[p.y, :, :, :, first], "y"),
+        )
+
+    def start3(self):
+        p, w = self.place, self.whole
+        first, second = self.parts
+        self.wait()
+        zn, zp, yn, yp = (p.z + 1) % 4, (p.z + 3) % 4, (p.y + 1) % 4, (p.y + 3) % 4
+        self.got = [
+            self.send(w.at[yp, 0, :, :, first], p.at(y=yn)),
+            self.send(w.at[:, 0, zp, :, second], p.at(z=zn)),
+            self.send(w.at[yn, 1, :, :, first], p.at(y=yp)),
+            self.send(w.at[:, 1, zn, :, second], p.at(z=zp)),
+        ]
+
+    def done(self):
+        self.wait()
+
+
+def greet(place):
+    p = place
+    barrier = pltpu.get_barrier_semaphore()
+    partners = (
+        p.at(z=(p.z + 1) % 4),
+        p.at(z=(p.z + 3) % 4),
+        p.at(y=(p.y + 1) % 4),
+        p.at(y=(p.y + 3) % 4),
+        p.at(x=(p.x + 1) % 4),
+        p.at(x=(p.x + 3) % 4),
+        p.at(x=(p.x + 2) % 4),
+        p.at(c=1 - p.c),
+    )
+    for device in partners:
+        pl.semaphore_signal(barrier, inc=1, device_id=device, device_id_type=MESH)
+
+    @pl.when(p.z == 3)
+    def _():
+        pl.semaphore_signal(barrier, inc=1, device_id=p.at(y=(p.y + 1) % 4, z=0 * p.z), device_id_type=MESH)
+
+    @pl.when(p.z == 0)
+    def _():
+        pl.semaphore_signal(barrier, inc=1, device_id=p.at(y=(p.y + 3) % 4, z=0 * p.z + 3), device_id_type=MESH)
+
+    pl.semaphore_wait(barrier, 8 + jnp.where((p.z == 3) | (p.z == 0), 1, 0))
+
+
+def unit_scale(values):
+    return values * lax.rsqrt(jnp.mean(values * values, axis=-1, keepdims=True) + epsilon)
+
+
+def forward_kernel(
+    pk_q, pk_o, pk_gu, pk_d, hid, cot, bias_in,
+    wq_o, wo_o, gu_o, d_o, xr_o, q_o, kv_o, mixed_o, resid_o, nm_o, cot_o,
+    wq, wo, hidg, xr, q_v, kvx, mixed, bias, send_c, recv_c, own, send_x, recv_x, nm,
+    send_sems, recv_sems, local_sems,
+):
+    p = Place()
+    links = Links(send_sems, recv_sems, local_sems)
+    sibling = p.at(c=1 - p.c)
+    facing = p.at(x=3 - p.x)
+    greet(p)
+
+    g_q = WeightGather(links, p, pk_q, wq, 384)
+    own_hidden = links.local(hid, hidg.at[p.xh])
+    rows = [pl.ds(p.c * 256 + k * 128, 128) for k in range(2)]
+    hidden_sent = [links.send(hid.at[r], hidg.at[p.xh, r], facing) for r in rows]
+    g_o = WeightGather(links, p, pk_o, wo, 128)
+    bias_copy = links.local(bias_in, bias)
+    g_gu = WeightGather(links, p, pk_gu, gu_o, 768)
+    g_d = WeightGather(links, p, pk_d, d_o, 384)
+    own_cot = links.local(cot, cot_o.at[p.xh])
+    g_q.start0()
+    g_o.start0()
+
+    def norm_rows(block, start, count):
+        def body(i, _):
+            r = pl.ds(start + i * 32, 32)
+            xr[block, r] = unit_scale(hidg[block, r].astype(f32)).astype(bf16)
+            return 0
+
+        lax.fori_loop(0, count // 32, body, 0)
+
+    own_hidden.wait()
+    norm_rows(p.xh, 0, BLOCK)
+    g_q.start1()
+    g_o.start1()
+    g_q.start2()
+    g_o.start2()
+    g_gu.start0()
+    g_d.start0()
+
+    shared = []
+    for k in range(2):
+        hidden_sent[k].wait_recv()
+        part = hidg.at[1 - p.xh, rows[k]]
+        shared.append(links.send(part, part, sibling))
+    cot_sent = [links.send(cot.at[r], cot_o.at[p.xh, r], facing) for r in rows]
+    norm_rows(1 - p.xh, p.c * 256, 256)
+    for copy in shared:
+        copy.wait_recv()
+    norm_rows(1 - p.xh, (1 - p.c) * 256, 256)
+    xr_copy = links.local(xr, xr_o)
+
+    g_q.start3()
+    g_o.start3()
+    g_gu.start1()
+    g_d.start1()
+    g_q.done()
+
+    def project(i, _):
+        block, r = i // 2, (i % 2) * 256
+        w = wq[...].reshape(2048, 768)
+        out = jnp.dot(xr[block, pl.ds(r, 256)], w, preferred_element_type=f32).astype(bf16)
+        q_v[block, pl.ds(r, 256)] = out[:, :256]
+        kvx[block, pl.ds(r + WINDOW, 256)] = out[:, 256:]
+        return 0
+
+    lax.fori_loop(0, 4, project, 0)
+
+    tails = []
+    last = jnp.where(p.z == 3, 1, 0)
+    for block in range(2):
+        to_y = p.y if block == 0 else (p.y + last) % 4
+        slot = last if block == 0 else 1 - last
+        tails.append(
+            links.send(
+                kvx.at[block, pl.ds(BLOCK, WINDOW)],
+                kvx.at[slot, pl.ds(0, WINDOW)],
+                p.at(y=to_y, z=(p.z + 1) % 4),
+            )
+        )
+    g_gu.start2()
+    wq_copy = links.local(wq, wq_o)
+    q_copy = links.local(q_v, q_o)
+    bias_copy.wait()
+
+    def attend(block, chunk, head):
+        r, lane = pl.multiple_of(chunk * 128, 128), pl.multiple_of(head * 128, 128)
+        query = q_v[block, pl.ds(r, 128), pl.ds(lane, 128)]
+        keys = kvx[block, pl.ds(r, 192), pl.ds(lane, 128)]
+        values = kvx[block, pl.ds(r, 192), pl.ds(lane + 256, 128)]
+        scores = lax.dot_general(query, keys, TURNED, preferred_element_type=f32) * SCALE
+        scores = scores + bias[block * 4 + chunk]
+        expo = jnp.exp(scores - jnp.max(scores, axis=-1, keepdims=True))
+        probs = (expo / jnp.sum(expo, axis=-1, keepdims=True)).astype(bf16)
+        out = jnp.dot(probs, values, preferred_element_type=f32)
+        mixed[block, pl.ds(r, 128), pl.ds(lane, 128)] = out.astype(bf16)
+
+    def inner(i, _):
+        attend(i // 6, (i % 6) // 2 + 1, i % 2)
+        return 0
+
+    lax.fori_loop(0, 12, inner, 0)
+    for copy in tails:
+        copy.wait_recv()
+
+    def first(i, _):
+        attend(i // 2, 0, i % 2)
+        return 0
+
+    lax.fori_loop(0, 4, first, 0)
+    kv_copy = links.local(kvx, kv_o)
+    mixed_copy = links.local(mixed, mixed_o)
+    g_o.done()
+
+    def branch_all():
+        def sib(n, _):
+            lanes = pl.ds(pl.multiple_of(n * 256, 256), 256)
+            w = wo[n // 2, n % 2].reshape(256, 256)
+            for x in range(4):
+                left = mixed[x // 2, pl.ds((x % 2) * 256 + (1 - p.c) * OWNED, OWNED)]
+                part = lax.dot_general(left, w, TURNED, preferred_element_type=f32)
+                send_c[x, :, lanes] = part.astype(bf16)
+            return 0
+
+        lax.fori_loop(0, 8, sib, 0)
+        crossed = links.send(send_c, recv_c, sibling)
+
+        def mine(n, _):
+            lanes = pl.ds(pl.multiple_of(n * 256, 256), 256)
+            w = wo[n // 2, n % 2].reshape(256, 256)
+            for x in range(4):
+                left = mixed[x // 2, pl.ds((x % 2) * 256 + p.c * OWNED, OWNED)]
+                own[x, :, lanes] = lax.dot_general(left, w, TURNED, preferred_element_type=f32)
+            return 0
+
+        lax.fori_loop(0, 8, mine, 0)
+        return crossed
+
+    crossed = branch_all()
+    crossed.wait_recv()
+    arrived = []
+    for k in (2, 1, 3):
+        to = (p.x + k) % 4
+
+        def add(i, _):
+            r = pl.ds(i * 16, 16)
+            send_x[k - 1, r] = (own[to, r] + recv_c[to, r].astype(f32)).astype(bf16)
+            return 0
+
+        lax.fori_loop(0, OWNED // 16, add, 0)
+        arrived.append(links.send(send_x.at[k - 1], recv_x.at[k - 1], p.at(x=to)))
+    g_d.start2()
+    g_gu.start3()
+    for copy in arrived:
+        copy.wait_recv()
+
+    def finish(i, _):
+        r = pl.ds(i * 16, 16)
+        total = hidg[p.xh, pl.ds(p.q * OWNED + i * 16, 16)].astype(f32)
+        total = total + own[p.x, r] + recv_c[p.x, r].astype(f32)
+        for k in range(3):
+            total = total + recv_x[k, r].astype(f32)
+        own[p.x, r] = total
+        nm[r] = unit_scale(total).astype(bf16)
+        return 0
+
+    lax.fori_loop(0, OWNED // 16, finish, 0)
+    resid_copy = links.local(own.at[p.x], resid_o)
+    spread = [links.send(nm, nm_o.at[p.x, p.c], p.at(x=(p.x + k) % 4)) for k in (2, 1, 3)]
+    nm_copy = links.local(nm, nm_o.at[p.x, p.c])
+    paired = [links.send(nm, nm_o.at[p.x, p.c], sibling)]
+    wo_copy = links.local(wo, wo_o)
+    cot_shared = []
+    for k in range(2):
+        cot_sent[k].wait_recv()
+        part = cot_o.at[1 - p.xh, rows[k]]
+        cot_shared.append(links.send(part, part, sibling))
+    for i, k in ((1, 1), (2, 3), (0, 2)):
+        spread[i].wait_recv()
+        part = nm_o.at[(p.x + 4 - k) % 4, p.c]
+        paired.append(links.send(part, part, sibling))
+    g_d.start3()
+    for copy in paired + cot_shared:
+        copy.wait_recv()
+    g_gu.done()
+    g_d.done()
+    for copy in (own_cot, xr_copy, wq_copy, q_copy, kv_copy, mixed_copy, resid_copy, nm_copy, wo_copy):
+        copy.wait()
+    links.finish()
+
+
+def forward_call(pk_q, pk_o, pk_gu, pk_d, hid, cot, bias):
+    sds = jax.ShapeDtypeStruct
+    return pl.pallas_call(
+        forward_kernel,
+        out_shape=(
+            sds((4, 2, 4, 64, 768), bf16),
+            sds((4, 2, 4, 64, 256), bf16),
+            sds((4, 2, 4, 64, 1408), bf16),
+            sds((4, 2, 4, 64, 768), bf16),
+            sds((2, BLOCK, 2048), bf16),
+            sds((2, BLOCK, 256), bf16),
+            sds((2, BLOCK + WINDOW, 512), bf16),
+            sds((2, BLOCK, 256), bf16),
+            sds((OWNED, 2048), f32),
+            sds((4, 2, OWNED, 2048), bf16),
+            sds((2, BLOCK, 2048), bf16),
+        ),
+        in_specs=[ANY] * 7,
+        out_specs=[ANY] * 11,
+        scratch_shapes=[
+            pltpu.VMEM((4, 2, 4, 64, 768), bf16),
+            pltpu.VMEM((4, 2, 4, 64, 256), bf16),
+            pltpu.VMEM((2, BLOCK, 2048), bf16),
+            pltpu.VMEM((2, BLOCK, 2048), bf16),
+            pltpu.VMEM((2, BLOCK, 256), bf16),
+            pltpu.VMEM((2, BLOCK + WINDOW, 512), bf16),
+            pltpu.VMEM((2, BLOCK, 256), bf16),
+            pltpu.VMEM((8, 128, 192), f32),
+            pltpu.VMEM((4, OWNED, 2048), bf16),
+            pltpu.VMEM((4, OWNED, 2048), bf16),
+            pltpu.VMEM((4, OWNED, 2048), f32),
+            pltpu.VMEM((3, OWNED, 2048), bf16),
+            pltpu.VMEM((3, OWNED, 2048), bf16),
+            pltpu.VMEM((OWNED, 2048), bf16),
+            pltpu.SemaphoreType.DMA((100,)),
+            pltpu.SemaphoreType.DMA((100,)),
+            pltpu.SemaphoreType.DMA((20,)),
+        ],
+        compiler_params=pltpu.CompilerParams(
+            collective_id=0, has_side_effects=True, vmem_limit_bytes=56 * 2**20
+        ),
+        name="forward_attention",
+    )(pk_q, pk_o, pk_gu, pk_d, hid, cot, bias)
+
+
+def attention_bias(lengths):
+    y, z = lax.axis_index("y"), lax.axis_index("z")
+    starts = (y * 8 + z + 4 * jnp.arange(2, dtype=jnp.int32)) * BLOCK
+    starts = (starts[:, None] + 128 * jnp.arange(4, dtype=jnp.int32)).reshape(8, 1, 1)
+    query = starts + jnp.arange(128, dtype=jnp.int32)[None, :, None]
+    key = starts - WINDOW + jnp.arange(192, dtype=jnp.int32)[None, None, :]
+    ends = jnp.cumsum(lengths)
+    segment = lambda t: sum((t >= ends[k]).astype(jnp.int32) for k in range(3))
+    visible = (key <= query) & (key > query - WINDOW) & (key >= 0) & (segment(key) == segment(query))
+    return jnp.where(visible, 0.0, masked_score).astype(f32)
+
+
+def pack_ff(gate, up, down):
+    def tail(w):
+        return jnp.pad(w[:, 640:], ((0, 0), (0, 16)))
+
+    def one(k):
+        g, u, d = (w[:, k * 688 : (k + 1) * 688] for w in (gate, up, down))
+        return (
+            jnp.concatenate([g[:, :640], u[:, :640], tail(g), tail(u)], axis=1),
+            jnp.pad(d, ((0, 0), (0, 80))),
+        )
+
+    (gu0, d0), (gu1, d1) = one(0), one(1)
+    return jnp.stack([gu0, gu1]), jnp.stack([d0, d1])
+
+
+def pack_attn(query, key, value, out):
+    def one(k):
+        part = slice(k * 256, (k + 1) * 256)
+        return jnp.concatenate([query[:, part], key[:, part], value[:, part]], axis=1), out[:, part]
+
+    (q0, o0), (q1, o1) = one(0), one(1)
+    return jnp.stack([q0, q1]), jnp.stack([o0, o1])
+
+
 def per_device(
     hidden_in,
     norm_gain_attn,
@@ -218,44 +656,34 @@
     cotangent,
 ):
     xh, xl, c = lax.axis_index("xh"), lax.axis_index("xl"), lax.axis_index("c")
-
-    def halves(w):
-        n = w.shape[1] // 2
-        return jnp.where(xh == 0, w[:, :n], w[:, n:]), jnp.where(xh == 0, w[:, n:], w[:, :n])
-
-    def swap(pairs):
-        mine = jnp.concatenate([p[0] for p in pairs], axis=1)
-        theirs = jnp.concatenate([p[1] for p in pairs], axis=1)
-        return in_order(xh, mine[None], flip(theirs, "xh")[None], 0)
-
-    gains = jnp.stack([norm_gain_attn, norm_gain_mlp], axis=1)
-    gains = jnp.pad(gains, ((0, 0), (0, 126)))
-    attn_pack = swap([halves(w) for w in (w_query, w_key, w_value, w_out.T)] + [(gains, gains)])
-    ff_pack = swap([halves(w) for w in (w_gate, w_up, w_down.T)])
-    attn_a, attn_b = gather_weights(attn_pack)
-    attn = jnp.concatenate([attn_a, attn_b], axis=1)
-    qkv_w = attn[:, :768]
-    out_w = attn[:, 768:1024]
-    gain_attn = attn[:, 1024].astype(f32)
-    gain_mlp = attn[:, 1025].astype(f32)
-
-    hidden = gather_block(hidden_in)
-    cot = gather_block(cotangent)
+    gain_attn = norm_gain_attn.astype(f32)[:, None]
+    gain_mlp = norm_gain_mlp.astype(f32)[:, None]
+    scaled = lambda w, g: (w.astype(f32) * g).astype(bf16)
+    pk_q, pk_o = pack_attn(
+        scaled(w_query, gain_attn), scaled(w_key, gain_attn), scaled(w_value, gain_attn), w_out.T
+    )
+    pk_gu, pk_d = pack_ff(scaled(w_gate, gain_mlp), scaled(w_up, gain_mlp), w_down.T)
+    bias = attention_bias(lengths)
+    wq, wo, gu, d, xr, queries, kv_ext, mixed, resid, nm, cot = forward_call(
+        pk_q, pk_o, pk_gu, pk_d, hidden_in, cotangent, bias
+    )
+    qkv_w = wq.reshape(2048, 768)
+    out_w = wo.reshape(2048, 256)
+    gu = gu.reshape(2048, 1408)
+    gate_w = jnp.concatenate([gu[:, :640], gu[:, 1280:1328]], axis=1)
+    up_w = jnp.concatenate([gu[:, 640:1280], gu[:, 1344:1392]], axis=1)
+    down_w = d.reshape(2048, 768)[:, :688]
+    normed_attn = xr.reshape(1024, 2048)
+    mixed = mixed.reshape(1024, 256)
+    normed_mlp = nm.reshape(1024, 2048)
+    cot = cot.reshape(1024, 2048)
+
     q = xl * 2 + c
     owned_rows = lambda a: lax.dynamic_slice_in_dim(a, q * OWNED, OWNED, 0)
     hidden_owned = owned_rows(hidden_in).astype(f32)
     cot_owned = owned_rows(cotangent).astype(f32)
-
-    ff_a, ff_b = gather_weights(ff_pack)
-    ff = jnp.concatenate([ff_a, ff_b], axis=1)
-    gate_w, up_w, down_w = ff[:, :688], ff[:, 688:1376], ff[:, 1376:]
-
     visible = visibility(lengths)
-    normed_attn = rms_scale(hidden.astype(f32), gain_attn).astype(bf16)
-    qkv = dot_plain(normed_attn, qkv_w).astype(bf16)
-    queries = qkv[:, :256].reshape(16, WINDOW, 2, HEAD_DIM)
-    kv = qkv[:, 256:].reshape(2, BLOCK, 512)
-    kv_ext = jnp.concatenate([tails_forward(kv[:, -WINDOW:]), kv], axis=1)
+    queries = queries.reshape(16, WINDOW, 2, HEAD_DIM)
     key_blocks = band_blocks(kv_ext[..., :256]).reshape(16, 2 * WINDOW, 2, HEAD_DIM)
     value_blocks = band_blocks(kv_ext[..., 256:]).reshape(16, 2 * WINDOW, 2, HEAD_DIM)
     scores = score_blocks(queries, key_blocks, visible)
@@ -263,10 +691,6 @@
     expo = jnp.exp(scores - highest)
     probs = expo / jnp.sum(expo, axis=-1, keepdims=True)
     probs_low = probs.astype(bf16)
-    mixed = jnp.einsum("bhqk,bkhd->bqhd", probs_low, value_blocks, preferred_element_type=f32)
-    mixed = mixed.reshape(1024, 256).astype(bf16)
-    resid = hidden_owned + reduce_group(dot_right_turned(mixed, out_w))
-    normed_mlp = gather_group(rms_scale(resid, gain_mlp).astype(bf16))
 
     gate = dot_plain(normed_mlp, gate_w)
     up = dot_plain(normed_mlp, up_w)
@@ -288,14 +712,11 @@
     grad_ff = jnp.concatenate([grad_gate, grad_up, grad_down], axis=1)
     grad_ff = reduce_weights(grad_ff[:, :1024], grad_ff[:, 1024:])
 
-    def norm_back(grad, values, gain):
+    def norm_back(e, values):
         r = lax.rsqrt(jnp.mean(values * values, axis=-1, keepdims=True) + epsilon)
-        e = grad * gain
-        back = r * e - values * r**3 * jnp.mean(e * values, axis=-1, keepdims=True)
-        return back, jnp.sum(grad * values * r, axis=0)
-
-    back, grad_gain_mlp = norm_back(grad_normed_mlp, resid, gain_mlp)
-    grad_resid = cot_owned + back
+        return r * e - values * r**3 * jnp.mean(e * values, axis=-1, keepdims=True)
+
+    grad_resid = cot_owned + norm_back(grad_normed_mlp, resid)
     grad_branch = gather_group(grad_resid.astype(bf16))
     grad_out = dot_left_turned(grad_branch, mixed).astype(bf16)
     grad_mixed = dot_plain(grad_branch, out_w).astype(bf16).reshape(16, WINDOW, 2, HEAD_DIM)
@@ -318,12 +739,9 @@
     grad_qkv_act = jnp.concatenate([grad_queries.reshape(1024, 256), grad_kv], axis=1).astype(bf16)
     grad_normed_attn = reduce_group(dot_right_turned(grad_qkv_act, qkv_w))
     grad_qkv = dot_left_turned(normed_attn, grad_qkv_act).astype(bf16)
-    back, grad_gain_attn = norm_back(grad_normed_attn, hidden_owned, gain_attn)
-    input_grad = gather_owned((grad_resid + back).astype(bf16))
-
-    grad_gains = jnp.stack([grad_gain_attn, grad_gain_mlp], axis=1)
-    grad_gains = jnp.pad(grad_gains, ((0, 0), (0, 126))).astype(bf16)
-    grad_attn = jnp.concatenate([grad_qkv, grad_out, grad_gains], axis=1)
+    input_grad = gather_owned((grad_resid + norm_back(grad_normed_attn, hidden_owned)).astype(bf16))
+
+    grad_attn = jnp.concatenate([grad_qkv, grad_out], axis=1)
     grad_attn = reduce_weights(grad_attn[:, :512], grad_attn[:, 512:])
 
     def unswap(pack):
@@ -336,20 +754,28 @@
     def whole(mine, other, start, width):
         return in_order(xh, mine[:, start : start + width], other[:, start : start + width], 1).astype(f32)
 
-    grads_gain = mine_a[:, 1024:1026].astype(f32) + other_a[:, 1024:1026].astype(f32)
+    dq, dk, dv = (whole(mine_a, other_a, 256 * i, 256) for i in range(3))
+    dg, du = (whole(mine_f, other_f, 688 * i, 688) for i in range(2))
+
+    def dots(pairs):
+        return sum(jnp.sum(w.astype(f32) * g, axis=1) for w, g in pairs)
+
+    grads_gain = jnp.stack(
+        [dots([(w_query, dq), (w_key, dk), (w_value, dv)]), dots([(w_gate, dg), (w_up, du)])]
+    )
     grads_gain = grads_gain + flip(grads_gain, "xl")
     grads_gain = grads_gain + flip(grads_gain, "c")
     return (
         result,
         input_grad,
-        grads_gain[:, 0],
-        whole(mine_a, other_a, 0, 256),
-        whole(mine_a, other_a, 256, 256),
-        whole(mine_a, other_a, 512, 256),
+        grads_gain[0],
+        dq * gain_attn,
+        dk * gain_attn,
+        dv * gain_attn,
         whole(mine_a, other_a, 768, 256).T,
-        grads_gain[:, 1],
-        whole(mine_f, other_f, 0, 688),
-        whole(mine_f, other_f, 688, 688),
+        grads_gain[1],
+        dg * gain_mlp,
+        du * gain_mlp,
         whole(mine_f, other_f, 1376, 688).T,
     )
 

time: 672 us -> 574 us (0.85)
  Pallas kernels: 0 us -> 129 us
  waiting for transfers between devices: 189 us -> 108 us
  starting transfers between devices: 187 us -> 109 us
  local copies, waits for them, and re-layouts: 112 us -> 82 us
  matrix products: 94.5 us -> 74.4 us
  other arithmetic: 78.1 us -> 63.2 us
    pallas_call x0 -> x1, Pallas kernels: none -> 129 us  [forward_call(): pl.pallas_call(forward_kernel, out_shape=(sds((4, 2, 4, 64, 768), bf16),...]
    ppermute x100 -> x61, waiting for transfers between devices: 175 us -> 91.6 us  [shift(): return lax.ppermute(value, axis, [(i, (i + steps) % 4) for i in range(4)])]
    ppermute x100 -> x61, starting transfers between devices: 127 us -> 71.4 us  [shift(): return lax.ppermute(value, axis, [(i, (i + steps) % 4) for i in range(4)])]
    ppermute x18 -> x12, starting transfers between devices: 56.3 us -> 35.8 us  [flip(): return lax.ppermute(value, axis, [(0, 1), (1, 0)])]
    dynamic_update_slice x30 -> x3, local copies, waits for them, and re-layouts: 18.7 us -> 2.48 us  [place(): total = lax.dynamic_update_slice_in_dim(total, piece, (index + k) % 4, axis)]
    select_n x10 -> x5, other arithmetic: 24.1 us -> 9.4 us  [in_order(): jnp.where(flag == 0, jnp.concatenate([mine, other], axis=axis), jnp.conca...]
    dot_general x5 -> x4, matrix products: 28.8 us -> 15.5 us  [dot_plain(): return jnp.dot(left, right, preferred_element_type=f32)]
    dot_general x5 -> x4, matrix products: 25.4 us -> 28.8 us  [dot_right_turned(): lax.dot_general(left, right, (((1,), (1,)), ((), ())), preferred_element_...]
  transfers between devices with their start and end apart: 122 -> 74, of which waited for: 37 -> 22; matrix products, arithmetic and copies ran while one was open for 32% -> 28% of each run, Pallas kernels for 0% -> 0%
where the time goes in v2:
time: 574 us; the launch traced here: 568 us
  Pallas kernels  129 us (22%)
  starting transfers between devices  109 us (19%)
  waiting for transfers between devices  108 us (19%)
  local copies, waits for them, and re-layouts  82 us (14%)
  matrix products  74.4 us (13%)
  other arithmetic  63.2 us (11%)
    pallas_call x1, Pallas kernels, forward_call(): pl.pallas_call(forward_kernel, out_shape=(sds((4, 2, 4, 64, 768), bf16),...  129 us
    ppermute x61, waiting for transfers between devices, shift(): return lax.ppermute(value, axis, [(i, (i + steps) % 4) for i in range(4)])  91.6 us
    ppermute x61, starting transfers between devices, shift(): return lax.ppermute(value, axis, [(i, (i + steps) % 4) for i in range(4)])  71.4 us
    ppermute x12, starting transfers between devices, flip(): return lax.ppermute(value, axis, [(0, 1), (1, 0)])  35.8 us
    dot_general x4, matrix products, dot_right_turned(): lax.dot_general(left, right, (((1,), (1,)), ((), ())), preferred_element_...  28.8 us
    dot_general x5, matrix products, dot_left_turned(): lax.dot_general(left, right, (((0,), (0,)), ((), ())), preferred_element_...  18.4 us
    ppermute x12, waiting for transfers between devices, flip(): return lax.ppermute(value, axis, [(0, 1), (1, 0)])  16.2 us
    dot_general x4, matrix products, dot_plain(): return jnp.dot(left, right, preferred_element_type=f32)  15.5 us
  transfers between devices with their start and end apart: 74, of which 22 were waited for; matrix products, arithmetic and copies ran while one was open for 28% of the time, Pallas kernels for 0%

profile of v2, /device:TPU:1, one launch (start us, length us, event | category | flops | bytes accessed | tf_op | source)
XLA Modules:
  0.0 567.6 jit_solution(1980203029425434710)
XLA Ops:
  16.4 129.3 %forward_attention.1 = (bf16[4,2,4,64,768]{4,3,2,1,0:T(8,128)(2,1)}, bf16[4,2,4,64,256]{4,3,2,1,0:T(8,128)(2,1)}, bf16[4,2,4,64,1408]{4,3,2,1,0:T(8,128)(2,1)}, ...) custom-call(bf16[2,64,768]{2,1,0:T(8,128)(2,1)} %pad_maximum_fusion., ...), custom_call_target="tpu_custom_call" | custom-call | tf_op jit(solution)/shard_map/forward_attention/pallas_call | solution.py:565
  145.7 4.5 fusion.90
  153.3 5.3 fusion.10
  161.9 5.7 multiply_convert_fusion
  176.6 6.4 %copy.106 = bf16[2048,1024]{1,0:T(8,128)(2,1)} copy(bf16[2048,1024]{0,1:T(8,128)(2,1)} %pad_maximum_fusion.1) | data formatting | bytes 8388608 | tf_op jit(solution)/shard_map/slice | solution.py:713
  188.6 5.7 %convolution_convert_fusion.1 = bf16[2048,688]{0,1:T(8,128)(2,1)S(1)} fusion(bf16[1024,688]{0,1:T(8,128)(2,1)} %get-tuple-element.53, bf16[1024,2048]{1,0:T(8,128)(2,1)} %bitcast.292), kind=kOutput, calls=%fused_computation.12 | convolution fusion | flops 2887090176 | bytes 8421376 | tf_op jit(solution)/shard_map/dot_general | solution.py:40
  196.8 6.4 %copy.107 = bf16[2048,1040]{1,0:T(8,128)(2,1)} copy(bf16[2048,1040]{0,1:T(8,128)(2,1)} %pad_maximum_fusion) | data formatting | bytes 8519680 | tf_op jit(solution)/shard_map/slice | solution.py:713
  209.4 7.7 %fusion.4 = f32[1024,2048]{1,0:T(8,128)} fusion(bf16[1024,688]{0,1:T(8,128)(2,1)S(1)} %copy-done.48, bf16[2048,768]{1,0:T(8,128)(2,1)} %bitcast.299), kind=kOutput, calls=%fused_computation.29 | convolution fusion | flops 2885681152 | bytes 12943360 | tf_op jit(solution)/shard_map/dot_general | solution.py:36
  217.1 9.3 %fusion.11 = f32[1024,2048]{1,0:T(8,128)} fusion(bf16[1024,688]{0,1:T(8,128)(2,1)} %copy-done.47, bf16[2048,48]{1,0:T(8,128)(2,1)} %get-tuple-element.49, bf16[2048,640]{1,0:T(8,128)(2,1)} %get-tuple-element.47), kind=kOutput, calls=%fused_computation.44 | convolution fusion | flops 2891317248 | bytes 12615680 | tf_op jit(solution)/shard_map/dot_general | solution.py:36
  226.8 8.3 %convolution_add_fusion = f32[1024,2048]{1,0:T(8,128)} fusion(f32[1024,2048]{1,0:T(8,128)} %fusion.11, bf16[1024,688]{0,1:T(8,128)(2,1)} %copy-done.46, bf16[2048,48]{1,0:T(8,128)(2,1)S(1)} %get-tuple-element.50, bf16[2048,640]{1,0:T(8,128)(2,1)S(1)} %copy-done.15), kind=kOutput, calls=%fused_computation.10 | convolution fusion | flops 2893414400 | bytes 21004288 | tf_op jit(solution)/shard_map/dot_general | solution.py:36
  269.2 7.4 %collective-permute-done.48 = bf16[1,2,4,32,1024]{4,3,2,1,0:T(8,128)(2,1)S(1)} collective-permute-done((bf16[1,2,4,32,1024]{4,3,2,1,0:T(8,128)(2,1)S(1)}, bf16[1,2,4,32,1024]{4,3,2,1,0:T(8,128)(2,1)S(1)}, u32[]{:S(2)}, u32[]{:S(2)}) %collective-permute-start.48) | collective-permute-done | bytes 524320 | tf_op jit(solution)/shard_map/ppermute | solution.py:24
  287.1 7.6 %collective-permute-done.60 = bf16[4,2,1,32,1040]{4,3,2,1,0:T(8,128)(2,1)S(1)} collective-permute-done((bf16[4,2,1,32,1040]{4,3,2,1,0:T(8,128)(2,1)S(1)}, bf16[4,2,1,32,1040]{4,3,2,1,0:T(8,128)(2,1)S(1)}, u32[]{:S(2)}, u32[]{:S(2)}) %collective-permute-start.60) | collective-permute-done | bytes 532512 | tf_op jit(solution)/shard_map/ppermute | solution.py:24
  319.4 7.4 %collective-permute-done.9 = bf16[128,2048]{1,0:T(8,128)(2,1)S(1)} collective-permute-done((bf16[128,2048]{1,0:T(8,128)(2,1)S(1)}, bf16[128,2048]{1,0:T(8,128)(2,1)S(1)}, u32[]{:S(2)}, u32[]{:S(2)}) %collective-permute-start.9) | collective-permute-done | bytes 524320 | tf_op jit(solution)/shard_map/ppermute | solution.py:24
  327.9 9.1 %collective-permute-done.1 = bf16[128,2048]{1,0:T(8,128)(2,1)S(1)} collective-permute-done((bf16[128,2048]{1,0:T(8,128)(2,1)S(1)}, bf16[128,2048]{1,0:T(8,128)(2,1)S(1)}, u32[]{:S(2)}, u32[]{:S(2)}) %collective-permute-start.1) | collective-permute-done | bytes 524320 | tf_op jit(solution)/shard_map/ppermute | solution.py:24
  339.5 9.9 %collective-permute-done.3 = bf16[128,2048]{1,0:T(8,128)(2,1)S(1)} collective-permute-done((bf16[128,2048]{1,0:T(8,128)(2,1)S(1)}, bf16[128,2048]{1,0:T(8,128)(2,1)S(1)}, u32[]{:S(2)}, u32[]{:S(2)}) %collective-permute-start.3) | collective-permute-done | bytes 524320 | tf_op jit(solution)/shard_map/ppermute | solution.py:24
  369.7 8.8 %collective-permute-done.12 = bf16[1,128,2048]{2,1,0:T(8,128)(2,1)S(1)} collective-permute-done((bf16[1,128,2048]{2,1,0:T(8,128)(2,1)S(1)}, bf16[1,128,2048]{2,1,0:T(8,128)(2,1)S(1)}, u32[]{:S(2)}, u32[]{:S(2)}) %collective-permute-start.12) | collective-permute-done | bytes 524320 | tf_op jit(solution)/shard_map/ppermute | solution.py:24
  379.3 12.7 %collective-permute-start.13 = (bf16[4,1,128,2048]{3,2,1,0:T(8,128)(2,1)}, bf16[4,1,128,2048]{3,2,1,0:T(8,128)(2,1)}, u32[]{:S(2)}, u32[]{:S(2)}) collective-permute-start(bf16[4,1,128,2048]{3,2,1,0:T(8,128)(2,1)} %bitcast_dynamic-update-slice_fusion), channel_id=1, source_target_pairs={{0,1},{1,0},{2,3},{3,2},{4,5},{5,4},{6,7},{7,6},{8,9},{9,8},{10,11... | collective-permute-start | bytes 6291464 | tf_op jit(solution)/shard_map/ppermute | solution.py:28
  395.4 7.6 %collective-permute-done.71 = bf16[64,2064]{1,0:T(8,128)(2,1)S(1)} collective-permute-done((bf16[64,2064]{1,0:T(8,128)(2,1)}, bf16[64,2064]{1,0:T(8,128)(2,1)S(1)}, u32[]{:S(2)}, u32[]{:S(2)}) %collective-permute-start.71) | collective-permute-done | bytes 264224 | tf_op jit(solution)/shard_map/ppermute | solution.py:28
  405.9 4.2 maximum_select_fusion
  414.4 7.1 %convolution_bitcast_fusion = f32[16,128,2,128]{1,3,2,0:T(8,128)} fusion(bf16[16,64,2,128]{3,2,1,0:T(2,128)(2,1)} %reshape.1057, f32[16,2,64]{2,1,0:T(2,128)S(1)} %copy-done.33, f32[16,2,64,128]{3,2,1,0:T(8,128)} %copy-done.9), kind=kOutput, calls=%fused_computation.47 | convolution fusion | flops 67897472 | bytes 3678208 | tf_op jit(solution)/shard_map/bhqk,bqhd->bkhd/dot_general | solution.py:733
  512.1 5.6 collective-permute-start.5
  526.9 8.1 %collective-permute-done.17 = bf16[128,2048]{1,0:T(8,128)(2,1)S(1)} collective-permute-done((bf16[128,2048]{1,0:T(8,128)(2,1)S(1)}, bf16[128,2048]{1,0:T(8,128)(2,1)S(1)}, u32[]{:S(2)}, u32[]{:S(2)}) %collective-permute-start.17) | collective-permute-done | bytes 524320 | tf_op jit(solution)/shard_map/ppermute | solution.py:24
  535.0 10.8 %collective-permute-done.19 = bf16[128,2048]{1,0:T(8,128)(2,1)S(1)} collective-permute-done((bf16[128,2048]{1,0:T(8,128)(2,1)S(1)}, bf16[128,2048]{1,0:T(8,128)(2,1)S(1)}, u32[]{:S(2)}, u32[]{:S(2)}) %collective-permute-start.19) | collective-permute-done | bytes 524320 | tf_op jit(solution)/shard_map/ppermute | solution.py:24
  550.3 8.1 %collective-permute-done.20 = bf16[128,2048]{1,0:T(8,128)(2,1)S(1)} collective-permute-done((bf16[128,2048]{1,0:T(8,128)(2,1)S(1)}, bf16[128,2048]{1,0:T(8,128)(2,1)S(1)}, u32[]{:S(2)}, u32[]{:S(2)}) %collective-permute-start.20) | collective-permute-done | bytes 524320 | tf_op jit(solution)/shard_map/ppermute | solution.py:28
  (418 shorter events, 262.2 us)
Async XLA Ops:
  185.9 68.6 %collective-permute-start.47 = (bf16[1,2,4,32,1024]{4,3,2,1,0:T(8,128)(2,1)}, bf16[1,2,4,32,1024]{4,3,2,1,0:T(8,128)(2,1)}, u32[]{:S(2)}, u32[]{:S(2)}) collective-permute-start(bf16[1,2,4,32,1024]{4,3,2,1,0:T(8,128)(2,1)} %get-tuple-element.61), channel_id=1, source_target_pairs={{0,32},{32,64},{64,96},{96,0},{1,33},{33,65},{65,97},{97,1},{2,34}... | collective-permute-start | bytes 1572872 | tf_op jit(solution)/shard_map/ppermute | solution.py:24
  185.9 71.4 %collective-permute-start.51 = (bf16[1,2,4,32,1024]{4,3,2,1,0:T(8,128)(2,1)}, bf16[1,2,4,32,1024]{4,3,2,1,0:T(8,128)(2,1)}, u32[]{:S(2)}, u32[]{:S(2)}) collective-permute-start(bf16[1,2,4,32,1024]{4,3,2,1,0:T(8,128)(2,1)} %get-tuple-element.62), channel_id=1, source_target_pairs={{0,96},{32,0},{64,32},{96,64},{1,97},{33,1},{65,33},{97,65},{2,98}... | collective-permute-start | bytes 1572872 | tf_op jit(solution)/shard_map/ppermute | solution.py:24
  188.6 77.8 %collective-permute-start.49 = (bf16[1,2,4,32,1024]{4,3,2,1,0:T(8,128)(2,1)}, bf16[1,2,4,32,1024]{4,3,2,1,0:T(8,128)(2,1)}, u32[]{:S(2)}, u32[]{:S(2)}) collective-permute-start(bf16[1,2,4,32,1024]{4,3,2,1,0:T(8,128)(2,1)} %get-tuple-element.63), channel_id=1, source_target_pairs={{0,32},{32,64},{64,96},{96,0},{1,33},{33,65},{65,97},{97,1},{2,34}... | collective-permute-start | bytes 1572872 | tf_op jit(solution)/shard_map/ppermute | solution.py:24
  206.4 55.4 %collective-permute-start.59 = (bf16[4,2,1,32,1040]{4,3,2,1,0:T(8,128)(2,1)}, bf16[4,2,1,32,1040]{4,3,2,1,0:T(8,128)(2,1)}, u32[]{:S(2)}, u32[]{:S(2)}) collective-permute-start(bf16[4,2,1,32,1040]{4,3,2,1,0:T(8,128)(2,1)} %get-tuple-element.55), channel_id=1, source_target_pairs={{0,4},{4,8},{8,12},{12,0},{1,5},{5,9},{9,13},{13,1},{2,6},{6,10},{... | collective-permute-start | bytes 1597448 | tf_op jit(solution)/shard_map/ppermute | solution.py:24
  206.4 55.5 %collective-permute-start.63 = (bf16[4,2,1,32,1040]{4,3,2,1,0:T(8,128)(2,1)}, bf16[4,2,1,32,1040]{4,3,2,1,0:T(8,128)(2,1)}, u32[]{:S(2)}, u32[]{:S(2)}) collective-permute-start(bf16[4,2,1,32,1040]{4,3,2,1,0:T(8,128)(2,1)} %get-tuple-element.56), channel_id=1, source_target_pairs={{0,12},{4,0},{8,4},{12,8},{1,13},{5,1},{9,5},{13,9},{2,14},{6,2},{... | collective-permute-start | bytes 1597448 | tf_op jit(solution)/shard_map/ppermute | solution.py:24
  257.3 46.6 %collective-permute-start.6 = (bf16[4,128,2048]{2,1,0:T(8,128)(2,1)S(1)}, bf16[4,128,2048]{2,1,0:T(8,128)(2,1)S(1)}, u32[]{:S(2)}, u32[]{:S(2)}) collective-permute-start(bf16[4,128,2048]{2,1,0:T(8,128)(2,1)S(1)} %fusion.8), channel_id=1, source_target_pairs={{0,1},{1,0},{2,3},{3,2},{4,5},{5,4},{6,7},{7,6},{8,9},{9,8},{10,11... | collective-permute-start | bytes 6291464 | tf_op jit(solution)/shard_map/ppermute | solution.py:28
  266.5 19.2 %collective-permute-start.62 = (bf16[4,2,1,32,1040]{4,3,2,1,0:T(8,128)(2,1)S(1)}, bf16[4,2,1,32,1040]{4,3,2,1,0:T(8,128)(2,1)S(1)}, u32[]{:S(2)}, u32[]{:S(2)}) collective-permute-start(bf16[4,2,1,32,1040]{4,3,2,1,0:T(8,128)(2,1)S(1)} %copy-done.22), channel_id=1, source_target_pairs={{0,12},{4,0},{8,4},{12,8},{1,13},{5,1},{9,5},{13,9},{2,14},{6,2},{... | collective-permute-start | bytes 1597448 | tf_op jit(solution)/shard_map/ppermute | solution.py:24
  276.6 18.0 %collective-permute-start.60 = (bf16[4,2,1,32,1040]{4,3,2,1,0:T(8,128)(2,1)S(1)}, bf16[4,2,1,32,1040]{4,3,2,1,0:T(8,128)(2,1)S(1)}, u32[]{:S(2)}, u32[]{:S(2)}) collective-permute-start(bf16[4,2,1,32,1040]{4,3,2,1,0:T(8,128)(2,1)S(1)} %get-tuple-element.59), channel_id=1, source_target_pairs={{0,4},{4,8},{8,12},{12,0},{1,5},{5,9},{9,13},{13,1},{2,6},{6,10},{... | collective-permute-start | bytes 1597448 | tf_op jit(solution)/shard_map/ppermute | solution.py:24
  283.9 24.1 %collective-permute-start = (bf16[4,128,2048]{2,1,0:T(8,128)(2,1)}, bf16[4,128,2048]{2,1,0:T(8,128)(2,1)S(1)}, u32[]{:S(2)}, u32[]{:S(2)}) collective-permute-start(bf16[4,128,2048]{2,1,0:T(8,128)(2,1)} %fusion.9), channel_id=1, source_target_pairs={{0,1},{1,0},{2,3},{3,2},{4,5},{5,4},{6,7},{7,6},{8,9},{9,8},{10,11... | collective-permute-start | bytes 6291464 | tf_op jit(solution)/shard_map/ppermute | solution.py:28
  294.6 58.2 %collective-permute-start.55 = (bf16[1,2,1,32,1024]{4,3,2,1,0:T(8,128)(2,1)}, bf16[1,2,1,32,1024]{4,3,2,1,0:T(8,128)(2,1)}, u32[]{:S(2)}, u32[]{:S(2)}) collective-permute-start(bf16[1,2,1,32,1024]{4,3,2,1,0:T(8,128)(2,1)} %get-tuple-element.104), channel_id=1, source_target_pairs={{0,4},{4,8},{8,12},{12,0},{1,5},{5,9},{9,13},{13,1},{2,6},{6,10},{... | collective-permute-start | bytes 393224 | tf_op jit(solution)/shard_map/ppermute | solution.py:24
  303.1 52.3 %collective-permute-start.56 = (bf16[1,2,1,32,1024]{4,3,2,1,0:T(8,128)(2,1)}, bf16[1,2,1,32,1024]{4,3,2,1,0:T(8,128)(2,1)}, u32[]{:S(2)}, u32[]{:S(2)}) collective-permute-start(bf16[1,2,1,32,1024]{4,3,2,1,0:T(8,128)(2,1)} %get-tuple-element.101), channel_id=1, source_target_pairs={{0,12},{4,0},{8,4},{12,8},{1,13},{5,1},{9,5},{13,9},{2,14},{6,2},{... | collective-permute-start | bytes 393224 | tf_op jit(solution)/shard_map/ppermute | solution.py:24
  309.3 17.5 %collective-permute-start.9 = (bf16[128,2048]{1,0:T(8,128)(2,1)S(1)}, bf16[128,2048]{1,0:T(8,128)(2,1)S(1)}, u32[]{:S(2)}, u32[]{:S(2)}) collective-permute-start(bf16[128,2048]{1,0:T(8,128)(2,1)S(1)} %get-tuple-element.88), channel_id=1, source_target_pairs={{0,16},{2,18},{16,0},{18,2},{1,17},{3,19},{17,1},{19,3},{4,20},{6,... | collective-permute-start | bytes 1572872 | tf_op jit(solution)/shard_map/ppermute | solution.py:24
  316.0 21.1 %collective-permute-start.1 = (bf16[128,2048]{1,0:T(8,128)(2,1)S(1)}, bf16[128,2048]{1,0:T(8,128)(2,1)S(1)}, u32[]{:S(2)}, u32[]{:S(2)}) collective-permute-start(bf16[128,2048]{1,0:T(8,128)(2,1)S(1)} %get-tuple-element.90), channel_id=1, source_target_pairs={{0,2},{2,16},{16,18},{18,0},{1,3},{3,17},{17,19},{19,1},{4,6},{6,2... | collective-permute-start | bytes 1572872 | tf_op jit(solution)/shard_map/ppermute | solution.py:24
  316.0 22.2 %collective-permute-start.2 = (bf16[128,2048]{1,0:T(8,128)(2,1)S(1)}, bf16[128,2048]{1,0:T(8,128)(2,1)S(1)}, u32[]{:S(2)}, u32[]{:S(2)}) collective-permute-start(bf16[128,2048]{1,0:T(8,128)(2,1)S(1)} %get-tuple-element.92), channel_id=1, source_target_pairs={{0,18},{2,0},{16,2},{18,16},{1,19},{3,1},{17,3},{19,17},{4,22},{6,... | collective-permute-start | bytes 1572872 | tf_op jit(solution)/shard_map/ppermute | solution.py:24
  326.9 22.5 %collective-permute-start.3 = (bf16[128,2048]{1,0:T(8,128)(2,1)S(1)}, bf16[128,2048]{1,0:T(8,128)(2,1)S(1)}, u32[]{:S(2)}, u32[]{:S(2)}) collective-permute-start(bf16[128,2048]{1,0:T(8,128)(2,1)S(1)} %get-tuple-element.91), channel_id=1, source_target_pairs={{0,16},{2,18},{16,0},{18,2},{1,17},{3,19},{17,1},{19,3},{4,20},{6,... | collective-permute-start | bytes 1572872 | tf_op jit(solution)/shard_map/ppermute | solution.py:24
  337.1 54.9 %collective-permute-start.67 = (bf16[1,2,1,32,1040]{4,3,2,1,0:T(8,128)(2,1)S(1)}, bf16[1,2,1,32,1040]{4,3,2,1,0:T(8,128)(2,1)S(1)}, u32[]{:S(2)}, u32[]{:S(2)}) collective-permute-start(bf16[1,2,1,32,1040]{4,3,2,1,0:T(8,128)(2,1)S(1)} %get-tuple-element.96), channel_id=1, source_target_pairs={{0,32},{32,64},{64,96},{96,0},{1,33},{33,65},{65,97},{97,1},{2,34}... | collective-permute-start | bytes 399368 | tf_op jit(solution)/shard_map/ppermute | solution.py:24
  352.9 39.1 %collective-permute-start.68 = (bf16[1,2,1,32,1040]{4,3,2,1,0:T(8,128)(2,1)S(1)}, bf16[1,2,1,32,1040]{4,3,2,1,0:T(8,128)(2,1)S(1)}, u32[]{:S(2)}, u32[]{:S(2)}) collective-permute-start(bf16[1,2,1,32,1040]{4,3,2,1,0:T(8,128)(2,1)S(1)} %get-tuple-element.93), channel_id=1, source_target_pairs={{0,96},{32,0},{64,32},{96,64},{1,97},{33,1},{65,33},{97,65},{2,98}... | collective-permute-start | bytes 399368 | tf_op jit(solution)/shard_map/ppermute | solution.py:24
  355.4 36.6 %collective-permute-start.66 = (bf16[1,2,1,32,1040]{4,3,2,1,0:T(8,128)(2,1)S(1)}, bf16[1,2,1,32,1040]{4,3,2,1,0:T(8,128)(2,1)S(1)}, u32[]{:S(2)}, u32[]{:S(2)}) collective-permute-start(bf16[1,2,1,32,1040]{4,3,2,1,0:T(8,128)(2,1)S(1)} %copy-done.32), channel_id=1, source_target_pairs={{0,32},{32,64},{64,96},{96,0},{1,33},{33,65},{65,97},{97,1},{2,34}... | collective-permute-start | bytes 399368 | tf_op jit(solution)/shard_map/ppermute | solution.py:24
  366.3 25.7 %collective-permute-start.70 = (bf16[1,2,1,32,1040]{4,3,2,1,0:T(8,128)(2,1)S(1)}, bf16[1,2,1,32,1040]{4,3,2,1,0:T(8,128)(2,1)S(1)}, u32[]{:S(2)}, u32[]{:S(2)}) collective-permute-start(bf16[1,2,1,32,1040]{4,3,2,1,0:T(8,128)(2,1)S(1)} %copy-done.31), channel_id=1, source_target_pairs={{0,96},{32,0},{64,32},{96,64},{1,97},{33,1},{65,33},{97,65},{2,98}... | collective-permute-start | bytes 399368 | tf_op jit(solution)/shard_map/ppermute | solution.py:24
  379.3 26.6 %collective-permute-start.13 = (bf16[4,1,128,2048]{3,2,1,0:T(8,128)(2,1)}, bf16[4,1,128,2048]{3,2,1,0:T(8,128)(2,1)}, u32[]{:S(2)}, u32[]{:S(2)}) collective-permute-start(bf16[4,1,128,2048]{3,2,1,0:T(8,128)(2,1)} %bitcast_dynamic-update-slice_fusion), channel_id=1, source_target_pairs={{0,1},{1,0},{2,3},{3,2},{4,5},{5,4},{6,7},{7,6},{8,9},{9,8},{10,11... | collective-permute-start | bytes 6291464 | tf_op jit(solution)/shard_map/ppermute | solution.py:28
  405.9 69.5 %collective-permute-start.4 = (bf16[128,2048]{1,0:T(8,128)(2,1)}, bf16[128,2048]{1,0:T(8,128)(2,1)}, u32[]{:S(2)}, u32[]{:S(2)}) collective-permute-start(bf16[128,2048]{1,0:T(8,128)(2,1)} %get-tuple-element.107), channel_id=1, source_target_pairs={{0,2},{2,0},{1,3},{3,1},{4,6},{6,4},{5,7},{7,5},{8,10},{10,8},{9,1... | collective-permute-start | bytes 1572872 | tf_op jit(solution)/shard_map/ppermute | solution.py:28
  475.4 45.6 %collective-permute-start.16 = (bf16[4,128,2048]{2,1,0:T(8,128)(2,1)S(1)}, bf16[4,128,2048]{2,1,0:T(8,128)(2,1)S(1)}, u32[]{:S(2)}, u32[]{:S(2)}) collective-permute-start(bf16[4,128,2048]{2,1,0:T(8,128)(2,1)S(1)} %fusion.7), channel_id=1, source_target_pairs={{0,1},{1,0},{2,3},{3,2},{4,5},{5,4},{6,7},{7,6},{8,9},{9,8},{10,11... | collective-permute-start | bytes 6291464 | tf_op jit(solution)/shard_map/ppermute | solution.py:28
  512.1 50.2 %collective-permute-start.5 = (bf16[2,1,128,2048]{3,2,1,0:T(8,128)(2,1)S(1)}, bf16[2,1,128,2048]{3,2,1,0:T(8,128)(2,1)S(1)}, u32[]{:S(2)}, u32[]{:S(2)}) collective-permute-start(bf16[2,1,128,2048]{3,2,1,0:T(8,128)(2,1)S(1)} %maximum_select_fusion.3), channel_id=1, source_target_pairs={{0,1},{1,0},{2,3},{3,2},{4,5},{5,4},{6,7},{7,6},{8,9},{9,8},{10,11... | collective-permute-start | bytes 3145736 | tf_op jit(solution)/shard_map/ppermute | solution.py:28
  525.2 20.6 %collective-permute-start.19 = (bf16[128,2048]{1,0:T(8,128)(2,1)S(1)}, bf16[128,2048]{1,0:T(8,128)(2,1)S(1)}, u32[]{:S(2)}, u32[]{:S(2)}) collective-permute-start(bf16[128,2048]{1,0:T(8,128)(2,1)S(1)} %get-tuple-element.81), channel_id=1, source_target_pairs={{0,16},{2,18},{16,0},{18,2},{1,17},{3,19},{17,1},{19,3},{4,20},{6,... | collective-permute-start | bytes 1572872 | tf_op jit(solution)/shard_map/ppermute | solution.py:24
  (105 other events, 975.6 us)

commit v3 on v2

--- a/solution.py
+++ b/solution.py
@@ -1,5 +1,3 @@
-import functools
-
 import jax
 import jax.numpy as jnp
 from jax import lax
@@ -12,7 +10,6 @@
 BLOCK = 512
 OWNED = 128
 AXES = ("y", "xh", "z", "xl", "c")
-RING = ("xh", "xl")
 
 epsilon = 1e-05
 masked_score = -1e30
@@ -20,191 +17,8 @@
 bf16 = jnp.bfloat16
 
 
-def shift(value, axis, steps):
-    return lax.ppermute(value, axis, [(i, (i + steps) % 4) for i in range(4)])
-
-
 def flip(value, axis):
     return lax.ppermute(value, axis, [(0, 1), (1, 0)])
-
-
-def dot_plain(left, right):
-    return jnp.dot(left, right, preferred_element_type=f32)
-
-
-def dot_right_turned(left, right):
-    return lax.dot_general(left, right, (((1,), (1,)), ((), ())), preferred_element_type=f32)
-
-
-def dot_left_turned(left, right):
-    return lax.dot_general(left, right, (((0,), (0,)), ((), ())), preferred_element_type=f32)
-
-
-def rms_scale(values, gain):
-    return values * lax.rsqrt(jnp.mean(values * values, axis=-1, keepdims=True) + epsilon) * gain
-
-
-def in_order(flag, mine, other, axis):
-    return jnp.where(
-        flag == 0,
-        jnp.concatenate([mine, other], axis=axis),
-        jnp.concatenate([other, mine], axis=axis),
-    )
-
-
-def pick(array, axis, index):
-    return lax.dynamic_slice_in_dim(array, index, 1, axis)
-
-
-def place(pieces, axis, index):
-    shape = list(pieces[0].shape)
-    shape[axis] = 4
-    total = jnp.zeros(shape, pieces[0].dtype)
-    for k, piece in enumerate(pieces):
-        total = lax.dynamic_update_slice_in_dim(total, piece, (index + k) % 4, axis)
-    return total
-
-
-def gather4(block, mesh_axis, axis, split):
-    index = lax.axis_index(mesh_axis)
-    before = shift(block, mesh_axis, 1)
-    after = shift(block, mesh_axis, -1)
-    half = block.shape[split] // 2
-    far = jnp.concatenate(
-        [
-            shift(lax.slice_in_dim(before, 0, half, axis=split), mesh_axis, 1),
-            shift(lax.slice_in_dim(after, half, 2 * half, axis=split), mesh_axis, -1),
-        ],
-        axis=split,
-    )
-    return place([block, after, far, before], axis, index)
-
-
-def reduce4(total, mesh_axis, axis, split):
-    index = lax.axis_index(mesh_axis)
-    half = total.shape[split] // 2
-    own, nxt, far, prev = [pick(total, axis, (index + k) % 4) for k in range(4)]
-    low = lambda a: lax.slice_in_dim(a, 0, half, axis=split)
-    high = lambda a: lax.slice_in_dim(a, half, 2 * half, axis=split)
-    add = lambda a, b: (a.astype(f32) + b.astype(f32)).astype(bf16)
-    from_prev = shift(low(far), mesh_axis, 1)
-    from_next = shift(high(far), mesh_axis, -1)
-    from_prev_own = shift(high(nxt), mesh_axis, 1)
-    from_next_own = shift(low(prev), mesh_axis, -1)
-    from_prev_sum = shift(add(low(nxt), from_prev), mesh_axis, 1)
-    from_next_sum = shift(add(high(prev), from_next), mesh_axis, -1)
-    got_prev = jnp.concatenate([from_prev_sum, from_prev_own], axis=split)
-    got_next = jnp.concatenate([from_next_own, from_next_sum], axis=split)
-    return (own.astype(f32) + got_prev.astype(f32) + got_next.astype(f32)).astype(bf16)
-
-
-def gather_weights(pack):
-    cols = pack.shape[2]
-    cut = cols // 256 * 128
-    a = pack[None, :, None, :, :cut]
-    b = pack[None, :, None, :, cut:]
-    a = gather4(gather4(a, "z", 2, 3), "y", 0, 3)
-    b = gather4(gather4(b, "y", 0, 3), "z", 2, 3)
-    return a.reshape(2048, cut), b.reshape(2048, cols - cut)
-
-
-def reduce_weights(a, b):
-    a = a.reshape(4, 2, 4, 64, a.shape[1])
-    b = b.reshape(4, 2, 4, 64, b.shape[1])
-    a = reduce4(reduce4(a, "y", 0, 3), "z", 2, 3)
-    b = reduce4(reduce4(b, "z", 2, 3), "y", 0, 3)
-    return jnp.concatenate([a[0, :, 0], b[0, :, 0]], axis=2)
-
-
-def gather_block(value):
-    c = lax.axis_index("c")
-    part = lax.dynamic_slice_in_dim(value, c * 256, 256, 0)
-    got = lax.ppermute(part, RING, [(i, 3 - i) for i in range(4)])
-    other = in_order(c, got, flip(got, "c"), 0)
-    return in_order(lax.axis_index("xh"), value, other, 0)
-
-
-def reduce_group(total):
-    c = lax.axis_index("c")
-    x = lax.axis_index(RING)
-    parts = total.reshape(4, 2, OWNED, 2048)
-    mine = pick(parts, 1, c)[:, 0]
-    theirs = pick(parts, 1, 1 - c)[:, 0].astype(bf16)
-    mine = mine + flip(theirs, "c").astype(f32)
-    low = mine.astype(bf16)
-    result = pick(mine, 0, x)[0]
-    for k in (1, 3, 2):
-        result = result + shift(pick(low, 0, (x + k) % 4)[0], RING, k).astype(f32)
-    return result
-
-
-def gather_group(owned):
-    c = lax.axis_index("c")
-    x = lax.axis_index(RING)
-    mine = owned[None]
-    pieces = [mine, shift(mine, RING, -1), shift(mine, RING, 2), shift(mine, RING, 1)]
-    half = place(pieces, 0, x)[:, None]
-    return in_order(c, half, flip(half, "c"), 1).reshape(1024, 2048)
-
-
-def gather_owned(owned):
-    pair = in_order(lax.axis_index("xl"), owned[None], flip(owned, "xl")[None], 0)[:, None]
-    return in_order(lax.axis_index("c"), pair, flip(pair, "c"), 1).reshape(BLOCK, 2048)
-
-
-def band_blocks(array):
-    shaped = array.reshape((2, 9, WINDOW) + array.shape[2:])
-    both = jnp.concatenate([shaped[:, :-1], shaped[:, 1:]], axis=2)
-    return both.reshape((16, 2 * WINDOW) + array.shape[2:])
-
-
-def fold_blocks(blocks):
-    shaped = blocks.reshape(2, 8, 2, WINDOW, -1)
-    edge = jnp.zeros((2, 1, WINDOW, shaped.shape[-1]), f32)
-    total = jnp.concatenate([shaped[:, :, 0], edge], axis=1) + jnp.concatenate(
-        [edge, shaped[:, :, 1]], axis=1
-    )
-    return total.reshape(2, 576, -1)
-
-
-def visibility(lengths):
-    y, z = lax.axis_index("y"), lax.axis_index("z")
-    starts = (y * 8 + z + 4 * jnp.arange(2, dtype=jnp.int32)) * BLOCK
-    positions = starts[:, None] - WINDOW + jnp.arange(BLOCK + WINDOW, dtype=jnp.int32)
-    ends = jnp.cumsum(lengths)
-    segment = jnp.sum((positions[..., None] >= ends).astype(jnp.int32), axis=-1)
-    key_pos = band_blocks(positions)
-    key_seg = band_blocks(segment)
-    query_pos = positions[:, WINDOW:].reshape(16, WINDOW)
-    query_seg = segment[:, WINDOW:].reshape(16, WINDOW)
-    visible = (key_pos[:, None, :] <= query_pos[:, :, None]) & (
-        key_pos[:, None, :] > query_pos[:, :, None] - WINDOW
-    )
-    return visible & (key_pos[:, None, :] >= 0) & (key_seg[:, None, :] == query_seg[:, :, None])
-
-
-YZ = ("y", "z")
-
-
-def tails_forward(tails):
-    z = lax.axis_index("z")
-    ring = shift(tails, "z", 1)
-    step = lax.ppermute(tails[1], YZ, [(4 * y + 3, 4 * y + 4) for y in range(3)])
-    return jnp.where(z == 0, jnp.stack([step, ring[0]]), ring)
-
-
-def tails_back(heads):
-    z = lax.axis_index("z")
-    ring = shift(heads, "z", -1)
-    step = lax.ppermute(heads[0], YZ, [(4 * y + 4, 4 * y + 3) for y in range(3)])
-    return jnp.where(z == 3, jnp.stack([ring[1], step]), ring)
-
-
-def score_blocks(query_blocks, key_blocks, visible):
-    scores = jnp.einsum(
-        "bqhd,bkhd->bhqk", query_blocks, key_blocks, preferred_element_type=f32
-    ) * HEAD_DIM ** (-0.5)
-    return jnp.where(visible[:, None], scores, masked_score)
 
 
 MESH = pl.DeviceIdType.MESH
@@ -460,7 +274,7 @@
         keys = kvx[block, pl.ds(r, 192), pl.ds(lane, 128)]
         values = kvx[block, pl.ds(r, 192), pl.ds(lane + 256, 128)]
         scores = lax.dot_general(query, keys, TURNED, preferred_element_type=f32) * SCALE
-        scores = scores + bias[block * 4 + chunk]
+        scores = scores + bias[block * 4 + chunk].astype(f32)
         expo = jnp.exp(scores - jnp.max(scores, axis=-1, keepdims=True))
         probs = (expo / jnp.sum(expo, axis=-1, keepdims=True)).astype(bf16)
         out = jnp.dot(probs, values, preferred_element_type=f32)
@@ -587,7 +401,7 @@
             pltpu.VMEM((2, BLOCK, 256), bf16),
             pltpu.VMEM((2, BLOCK + WINDOW, 512), bf16),
             pltpu.VMEM((2, BLOCK, 256), bf16),
-            pltpu.VMEM((8, 128, 192), f32),
+            pltpu.VMEM((8, 128, 192), bf16),
             pltpu.VMEM((4, OWNED, 2048), bf16),
             pltpu.VMEM((4, OWNED, 2048), bf16),
             pltpu.VMEM((4, OWNED, 2048), f32),
@@ -614,7 +428,7 @@
     ends = jnp.cumsum(lengths)
     segment = lambda t: sum((t >= ends[k]).astype(jnp.int32) for k in range(3))
     visible = (key <= query) & (key > query - WINDOW) & (key >= 0) & (segment(key) == segment(query))
-    return jnp.where(visible, 0.0, masked_score).astype(f32)
+    return jnp.where(visible, 0.0, masked_score).astype(bf16)
 
 
 def pack_ff(gate, up, down):
@@ -639,6 +453,609 @@
 
     (q0, o0), (q1, o1) = one(0), one(1)
     return jnp.stack([q0, q1]), jnp.stack([o0, o1])
+
+
+class WeightReduce:
+    def __init__(self, links, place, total, first_in, second_in, out, cut):
+        self.links, self.place, self.total, self.out = links, place, total, out
+        self.one, self.two = first_in, second_in
+        cols = total.shape[-1]
+        self.cols = cols
+        self.parts = (pl.ds(0, cut), pl.ds(cut, cols - cut))
+        p = place
+        self.yn, self.yp, self.yf = (p.y + 1) % 4, (p.y + 3) % 4, (p.y + 2) % 4
+        self.zn, self.zp, self.zf = (p.z + 1) % 4, (p.z + 3) % 4, (p.z + 2) % 4
+        self.next_y, self.prev_y = p.at(y=self.yn), p.at(y=self.yp)
+        self.next_z, self.prev_z = p.at(z=self.zn), p.at(z=self.zp)
+
+    def start0(self):
+        a, b = self.parts
+        t, one, send = self.total, self.one, self.links.send
+        self.far = [
+            send(t.at[self.yf, 0, :, :, a], one.at[0, :, :, a], self.next_y),
+            send(t.at[:, 0, self.zf, :, b], one.at[0, :, :, b], self.next_z),
+            send(t.at[self.yf, 1, :, :, a], one.at[2, :, :, a], self.prev_y),
+            send(t.at[:, 1, self.zf, :, b], one.at[2, :, :, b], self.prev_z),
+        ]
+        self.near = [
+            send(t.at[self.yn, 1, :, :, a], one.at[1, :, :, a], self.next_y),
+            send(t.at[:, 1, self.zn, :, b], one.at[1, :, :, b], self.next_z),
+            send(t.at[self.yp, 0, :, :, a], one.at[3, :, :, a], self.prev_y),
+            send(t.at[:, 0, self.zp, :, b], one.at[3, :, :, b], self.prev_z),
+        ]
+
+    def add(self, target, sources, rows):
+        def body(i, _):
+            ref = target(i)
+            value = ref[...].astype(f32)
+            for source in sources:
+                value = value + source(i)[...].astype(f32)
+            ref[...] = value.astype(bf16)
+            return 0
+
+        lax.fori_loop(0, rows, body, 0)
+
+    def start1(self):
+        a, b = self.parts
+        t, one, send = self.total, self.one, self.links.send
+        yn, yp, zn, zp = self.yn, self.yp, self.zn, self.zp
+        self.sums = []
+        self.far[0].wait_recv()
+        self.add(lambda i: t.at[yn, 0, i, :, a], [lambda i: one.at[0, i, :, a]], 4)
+        self.sums.append(send(t.at[yn, 0, :, :, a], one.at[4, :, :, a], self.next_y))
+        self.far[1].wait_recv()
+        self.add(lambda i: t.at[i, 0, zn, :, b], [lambda i: one.at[0, i, :, b]], 4)
+        self.sums.append(send(t.at[:, 0, zn, :, b], one.at[4, :, :, b], self.next_z))
+        self.far[2].wait_recv()
+        self.add(lambda i: t.at[yp, 1, i, :, a], [lambda i: one.at[2, i, :, a]], 4)
+        self.sums.append(send(t.at[yp, 1, :, :, a], one.at[5, :, :, a], self.prev_y))
+        self.far[3].wait_recv()
+        self.add(lambda i: t.at[i, 1, zp, :, b], [lambda i: one.at[2, i, :, b]], 4)
+        self.sums.append(send(t.at[:, 1, zp, :, b], one.at[5, :, :, b], self.prev_z))
+
+    def start2(self):
+        a, b = self.parts
+        t, one, two, send = self.total, self.one, self.two, self.links.send
+        p = self.place
+        for copy in self.near + self.sums:
+            copy.wait_recv()
+        self.add(lambda i: t.at[p.y, 0, i, :, a], [lambda i: one.at[3, i, :, a], lambda i: one.at[4, i, :, a]], 4)
+        self.add(lambda i: t.at[p.y, 1, i, :, a], [lambda i: one.at[1, i, :, a], lambda i: one.at[5, i, :, a]], 4)
+        self.add(lambda i: t.at[i, 0, p.z, :, b], [lambda i: one.at[3, i, :, b], lambda i: one.at[4, i, :, b]], 4)
+        self.add(lambda i: t.at[i, 1, p.z, :, b], [lambda i: one.at[1, i, :, b], lambda i: one.at[5, i, :, b]], 4)
+        self.far = [
+            send(t.at[p.y, 0, self.zf, :, a], two.at[0, :, a], self.next_z),
+            send(t.at[self.yf, 0, p.z, :, b], two.at[0, :, b], self.next_y),
+            send(t.at[p.y, 1, self.zf, :, a], two.at[2, :, a], self.prev_z),
+            send(t.at[self.yf, 1, p.z, :, b], two.at[2, :, b], self.prev_y),
+        ]
+        self.near = [
+            send(t.at[p.y, 1, self.zn, :, a], two.at[1, :, a], self.next_z),
+            send(t.at[self.yn, 1, p.z, :, b], two.at[1, :, b], self.next_y),
+            send(t.at[p.y, 0, self.zp, :, a], two.at[3, :, a], self.prev_z),
+            send(t.at[self.yp, 0, p.z, :, b], two.at[3, :, b], self.prev_y),
+        ]
+
+    def plus(self, target, *sources):
+        value = target[...].astype(f32)
+        for source in sources:
+            value = value + source[...].astype(f32)
+        target[...] = value.astype(bf16)
+
+    def start3(self):
+        a, b = self.parts
+        t, two, send = self.total, self.two, self.links.send
+        p = self.place
+        yn, yp, zn, zp = self.yn, self.yp, self.zn, self.zp
+        self.sums = []
+        for k, ref, lanes, slot, other, device in (
+            (0, t.at[p.y, 0, zn, :, a], a, 0, 4, self.next_z),
+            (1, t.at[yn, 0, p.z, :, b], b, 0, 4, self.next_y),
+            (2, t.at[p.y, 1, zp, :, a], a, 2, 5, self.prev_z),
+            (3, t.at[yp, 1, p.z, :, b], b, 2, 5, self.prev_y),
+        ):
+            self.far[k].wait_recv()
+            self.plus(ref, two.at[slot, :, lanes])
+            self.sums.append(send(ref, two.at[other, :, lanes], device))
+
+    def start4(self):
+        t, two, out = self.total, self.two, self.out
+        p = self.place
+        for copy in self.near + self.sums:
+            copy.wait_recv()
+        self.plus(t.at[p.y, 0, p.z], two.at[3], two.at[4])
+        self.plus(t.at[p.y, 1, p.z], two.at[1], two.at[5])
+        self.swap = self.links.send(t.at[p.y, 1 - p.xh, p.z], out.at[p.xh], p.at(x=(p.x + 2) % 4))
+        self.mine = self.links.local(t.at[p.y, p.xh, p.z], out.at[p.xh])
+
+    def done(self):
+        self.swap.wait_recv()
+        self.mine.wait()
+
+
+class GroupReduce:
+    def __init__(self, place, partial, bufs, sems):
+        self.place, self.partial = place, partial
+        self.send_c, self.recv_c, self.tmp, self.snd, self.rcv, self.own = bufs
+        self.send_sems, self.recv_sems = sems
+
+    def copy(self, src, dst, index, device):
+        return pltpu.make_async_remote_copy(
+            src_ref=src,
+            dst_ref=dst,
+            send_sem=self.send_sems.at[index],
+            recv_sem=self.recv_sems.at[index],
+            device_id=device,
+            device_id_type=MESH,
+        )
+
+    def crossing(self, n):
+        return self.copy(self.send_c.at[n], self.recv_c.at[n], n, self.place.at(c=1 - self.place.c))
+
+    def to_next(self, n):
+        pair = pl.ds(0, 2)
+        return self.copy(
+            self.snd.at[n, pair], self.rcv.at[n, pair], 4 + n, self.place.at(x=(self.place.x + 1) % 4)
+        )
+
+    def to_prev(self, n):
+        pair = pl.ds(2, 2)
+        return self.copy(
+            self.snd.at[n, pair], self.rcv.at[n, pair], 8 + n, self.place.at(x=(self.place.x + 3) % 4)
+        )
+
+    def sum_next(self, n):
+        return self.copy(
+            self.snd.at[n, 4], self.rcv.at[n, 4], 12 + n, self.place.at(x=(self.place.x + 1) % 4)
+        )
+
+    def sum_prev(self, n):
+        return self.copy(
+            self.snd.at[n, 5], self.rcv.at[n, 5], 16 + n, self.place.at(x=(self.place.x + 3) % 4)
+        )
+
+    def sibling_part(self, n):
+        part = self.partial(n, 1 - self.place.c)
+        self.send_c[n] = part.astype(bf16).reshape(4, OWNED, 512)
+        self.crossing(n).start()
+
+    def own_part(self, n):
+        p, tmp, snd = self.place, self.tmp, self.snd
+        part = self.partial(n, p.c).reshape(4, OWNED, 512)
+        self.crossing(n).wait_recv()
+        tmp[...] = part + self.recv_c[n].astype(f32)
+        far, nxt, prev = (p.x + 2) % 4, (p.x + 1) % 4, (p.x + 3) % 4
+        low, high = pl.ds(0, 64), pl.ds(64, 64)
+        snd[n, 0] = tmp[far, low].astype(bf16)
+        snd[n, 1] = tmp[nxt, high].astype(bf16)
+        self.to_next(n).start()
+        snd[n, 2] = tmp[far, high].astype(bf16)
+        snd[n, 3] = tmp[prev, low].astype(bf16)
+        self.to_prev(n).start()
+        snd[n, 4] = tmp[nxt, low].astype(bf16)
+        snd[n, 5] = tmp[prev, high].astype(bf16)
+        self.own[:, pl.ds(pl.multiple_of(n * 512, 512), 512)] = tmp[p.x]
+
+    def pass_on(self, n):
+        snd, rcv = self.snd, self.rcv
+        self.to_next(n).wait_recv()
+        snd[n, 4] = (snd[n, 4].astype(f32) + rcv[n, 0].astype(f32)).astype(bf16)
+        self.sum_next(n).start()
+        self.to_prev(n).wait_recv()
+        snd[n, 5] = (snd[n, 5].astype(f32) + rcv[n, 2].astype(f32)).astype(bf16)
+        self.sum_prev(n).start()
+
+    def run(self):
+        def body(i, _):
+            @pl.when(i < 4)
+            def _():
+                self.sibling_part(i)
+
+            @pl.when((i >= 1) & (i < 5))
+            def _():
+                self.own_part(i - 1)
+
+            @pl.when(i >= 2)
+            def _():
+                self.pass_on(i - 2)
+
+            return 0
+
+        lax.fori_loop(0, 6, body, 0)
+
+    def finish(self):
+        def body(n, _):
+            lanes = pl.ds(pl.multiple_of(n * 512, 512), 512)
+            low, high = pl.ds(0, 64), pl.ds(64, 64)
+            rcv, own = self.rcv, self.own
+            self.sum_next(n).wait_recv()
+            own[low, lanes] = own[low, lanes] + rcv[n, 3].astype(f32) + rcv[n, 4].astype(f32)
+            self.sum_prev(n).wait_recv()
+            own[high, lanes] = own[high, lanes] + rcv[n, 1].astype(f32) + rcv[n, 5].astype(f32)
+            return 0
+
+        lax.fori_loop(0, 4, body, 0)
+
+    def sent(self):
+        def body(n, _):
+            for copy in (self.crossing, self.to_next, self.to_prev, self.sum_next, self.sum_prev):
+                copy(n).wait_send()
+            return 0
+
+        lax.fori_loop(0, 4, body, 0)
+
+
+class GroupGather:
+    def __init__(self, links, place, whole):
+        self.links, self.place, self.whole = links, place, whole
+        self.low, self.high = pl.ds(0, 64), pl.ds(64, 64)
+
+    def send(self, ref, device):
+        return self.links.send(ref, ref, device)
+
+    def start(self):
+        p, w = self.place, self.whole
+        self.nxt, self.prev, self.far = (p.x + 1) % 4, (p.x + 3) % 4, (p.x + 2) % 4
+        self.to_next, self.to_prev = p.at(x=self.nxt), p.at(x=self.prev)
+        self.sibling = p.at(c=1 - p.c)
+        low, high = w.at[p.x, p.c, self.low], w.at[p.x, p.c, self.high]
+        self.first = [self.send(low, self.to_next), self.send(high, self.to_prev)]
+        self.second = [self.send(high, self.to_next), self.send(low, self.to_prev)]
+        self.paired = [self.send(w.at[p.x, p.c], self.sibling)]
+
+    def forward(self):
+        p, w = self.place, self.whole
+        self.first[0].wait_recv()
+        self.third = [self.send(w.at[self.prev, p.c, self.low], self.to_next)]
+        self.first[1].wait_recv()
+        self.third.append(self.send(w.at[self.nxt, p.c, self.high], self.to_prev))
+
+    def share(self):
+        p, w = self.place, self.whole
+        self.second[0].wait_recv()
+        self.paired.append(self.send(w.at[self.prev, p.c], self.sibling))
+        self.second[1].wait_recv()
+        self.paired.append(self.send(w.at[self.nxt, p.c], self.sibling))
+        for copy in self.third:
+            copy.wait_recv()
+        self.paired.append(self.send(w.at[self.far, p.c], self.sibling))
+
+    def done(self):
+        for copy in self.paired:
+            copy.wait_recv()
+
+
+class BlockGather:
+    def __init__(self, links, place, own, out):
+        p = place
+        self.links, self.place, self.out = links, place, out
+        self.sibling = p.at(c=1 - p.c)
+        mine = out.at[pl.ds(p.q * OWNED, OWNED)]
+        self.local = links.local(own, mine)
+        self.across = links.send(own, mine, p.at(x=p.xh * 2 + 1 - p.xl))
+        self.paired = [links.send(own, mine, self.sibling)]
+
+    def share(self):
+        p = self.place
+        self.across.wait_recv()
+        theirs = self.out.at[pl.ds(((1 - p.xl) * 2 + p.c) * OWNED, OWNED)]
+        self.paired.append(self.links.send(theirs, theirs, self.sibling))
+
+    def done(self):
+        for copy in self.paired:
+            copy.wait_recv()
+        self.local.wait()
+
+
+def norm_back(e, values):
+    r = lax.rsqrt(jnp.mean(values * values, axis=-1, keepdims=True) + epsilon)
+    return r * e - values * r**3 * jnp.mean(e * values, axis=-1, keepdims=True)
+
+
+def backward_kernel(
+    wq_in, wo_in, gu_in, d_in, xr_in, q_in, kv_in, mixed_in, resid_in, nm_in, cot_in, hid, bias_in,
+    result_o, grad_o, fin_gu, fin_d, fin_q, fin_o,
+    wq, wo, gu, d, nm, cot, act, gg, kv, bias, resid, hid_own, gres, own, low_own, res_own, gb,
+    acc, last_kv, tail_out, tail_in, in_gu, in_d, in_q, in_o, in2_gu, in2_d, in2_q, in2_o,
+    send_c, snd, tmp, recv_c1, rcv1,
+    send_sems, recv_sems, local_sems, group_send, group_recv, ready,
+):
+    p = Place()
+    links = Links(send_sems, recv_sems, local_sems)
+    sibling = p.at(c=1 - p.c)
+    load_nm = links.local(nm_in, nm)
+    load_gu = links.local(gu_in, gu)
+    load_cot = links.local(cot_in, cot)
+    load_d = links.local(d_in, d)
+    load_resid = links.local(resid_in, resid)
+    load_wo = links.local(wo_in, wo)
+    load_kv = links.local(kv_in, kv)
+    load_bias = links.local(bias_in, bias)
+    load_wq = links.local(wq_in, wq)
+    load_hid = links.local(hid.at[pl.ds(p.q * OWNED, OWNED)], hid_own)
+    greet(p)
+    for copy in (load_nm, load_gu, load_cot, load_d):
+        copy.wait()
+
+    def feed(t, _):
+        part = jnp.dot(nm[t].reshape(256, 2048), gu[...].reshape(2048, 1408), preferred_element_type=f32)
+        back = jnp.dot(cot[t].reshape(256, 2048), d[...].reshape(2048, 768), preferred_element_type=f32)
+        tail = part[:, 1280:]
+        flipped = pltpu.roll(tail, 64, 1)
+        lane = lax.broadcasted_iota(jnp.int32, (256, 128), 1)
+        for lanes, gate, up in (
+            (slice(0, 640), part[:, :640], part[:, 640:1280]),
+            (slice(640, 768), tail, flipped),
+        ):
+            sig = 1 / (1 + jnp.exp(-gate))
+            silu = gate * sig
+            grad_act = back[:, lanes]
+            act[t, :, :, lanes] = (silu * up).astype(bf16).reshape(2, OWNED, -1)
+            grad_gate = grad_act * up * sig * (1 + gate * (1 - sig))
+            grad_up = grad_act * silu
+            if lanes.start == 0:
+                gg[t, :, :, :640] = grad_gate.astype(bf16).reshape(2, OWNED, 640)
+                gg[t, :, :, 640:1280] = grad_up.astype(bf16).reshape(2, OWNED, 640)
+            else:
+                both = jnp.where(lane < 64, grad_gate, pltpu.roll(grad_up, 64, 1))
+                gg[t, :, :, 1280:] = both.astype(bf16).reshape(2, OWNED, 128)
+        return 0
+
+    lax.fori_loop(0, 4, feed, 0)
+
+    def partial_of(left, right, width):
+        def partial(n, core):
+            return lax.dot_general(
+                left[:, core].reshape(512, width),
+                right[n].reshape(512, width),
+                TURNED,
+                preferred_element_type=f32,
+            )
+
+        return partial
+
+    def sems(k):
+        span = pl.ds(20 * k, 20)
+        return group_send.at[span], group_recv.at[span]
+
+    r_mlp = GroupReduce(p, partial_of(gg, gu, 1408), (send_c, recv_c1, tmp, snd, rcv1, own), sems(0))
+    r_mlp.run()
+
+    def grads_into(out, left, right, width):
+        def body(n, _):
+            lanes = pl.ds(pl.multiple_of(n * 256, 256), 256)
+            part = lax.dot_general(
+                left[:, :, :, lanes].reshape(1024, 256),
+                right[...].reshape(1024, width),
+                LEFT_TURNED,
+                preferred_element_type=f32,
+            )
+            out[n // 2, n % 2] = part.astype(bf16).reshape(4, 64, width)
+            return 0
+
+        lax.fori_loop(0, 8, body, 0)
+
+    load_resid.wait()
+    r_mlp.finish()
+
+    def grad_rows(i, _):
+        r = pl.ds(i * 16, 16)
+        grad = cot[p.x, p.c, r].astype(f32) + norm_back(own[r], resid[r])
+        gres[r] = grad
+        gb[p.x, p.c, r] = grad.astype(bf16)
+        return 0
+
+    lax.fori_loop(0, OWNED // 16, grad_rows, 0)
+    g_branch = GroupGather(links, p, gb)
+    g_branch.start()
+    grads_into(gu, nm, gg, 1408)
+    load_xr = links.local(xr_in, nm)
+    load_q = links.local(q_in, gg.at[:, :, :, pl.ds(0, 256)])
+    load_mixed = links.local(mixed_in, gg.at[:, :, :, pl.ds(256, 256)])
+    w_gu = WeightReduce(links, p, gu, in_gu, in2_gu, fin_gu, 768)
+    w_gu.start0()
+    g_branch.forward()
+    r_mlp.sent()
+
+    r_out = GroupReduce(p, partial_of(act, d, 768), (send_c, recv_c1, tmp, snd, rcv1, own), sems(1))
+    g_branch.share()
+    g_branch.done()
+    r_out.run()
+    grads_into(d, cot, act, 768)
+    w_d = WeightReduce(links, p, d, in_d, in2_d, fin_d, 384)
+    w_d.start0()
+    r_out.finish()
+
+    def result_rows(i, _):
+        r = pl.ds(i * 16, 16)
+        res_own[r] = (resid[r] + own[r]).astype(bf16)
+        return 0
+
+    lax.fori_loop(0, OWNED // 16, result_rows, 0)
+    w_gu.start1()
+    for device in (sibling, p.at(x=(p.x + 1) % 4), p.at(x=(p.x + 3) % 4)):
+        pl.semaphore_signal(ready, inc=1, device_id=device, device_id_type=MESH)
+    b_out = BlockGather(links, p, res_own, result_o)
+
+    for copy in (load_wo, load_q, load_mixed, load_kv, load_bias):
+        copy.wait()
+
+    def grad_mixed(t, _):
+        out = jnp.dot(gb[t].reshape(256, 2048), wo[...].reshape(2048, 256), preferred_element_type=f32)
+        gg[t, :, :, 512:768] = out.astype(bf16).reshape(2, OWNED, 256)
+        return 0
+
+    lax.fori_loop(0, 4, grad_mixed, 0)
+
+    def attend_back(block, head):
+        lane = pl.multiple_of(head * 128, 128)
+        acc[...] = jnp.zeros_like(acc)
+
+        def chunk_body(chunk, _):
+            x, core = block * 2 + chunk // 2, chunk % 2
+            r = pl.multiple_of(chunk * 128, 128)
+            query = gg[x, core, :, pl.ds(lane, 128)]
+            grad = gg[x, core, :, pl.ds(lane + 512, 128)]
+            keys = kv[block, pl.ds(r, 192), pl.ds(lane, 128)]
+            values = kv[block, pl.ds(r, 192), pl.ds(lane + 256, 128)]
+            scores = lax.dot_general(query, keys, TURNED, preferred_element_type=f32) * SCALE
+            scores = scores + bias[block * 4 + chunk].astype(f32)
+            expo = jnp.exp(scores - jnp.max(scores, axis=-1, keepdims=True))
+            probs = expo / jnp.sum(expo, axis=-1, keepdims=True)
+            probs_low = probs.astype(bf16)
+            grad_probs = lax.dot_general(grad, values, TURNED, preferred_element_type=f32)
+            inner = jnp.sum(probs * grad_probs, axis=-1, keepdims=True)
+            grad_scores = (probs * (grad_probs - inner)).astype(bf16)
+            grad_query = jnp.dot(grad_scores, keys, preferred_element_type=f32) * SCALE
+            act[x, core, :, pl.ds(lane, 128)] = grad_query.astype(bf16)
+            rows = pl.ds(r, 192)
+            grad_keys = lax.dot_general(grad_scores, query, LEFT_TURNED, preferred_element_type=f32)
+            acc[0, rows] = acc[0, rows] + grad_keys * SCALE
+            acc[1, rows] = acc[1, rows] + lax.dot_general(
+                probs_low, grad, LEFT_TURNED, preferred_element_type=f32
+            )
+            return 0
+
+        lax.fori_loop(0, 4, chunk_body, 0)
+        for k in range(2):
+            lanes = pl.ds(pl.multiple_of(lane + 256 * k, 128), 128)
+            tail_out[block, :, lanes] = acc[k, pl.ds(0, WINDOW)].astype(bf16)
+            last_kv[block, :, lanes] = acc[k, pl.ds(BLOCK, WINDOW)]
+
+            def store(i, _):
+                x, core = block * 2 + i // 2, i % 2
+                out = pl.ds(pl.multiple_of(lane + 256 + 256 * k, 128), 128)
+                act[x, core, :, out] = acc[k, pl.ds(WINDOW + i * 128, 128)].astype(bf16)
+                return 0
+
+            lax.fori_loop(0, 4, store, 0)
+
+    def all_heads(i, _):
+        attend_back(i // 2, i % 2)
+        return 0
+
+    lax.fori_loop(0, 4, all_heads, 0)
+    first = jnp.where(p.z == 0, 1, 0)
+    tails = []
+    for block in range(2):
+        to_y = (p.y + 4 - first) % 4 if block == 0 else p.y
+        slot = first if block == 0 else 1 - first
+        tails.append(links.send(tail_out.at[block], tail_in.at[slot], p.at(y=to_y, z=(p.z + 3) % 4)))
+    w_gu.start2()
+    w_d.start1()
+    r_out.sent()
+    b_out.share()
+    for copy in tails:
+        copy.wait_recv()
+    for block in range(2):
+        whole = last_kv[block] + tail_in[block].astype(f32)
+        act[2 * block + 1, 1, pl.ds(64, 64), 256:] = whole.astype(bf16)
+
+    load_wq.wait()
+    r_attn = GroupReduce(p, partial_of(act, wq, 768), (send_c, recv_c1, tmp, snd, rcv1, own), sems(2))
+    pl.semaphore_wait(ready, 3)
+    r_attn.run()
+    load_xr.wait()
+    grads_into(wq, nm, act, 768)
+    w_q = WeightReduce(links, p, wq, in_q, in2_q, fin_q, 384)
+    w_q.start0()
+    w_gu.start3()
+    w_d.start2()
+    mixed_part = gg.at[:, :, :, pl.ds(256, 256)]
+    grads_into(wo, gb, mixed_part, 256)
+    w_o = WeightReduce(links, p, wo, in_o, in2_o, fin_o, 128)
+    w_o.start0()
+    load_hid.wait()
+    r_attn.finish()
+
+    def input_rows(i, _):
+        r = pl.ds(i * 16, 16)
+        low_own[r] = (gres[r] + norm_back(own[r], hid_own[r].astype(f32))).astype(bf16)
+        return 0
+
+    lax.fori_loop(0, OWNED // 16, input_rows, 0)
+    b_in = BlockGather(links, p, low_own, grad_o)
+    w_q.start1()
+    w_gu.start4()
+    w_d.start3()
+    w_o.start1()
+    w_q.start2()
+    w_o.start2()
+    w_d.start4()
+    w_q.start3()
+    w_o.start3()
+    b_in.share()
+    w_q.start4()
+    w_o.start4()
+    for item in (b_out, b_in, w_gu, w_d, w_q, w_o):
+        item.done()
+    r_attn.sent()
+    links.finish()
+
+
+def backward_call(wq, wo, gu, d, xr, q, kv, mixed, resid, nm, cot, hid, bias):
+    sds = jax.ShapeDtypeStruct
+    group = (4, 2, OWNED)
+    vm = pltpu.VMEM
+    return pl.pallas_call(
+        backward_kernel,
+        out_shape=(
+            sds((BLOCK, 2048), bf16),
+            sds((BLOCK, 2048), bf16),
+            sds((2, 64, 1408), bf16),
+            sds((2, 64, 768), bf16),
+            sds((2, 64, 768), bf16),
+            sds((2, 64, 256), bf16),
+        ),
+        in_specs=[ANY] * 13,
+        out_specs=[ANY] * 6,
+        scratch_shapes=[
+            vm((4, 2, 4, 64, 768), bf16),
+            vm((4, 2, 4, 64, 256), bf16),
+            vm((4, 2, 4, 64, 1408), bf16),
+            vm((4, 2, 4, 64, 768), bf16),
+            vm(group + (2048,), bf16),
+            vm(group + (2048,), bf16),
+            vm(group + (768,), bf16),
+            vm(group + (1408,), bf16),
+            vm((2, BLOCK + WINDOW, 512), bf16),
+            vm((8, 128, 192), bf16),
+            vm((OWNED, 2048), f32),
+            vm((OWNED, 2048), bf16),
+            vm((OWNED, 2048), f32),
+            vm((OWNED, 2048), f32),
+            vm((OWNED, 2048), bf16),
+            vm((OWNED, 2048), bf16),
+            vm(group + (2048,), bf16),
+            vm((2, BLOCK + WINDOW, 128), f32),
+            vm((2, WINDOW, 512), f32),
+            vm((2, WINDOW, 512), bf16),
+            vm((2, WINDOW, 512), bf16),
+            vm((6, 4, 64, 1408), bf16),
+            vm((6, 4, 64, 768), bf16),
+            vm((6, 4, 64, 768), bf16),
+            vm((6, 4, 64, 256), bf16),
+            vm((6, 64, 1408), bf16),
+            vm((6, 64, 768), bf16),
+            vm((6, 64, 768), bf16),
+            vm((6, 64, 256), bf16),
+            vm((4, 4, OWNED, 512), bf16),
+            vm((4, 6, 64, 512), bf16),
+            vm((4, OWNED, 512), f32),
+            vm((4, 4, OWNED, 512), bf16),
+            vm((4, 6, 64, 512), bf16),
+            pltpu.SemaphoreType.DMA((130,)),
+            pltpu.SemaphoreType.DMA((130,)),
+            pltpu.SemaphoreType.DMA((24,)),
+            pltpu.SemaphoreType.DMA((60,)),
+            pltpu.SemaphoreType.DMA((60,)),
+            pltpu.SemaphoreType.REGULAR,
+        ],
+        compiler_params=pltpu.CompilerParams(
+            collective_id=1, has_side_effects=True, vmem_limit_bytes=60 * 2**20
+        ),
+        name="backward",
+    )(wq, wo, gu, d, xr, q, kv, mixed, resid, nm, cot, hid, bias)
 
 
 def per_device(
@@ -655,7 +1072,7 @@
     lengths,
     cotangent,
 ):
-    xh, xl, c = lax.axis_index("xh"), lax.axis_index("xl"), lax.axis_index("c")
+    xh = lax.axis_index("xh")
     gain_attn = norm_gain_attn.astype(f32)[:, None]
     gain_mlp = norm_gain_mlp.astype(f32)[:, None]
     scaled = lambda w, g: (w.astype(f32) * g).astype(bf16)
@@ -664,98 +1081,29 @@
     )
     pk_gu, pk_d = pack_ff(scaled(w_gate, gain_mlp), scaled(w_up, gain_mlp), w_down.T)
     bias = attention_bias(lengths)
-    wq, wo, gu, d, xr, queries, kv_ext, mixed, resid, nm, cot = forward_call(
+    wq, wo, gu, d, xr, q, kv, mixed, resid, nm, cot = forward_call(
         pk_q, pk_o, pk_gu, pk_d, hidden_in, cotangent, bias
     )
-    qkv_w = wq.reshape(2048, 768)
-    out_w = wo.reshape(2048, 256)
-    gu = gu.reshape(2048, 1408)
-    gate_w = jnp.concatenate([gu[:, :640], gu[:, 1280:1328]], axis=1)
-    up_w = jnp.concatenate([gu[:, 640:1280], gu[:, 1344:1392]], axis=1)
-    down_w = d.reshape(2048, 768)[:, :688]
-    normed_attn = xr.reshape(1024, 2048)
-    mixed = mixed.reshape(1024, 256)
-    normed_mlp = nm.reshape(1024, 2048)
-    cot = cot.reshape(1024, 2048)
-
-    q = xl * 2 + c
-    owned_rows = lambda a: lax.dynamic_slice_in_dim(a, q * OWNED, OWNED, 0)
-    hidden_owned = owned_rows(hidden_in).astype(f32)
-    cot_owned = owned_rows(cotangent).astype(f32)
-    visible = visibility(lengths)
-    queries = queries.reshape(16, WINDOW, 2, HEAD_DIM)
-    key_blocks = band_blocks(kv_ext[..., :256]).reshape(16, 2 * WINDOW, 2, HEAD_DIM)
-    value_blocks = band_blocks(kv_ext[..., 256:]).reshape(16, 2 * WINDOW, 2, HEAD_DIM)
-    scores = score_blocks(queries, key_blocks, visible)
-    highest = jnp.max(scores, axis=-1, keepdims=True)
-    expo = jnp.exp(scores - highest)
-    probs = expo / jnp.sum(expo, axis=-1, keepdims=True)
-    probs_low = probs.astype(bf16)
-
-    gate = dot_plain(normed_mlp, gate_w)
-    up = dot_plain(normed_mlp, up_w)
-    sig = 1 / (1 + jnp.exp(-gate))
-    silu = gate * sig
-    activated = (silu * up).astype(bf16)
-    result = resid + reduce_group(dot_right_turned(activated, down_w))
-    result = gather_owned(result.astype(bf16))
-
-    grad_act = dot_plain(cot, down_w)
-    grad_gate_act = (grad_act * up * sig * (1 + gate * (1 - sig))).astype(bf16)
-    grad_up_act = (grad_act * silu).astype(bf16)
-    grad_normed_mlp = reduce_group(
-        dot_right_turned(grad_gate_act, gate_w) + dot_right_turned(grad_up_act, up_w)
+    group = (4, 2, OWNED)
+    result, input_grad, fin_gu, fin_d, fin_q, fin_o = backward_call(
+        wq, wo, gu, d,
+        xr.reshape(group + (2048,)),
+        q.reshape(group + (256,)),
+        kv,
+        mixed.reshape(group + (256,)),
+        resid,
+        nm,
+        cot.reshape(group + (2048,)),
+        hidden_in,
+        bias,
     )
-    grad_down = dot_left_turned(cot, activated).astype(bf16)
-    grad_gate = dot_left_turned(normed_mlp, grad_gate_act).astype(bf16)
-    grad_up = dot_left_turned(normed_mlp, grad_up_act).astype(bf16)
-    grad_ff = jnp.concatenate([grad_gate, grad_up, grad_down], axis=1)
-    grad_ff = reduce_weights(grad_ff[:, :1024], grad_ff[:, 1024:])
-
-    def norm_back(e, values):
-        r = lax.rsqrt(jnp.mean(values * values, axis=-1, keepdims=True) + epsilon)
-        return r * e - values * r**3 * jnp.mean(e * values, axis=-1, keepdims=True)
-
-    grad_resid = cot_owned + norm_back(grad_normed_mlp, resid)
-    grad_branch = gather_group(grad_resid.astype(bf16))
-    grad_out = dot_left_turned(grad_branch, mixed).astype(bf16)
-    grad_mixed = dot_plain(grad_branch, out_w).astype(bf16).reshape(16, WINDOW, 2, HEAD_DIM)
-    grad_probs = jnp.einsum("bqhd,bkhd->bhqk", grad_mixed, value_blocks, preferred_element_type=f32)
-    inner = jnp.sum(probs * grad_probs, axis=-1, keepdims=True)
-    grad_scores = (probs * (grad_probs - inner)).astype(bf16)
-    scale = HEAD_DIM ** (-0.5)
-    grad_queries = (
-        jnp.einsum("bhqk,bkhd->bqhd", grad_scores, key_blocks, preferred_element_type=f32) * scale
-    )
-    grad_keys = (
-        jnp.einsum("bhqk,bqhd->bkhd", grad_scores, queries, preferred_element_type=f32) * scale
-    )
-    grad_values = jnp.einsum("bhqk,bqhd->bkhd", probs_low, grad_mixed, preferred_element_type=f32)
-    grad_kv = jnp.concatenate([fold_blocks(grad_keys), fold_blocks(grad_values)], axis=-1)
-    returned = tails_back(grad_kv[:, :WINDOW].astype(bf16)).astype(f32)
-    grad_kv = jnp.concatenate(
-        [grad_kv[:, WINDOW:BLOCK], grad_kv[:, BLOCK:] + returned], axis=1
-    ).reshape(1024, 512)
-    grad_qkv_act = jnp.concatenate([grad_queries.reshape(1024, 256), grad_kv], axis=1).astype(bf16)
-    grad_normed_attn = reduce_group(dot_right_turned(grad_qkv_act, qkv_w))
-    grad_qkv = dot_left_turned(normed_attn, grad_qkv_act).astype(bf16)
-    input_grad = gather_owned((grad_resid + norm_back(grad_normed_attn, hidden_owned)).astype(bf16))
-
-    grad_attn = jnp.concatenate([grad_qkv, grad_out], axis=1)
-    grad_attn = reduce_weights(grad_attn[:, :512], grad_attn[:, 512:])
-
-    def unswap(pack):
-        mine = pick(pack, 0, xh)[0]
-        return mine, flip(pick(pack, 0, 1 - xh)[0], "xh")
-
-    mine_a, other_a = unswap(grad_attn)
-    mine_f, other_f = unswap(grad_ff)
-
-    def whole(mine, other, start, width):
-        return in_order(xh, mine[:, start : start + width], other[:, start : start + width], 1).astype(f32)
-
-    dq, dk, dv = (whole(mine_a, other_a, 256 * i, 256) for i in range(3))
-    dg, du = (whole(mine_f, other_f, 688 * i, 688) for i in range(2))
+
+    def joined(fin, *spans):
+        return jnp.concatenate([fin[k][:, s] for k in range(2) for s in spans], axis=1).astype(f32)
+
+    dq, dk, dv = (joined(fin_q, slice(256 * i, 256 * i + 256)) for i in range(3))
+    dg = joined(fin_gu, slice(0, 640), slice(1280, 1328))
+    du = joined(fin_gu, slice(640, 1280), slice(1344, 1392))
 
     def dots(pairs):
         return sum(jnp.sum(w.astype(f32) * g, axis=1) for w, g in pairs)
@@ -772,11 +1120,11 @@
         dq * gain_attn,
         dk * gain_attn,
         dv * gain_attn,
-        whole(mine_a, other_a, 768, 256).T,
+        joined(fin_o, slice(0, 256)).T,
         grads_gain[1],
         dg * gain_mlp,
         du * gain_mlp,
-        whole(mine_f, other_f, 1376, 688).T,
+        joined(fin_d, slice(0, 688)).T,
     )
 
 

time: 574 us -> 336 us (0.59); the launches traced: 568 us -> 335 us
  Pallas kernels: 129 us -> 298 us
  waiting for transfers between devices: 108 us -> 1.68 us
  starting transfers between devices: 109 us -> 4.15 us
  matrix products: 74.4 us -> 0 us
  local copies, waits for them, and re-layouts: 82 us -> 12.5 us
  other arithmetic: 63.2 us -> 17.7 us
    pallas_call x0 -> x1, Pallas kernels: none -> 169 us  [backward_call(): pl.pallas_call(backward_kernel, out_shape=(sds((BLOCK, 2048), bf16), sds(...]
    ppermute x62 -> x0, waiting for transfers between devices: 91.6 us -> none  [the longest x61 91.6 us: shift(): return lax.ppermute(value, axis, [(i, (i + steps) % 4) for i in range(4)])]
    dot_general x18 -> x0, matrix products: 74.4 us -> none  [the longest x4 28.8 us: dot_right_turned(): lax.dot_general(left, right, (((1,), (1,)), ((), ())), preferred_element_...]
    ppermute x62 -> x0, starting transfers between devices: 72.8 us -> none  [the longest x61 71.4 us: shift(): return lax.ppermute(value, axis, [(i, (i + steps) % 4) for i in range(4)])]
    ppermute x12 -> x2, starting transfers between devices: 35.8 us -> 4.15 us  [flip(): return lax.ppermute(value, axis, [(0, 1), (1, 0)])]
    slice x24 -> x6, local copies, waits for them, and re-layouts: 30.9 us -> 1.42 us  [joined(): fin[k][:, s]]
    ppermute x12 -> x2, waiting for transfers between devices: 16.2 us -> 1.68 us  [flip(): return lax.ppermute(value, axis, [(0, 1), (1, 0)])]
    convert_element_type x18 -> x1, other arithmetic: 14.2 us -> 1.27 us  [attention_bias(): return jnp.where(visible, 0.0, masked_score).astype(bf16)]
  transfers between devices with their start and end apart: 74 -> 2, of which waited for: 22 -> 2; matrix products, arithmetic and copies ran while one was open for 28% -> 0% of each run, Pallas kernels for 0% -> 0%
where the time goes in v3:
time: 336 us; the launch traced here: 335 us
  Pallas kernels  298 us (89%)
  other arithmetic  17.7 us (5%)
  local copies, waits for them, and re-layouts  12.5 us (4%)
  starting transfers between devices  4.15 us (1%)
    pallas_call x1, Pallas kernels, backward_call(): pl.pallas_call(backward_kernel, out_shape=(sds((BLOCK, 2048), bf16), sds(...  169 us
    pallas_call x1, Pallas kernels, forward_call(): pl.pallas_call(forward_kernel, out_shape=(sds((4, 2, 4, 64, 768), bf16),...  129 us
  transfers between devices with their start and end apart: 2, of which 2 were waited for; matrix products, arithmetic and copies ran while one was open for 0% of the time, Pallas kernels for 0%

profile of v3, /device:TPU:1, one launch (start us, length us, event | category | flops | bytes accessed | tf_op | source)
XLA Modules:
  0.0 335.5 jit_solution(9441152563852720293)
XLA Ops:
  0.9 0.8 reduce-window.4
  2.4 2.0 iota_add_fusion.1
  4.4 2.0 iota_add_fusion
  7.0 1.1 fusion.1
  9.0 0.8 slice_bitcast_fusion.7
  9.8 1.0 slice.234
  10.8 1.0 fusion.4
  12.6 0.7 pad_maximum_fusion.2.pk_d
  14.2 0.8 pad_maximum_fusion.pk_gu
  15.0 1.3 select_convert_fusion.bias_in
  16.3 129.3 %forward_attention.1 = (bf16[4,2,4,64,768]{4,3,2,1,0:T(8,128)(2,1)}, bf16[4,2,4,64,256]{4,3,2,1,0:T(8,128)(2,1)}, bf16[4,2,4,64,1408]{4,3,2,1,0:T(8,128)(2,1)}, ...) custom-call(bf16[2,64,768]{2,1,0:T(8,128)(2,1)} %pad_maximum_fusion., ...), custom_call_target="tpu_custom_call" | custom-call | tf_op jit(solution)/shard_map/forward_attention/pallas_call | solution.py:379
  145.6 169.1 %backward.1 = (bf16[512,2048]{1,0:T(8,128)(2,1)}, bf16[512,2048]{1,0:T(8,128)(2,1)}, bf16[2,64,1408]{2,1,0:T(8,128)(2,1)}, bf16[2,64,768]{2,1,0:T(8,128)(2,1)}, ...) custom-call(bf16[4,2,4,64,768]{4,3,2,1,0:T(8,128)(2,1)} %get-tuple-element.28.wq_in, ...), custom_call_target="tpu_custom_call" | custom-call | tf_op jit(solution)/shard_map/backward/pallas_call | solution.py:1000
  314.8 1.1 slice_bitcast_fusion
  316.8 1.0 slice_bitcast_fusion.5
  318.4 1.0 concatenate.41
  319.4 0.9 concatenate.40
  320.3 1.8 convert_multiply_fusion
  322.1 1.8 convert_multiply_fusion.6
  324.0 0.8 convert_bitcast_fusion
  324.8 1.5 collective-permute-done
  326.4 4.1 %collective-permute-start.1 = (f32[2,64]{1,0:T(2,128)S(1)}, f32[2,64]{1,0:T(2,128)S(1)}, u32[]{:S(2)}, u32[]{:S(2)}) collective-permute-start(f32[2,64]{1,0:T(2,128)S(1)} %fusion.19), channel_id=1, source_target_pairs={{0,1},{1,0},{2,3},{3,2},{4,5},{5,4},{6,7},{7,6},{8,9},{9,8},{10,11... | collective-permute-start | bytes 1544 | tf_op jit(solution)/shard_map/ppermute | solution.py:21
  331.8 1.3 copy.25
  333.1 1.0 copy-done
  334.1 1.3 copy.26
  (66 shorter events, 6.9 us)
Async XLA Ops:
  0.6 11.9 %copy-start.12 = (pred[768]{0:T(1024)(128)(4,1)S(1)}, pred[768]{0:T(1024)(128)(4,1)}, u32[]{:S(2)}) copy-start(pred[768]{0:T(1024)(128)(4,1)} %constant.11.clone.1) | copy-start | bytes 2308
  0.7 11.9 %copy-start.7 = (bf16[1376,64]{0,1:T(8,128)(2,1)S(1)}, bf16[1376,64]{0,1:T(8,128)(2,1)}, u32[]{:S(2)}) copy-start(bf16[1376,64]{0,1:T(8,128)(2,1)} %param.21) | copy-start | bytes 528388
  7.0 7.0 %copy-start.10 = (f32[64]{0:T(128)}, f32[64]{0:T(128)S(1)}, u32[]{:S(2)}) copy-start(f32[64]{0:T(128)S(1)} %convert_element_type.125) | copy-start | bytes 772
  9.0 2.8 copy-start.11
  314.8 5.5 %copy-start.2 = (bf16[64,1376]{1,0:T(8,128)(2,1)S(1)}, bf16[64,1376]{1,0:T(8,128)(2,1)}, u32[]{:S(2)}) copy-start(bf16[64,1376]{1,0:T(8,128)(2,1)} %param.20) | copy-start | bytes 528388
  314.8 5.5 %copy-start.3 = (bf16[64,1376]{1,0:T(8,128)(2,1)S(1)}, bf16[64,1376]{1,0:T(8,128)(2,1)}, u32[]{:S(2)}) copy-start(bf16[64,1376]{1,0:T(8,128)(2,1)} %param.19) | copy-start | bytes 528388
  314.8 7.3 %copy-start.4 = (bf16[64,512]{1,0:T(8,128)(2,1)S(1)}, bf16[64,512]{1,0:T(8,128)(2,1)}, u32[]{:S(2)}) copy-start(bf16[64,512]{1,0:T(8,128)(2,1)} %param.14) | copy-start | bytes 196612
  314.8 7.3 %copy-start.5 = (bf16[64,512]{1,0:T(8,128)(2,1)S(1)}, bf16[64,512]{1,0:T(8,128)(2,1)}, u32[]{:S(2)}) copy-start(bf16[64,512]{1,0:T(8,128)(2,1)} %param.15) | copy-start | bytes 196612
  314.8 7.3 %copy-start.6 = (bf16[64,512]{1,0:T(8,128)(2,1)S(1)}, bf16[64,512]{1,0:T(8,128)(2,1)}, u32[]{:S(2)}) copy-start(bf16[64,512]{1,0:T(8,128)(2,1)} %param.16) | copy-start | bytes 196612
  316.0 7.9 %copy-start.8 = (bf16[2,64,768]{2,1,0:T(8,128)(2,1)S(1)}, bf16[2,64,768]{2,1,0:T(8,128)(2,1)}, u32[]{:S(2)}) copy-start(bf16[2,64,768]{2,1,0:T(8,128)(2,1)} %get-tuple-element.44) | copy-start | bytes 589828
  318.4 13.4 %copy-start.1 = (bf16[512,2048]{1,0:T(8,128)(2,1)S(1)}, bf16[512,2048]{1,0:T(8,128)(2,1)}, u32[]{:S(2)}) copy-start(bf16[512,2048]{1,0:T(8,128)(2,1)} %get-tuple-element.133) | copy-start | bytes 6291460
  320.3 4.6 %copy-start.9 = (bf16[2,64,256]{2,1,0:T(8,128)(2,1)S(1)}, bf16[2,64,256]{2,1,0:T(8,128)(2,1)}, u32[]{:S(2)}) copy-start(bf16[2,64,256]{2,1,0:T(8,128)(2,1)} %get-tuple-element.43) | copy-start | bytes 196612
  323.9 2.5 collective-permute-start
  326.4 4.9 %collective-permute-start.1 = (f32[2,64]{1,0:T(2,128)S(1)}, f32[2,64]{1,0:T(2,128)S(1)}, u32[]{:S(2)}, u32[]{:S(2)}) collective-permute-start(f32[2,64]{1,0:T(2,128)S(1)} %fusion.19), channel_id=1, source_target_pairs={{0,1},{1,0},{2,3},{3,2},{4,5},{5,4},{6,7},{7,6},{8,9},{9,8},{10,11... | collective-permute-start | bytes 1544 | tf_op jit(solution)/shard_map/ppermute | solution.py:21
  331.8 2.3 copy-start

commit v4 on v3

--- a/solution.py
+++ b/solution.py
@@ -49,6 +49,11 @@
         self.count, self.local_count, self.started = 0, 0, []
 
     def send(self, src, dst, device):
+        copy = self.prepare(src, dst, device)
+        copy.start()
+        return copy
+
+    def prepare(self, src, dst, device):
         copy = pltpu.make_async_remote_copy(
             src_ref=src,
             dst_ref=dst,
@@ -58,7 +63,6 @@
             device_id_type=MESH,
         )
         self.count += 1
-        copy.start()
         self.started.append(copy)
         return copy
 
@@ -68,9 +72,12 @@
         copy.start()
         return copy
 
-    def finish(self):
+    def settle(self):
         for copy in self.started:
             copy.wait_send()
+        self.started = []
+
+    finish = settle
 
 
 class WeightGather:
@@ -180,279 +187,6 @@
 
 def unit_scale(values):
     return values * lax.rsqrt(jnp.mean(values * values, axis=-1, keepdims=True) + epsilon)
-
-
-def forward_kernel(
-    pk_q, pk_o, pk_gu, pk_d, hid, cot, bias_in,
-    wq_o, wo_o, gu_o, d_o, xr_o, q_o, kv_o, mixed_o, resid_o, nm_o, cot_o,
-    wq, wo, hidg, xr, q_v, kvx, mixed, bias, send_c, recv_c, own, send_x, recv_x, nm,
-    send_sems, recv_sems, local_sems,
-):
-    p = Place()
-    links = Links(send_sems, recv_sems, local_sems)
-    sibling = p.at(c=1 - p.c)
-    facing = p.at(x=3 - p.x)
-    greet(p)
-
-    g_q = WeightGather(links, p, pk_q, wq, 384)
-    own_hidden = links.local(hid, hidg.at[p.xh])
-    rows = [pl.ds(p.c * 256 + k * 128, 128) for k in range(2)]
-    hidden_sent = [links.send(hid.at[r], hidg.at[p.xh, r], facing) for r in rows]
-    g_o = WeightGather(links, p, pk_o, wo, 128)
-    bias_copy = links.local(bias_in, bias)
-    g_gu = WeightGather(links, p, pk_gu, gu_o, 768)
-    g_d = WeightGather(links, p, pk_d, d_o, 384)
-    own_cot = links.local(cot, cot_o.at[p.xh])
-    g_q.start0()
-    g_o.start0()
-
-    def norm_rows(block, start, count):
-        def body(i, _):
-            r = pl.ds(start + i * 32, 32)
-            xr[block, r] = unit_scale(hidg[block, r].astype(f32)).astype(bf16)
-            return 0
-
-        lax.fori_loop(0, count // 32, body, 0)
-
-    own_hidden.wait()
-    norm_rows(p.xh, 0, BLOCK)
-    g_q.start1()
-    g_o.start1()
-    g_q.start2()
-    g_o.start2()
-    g_gu.start0()
-    g_d.start0()
-
-    shared = []
-    for k in range(2):
-        hidden_sent[k].wait_recv()
-        part = hidg.at[1 - p.xh, rows[k]]
-        shared.append(links.send(part, part, sibling))
-    cot_sent = [links.send(cot.at[r], cot_o.at[p.xh, r], facing) for r in rows]
-    norm_rows(1 - p.xh, p.c * 256, 256)
-    for copy in shared:
-        copy.wait_recv()
-    norm_rows(1 - p.xh, (1 - p.c) * 256, 256)
-    xr_copy = links.local(xr, xr_o)
-
-    g_q.start3()
-    g_o.start3()
-    g_gu.start1()
-    g_d.start1()
-    g_q.done()
-
-    def project(i, _):
-        block, r = i // 2, (i % 2) * 256
-        w = wq[...].reshape(2048, 768)
-        out = jnp.dot(xr[block, pl.ds(r, 256)], w, preferred_element_type=f32).astype(bf16)
-        q_v[block, pl.ds(r, 256)] = out[:, :256]
-        kvx[block, pl.ds(r + WINDOW, 256)] = out[:, 256:]
-        return 0
-
-    lax.fori_loop(0, 4, project, 0)
-
-    tails = []
-    last = jnp.where(p.z == 3, 1, 0)
-    for block in range(2):
-        to_y = p.y if block == 0 else (p.y + last) % 4
-        slot = last if block == 0 else 1 - last
-        tails.append(
-            links.send(
-                kvx.at[block, pl.ds(BLOCK, WINDOW)],
-                kvx.at[slot, pl.ds(0, WINDOW)],
-                p.at(y=to_y, z=(p.z + 1) % 4),
-            )
-        )
-    g_gu.start2()
-    wq_copy = links.local(wq, wq_o)
-    q_copy = links.local(q_v, q_o)
-    bias_copy.wait()
-
-    def attend(block, chunk, head):
-        r, lane = pl.multiple_of(chunk * 128, 128), pl.multiple_of(head * 128, 128)
-        query = q_v[block, pl.ds(r, 128), pl.ds(lane, 128)]
-        keys = kvx[block, pl.ds(r, 192), pl.ds(lane, 128)]
-        values = kvx[block, pl.ds(r, 192), pl.ds(lane + 256, 128)]
-        scores = lax.dot_general(query, keys, TURNED, preferred_element_type=f32) * SCALE
-        scores = scores + bias[block * 4 + chunk].astype(f32)
-        expo = jnp.exp(scores - jnp.max(scores, axis=-1, keepdims=True))
-        probs = (expo / jnp.sum(expo, axis=-1, keepdims=True)).astype(bf16)
-        out = jnp.dot(probs, values, preferred_element_type=f32)
-        mixed[block, pl.ds(r, 128), pl.ds(lane, 128)] = out.astype(bf16)
-
-    def inner(i, _):
-        attend(i // 6, (i % 6) // 2 + 1, i % 2)
-        return 0
-
-    lax.fori_loop(0, 12, inner, 0)
-    for copy in tails:
-        copy.wait_recv()
-
-    def first(i, _):
-        attend(i // 2, 0, i % 2)
-        return 0
-
-    lax.fori_loop(0, 4, first, 0)
-    kv_copy = links.local(kvx, kv_o)
-    mixed_copy = links.local(mixed, mixed_o)
-    g_o.done()
-
-    def branch_all():
-        def sib(n, _):
-            lanes = pl.ds(pl.multiple_of(n * 256, 256), 256)
-            w = wo[n // 2, n % 2].reshape(256, 256)
-            for x in range(4):
-                left = mixed[x // 2, pl.ds((x % 2) * 256 + (1 - p.c) * OWNED, OWNED)]
-                part = lax.dot_general(left, w, TURNED, preferred_element_type=f32)
-                send_c[x, :, lanes] = part.astype(bf16)
-            return 0
-
-        lax.fori_loop(0, 8, sib, 0)
-        crossed = links.send(send_c, recv_c, sibling)
-
-        def mine(n, _):
-            lanes = pl.ds(pl.multiple_of(n * 256, 256), 256)
-            w = wo[n // 2, n % 2].reshape(256, 256)
-            for x in range(4):
-                left = mixed[x // 2, pl.ds((x % 2) * 256 + p.c * OWNED, OWNED)]
-                own[x, :, lanes] = lax.dot_general(left, w, TURNED, preferred_element_type=f32)
-            return 0
-
-        lax.fori_loop(0, 8, mine, 0)
-        return crossed
-
-    crossed = branch_all()
-    crossed.wait_recv()
-    arrived = []
-    for k in (2, 1, 3):
-        to = (p.x + k) % 4
-
-        def add(i, _):
-            r = pl.ds(i * 16, 16)
-            send_x[k - 1, r] = (own[to, r] + recv_c[to, r].astype(f32)).astype(bf16)
-            return 0
-
-        lax.fori_loop(0, OWNED // 16, add, 0)
-        arrived.append(links.send(send_x.at[k - 1], recv_x.at[k - 1], p.at(x=to)))
-    g_d.start2()
-    g_gu.start3()
-    for copy in arrived:
-        copy.wait_recv()
-
-    def finish(i, _):
-        r = pl.ds(i * 16, 16)
-        total = hidg[p.xh, pl.ds(p.q * OWNED + i * 16, 16)].astype(f32)
-        total = total + own[p.x, r] + recv_c[p.x, r].astype(f32)
-        for k in range(3):
-            total = total + recv_x[k, r].astype(f32)
-        own[p.x, r] = total
-        nm[r] = unit_scale(total).astype(bf16)
-        return 0
-
-    lax.fori_loop(0, OWNED // 16, finish, 0)
-    resid_copy = links.local(own.at[p.x], resid_o)
-    spread = [links.send(nm, nm_o.at[p.x, p.c], p.at(x=(p.x + k) % 4)) for k in (2, 1, 3)]
-    nm_copy = links.local(nm, nm_o.at[p.x, p.c])
-    paired = [links.send(nm, nm_o.at[p.x, p.c], sibling)]
-    wo_copy = links.local(wo, wo_o)
-    cot_shared = []
-    for k in range(2):
-        cot_sent[k].wait_recv()
-        part = cot_o.at[1 - p.xh, rows[k]]
-        cot_shared.append(links.send(part, part, sibling))
-    for i, k in ((1, 1), (2, 3), (0, 2)):
-        spread[i].wait_recv()
-        part = nm_o.at[(p.x + 4 - k) % 4, p.c]
-        paired.append(links.send(part, part, sibling))
-    g_d.start3()
-    for copy in paired + cot_shared:
-        copy.wait_recv()
-    g_gu.done()
-    g_d.done()
-    for copy in (own_cot, xr_copy, wq_copy, q_copy, kv_copy, mixed_copy, resid_copy, nm_copy, wo_copy):
-        copy.wait()
-    links.finish()
-
-
-def forward_call(pk_q, pk_o, pk_gu, pk_d, hid, cot, bias):
-    sds = jax.ShapeDtypeStruct
-    return pl.pallas_call(
-        forward_kernel,
-        out_shape=(
-            sds((4, 2, 4, 64, 768), bf16),
-            sds((4, 2, 4, 64, 256), bf16),
-            sds((4, 2, 4, 64, 1408), bf16),
-            sds((4, 2, 4, 64, 768), bf16),
-            sds((2, BLOCK, 2048), bf16),
-            sds((2, BLOCK, 256), bf16),
-            sds((2, BLOCK + WINDOW, 512), bf16),
-            sds((2, BLOCK, 256), bf16),
-            sds((OWNED, 2048), f32),
-            sds((4, 2, OWNED, 2048), bf16),
-            sds((2, BLOCK, 2048), bf16),
-        ),
-        in_specs=[ANY] * 7,
-        out_specs=[ANY] * 11,
-        scratch_shapes=[
-            pltpu.VMEM((4, 2, 4, 64, 768), bf16),
-            pltpu.VMEM((4, 2, 4, 64, 256), bf16),
-            pltpu.VMEM((2, BLOCK, 2048), bf16),
-            pltpu.VMEM((2, BLOCK, 2048), bf16),
-            pltpu.VMEM((2, BLOCK, 256), bf16),
-            pltpu.VMEM((2, BLOCK + WINDOW, 512), bf16),
-            pltpu.VMEM((2, BLOCK, 256), bf16),
-            pltpu.VMEM((8, 128, 192), bf16),
-            pltpu.VMEM((4, OWNED, 2048), bf16),
-            pltpu.VMEM((4, OWNED, 2048), bf16),
-            pltpu.VMEM((4, OWNED, 2048), f32),
-            pltpu.VMEM((3, OWNED, 2048), bf16),
-            pltpu.VMEM((3, OWNED, 2048), bf16),
-            pltpu.VMEM((OWNED, 2048), bf16),
-            pltpu.SemaphoreType.DMA((100,)),
-            pltpu.SemaphoreType.DMA((100,)),
-            pltpu.SemaphoreType.DMA((20,)),
-        ],
-        compiler_params=pltpu.CompilerParams(
-            collective_id=0, has_side_effects=True, vmem_limit_bytes=56 * 2**20
-        ),
-        name="forward_attention",
-    )(pk_q, pk_o, pk_gu, pk_d, hid, cot, bias)
-
-
-def attention_bias(lengths):
-    y, z = lax.axis_index("y"), lax.axis_index("z")
-    starts = (y * 8 + z + 4 * jnp.arange(2, dtype=jnp.int32)) * BLOCK
-    starts = (starts[:, None] + 128 * jnp.arange(4, dtype=jnp.int32)).reshape(8, 1, 1)
-    query = starts + jnp.arange(128, dtype=jnp.int32)[None, :, None]
-    key = starts - WINDOW + jnp.arange(192, dtype=jnp.int32)[None, None, :]
-    ends = jnp.cumsum(lengths)
-    segment = lambda t: sum((t >= ends[k]).astype(jnp.int32) for k in range(3))
-    visible = (key <= query) & (key > query - WINDOW) & (key >= 0) & (segment(key) == segment(query))
-    return jnp.where(visible, 0.0, masked_score).astype(bf16)
-
-
-def pack_ff(gate, up, down):
-    def tail(w):
-        return jnp.pad(w[:, 640:], ((0, 0), (0, 16)))
-
-    def one(k):
-        g, u, d = (w[:, k * 688 : (k + 1) * 688] for w in (gate, up, down))
-        return (
-            jnp.concatenate([g[:, :640], u[:, :640], tail(g), tail(u)], axis=1),
-            jnp.pad(d, ((0, 0), (0, 80))),
-        )
-
-    (gu0, d0), (gu1, d1) = one(0), one(1)
-    return jnp.stack([gu0, gu1]), jnp.stack([d0, d1])
-
-
-def pack_attn(query, key, value, out):
-    def one(k):
-        part = slice(k * 256, (k + 1) * 256)
-        return jnp.concatenate([query[:, part], key[:, part], value[:, part]], axis=1), out[:, part]
-
-    (q0, o0), (q1, o1) = one(0), one(1)
-    return jnp.stack([q0, q1]), jnp.stack([o0, o1])
 
 
 class WeightReduce:
@@ -619,7 +353,7 @@
         self.send_c[n] = part.astype(bf16).reshape(4, OWNED, 512)
         self.crossing(n).start()
 
-    def own_part(self, n):
+    def own_part(self, n, launch):
         p, tmp, snd = self.place, self.tmp, self.snd
         part = self.partial(n, p.c).reshape(4, OWNED, 512)
         self.crossing(n).wait_recv()
@@ -628,10 +362,12 @@
         low, high = pl.ds(0, 64), pl.ds(64, 64)
         snd[n, 0] = tmp[far, low].astype(bf16)
         snd[n, 1] = tmp[nxt, high].astype(bf16)
-        self.to_next(n).start()
+        if launch:
+            self.to_next(n).start()
         snd[n, 2] = tmp[far, high].astype(bf16)
         snd[n, 3] = tmp[prev, low].astype(bf16)
-        self.to_prev(n).start()
+        if launch:
+            self.to_prev(n).start()
         snd[n, 4] = tmp[nxt, low].astype(bf16)
         snd[n, 5] = tmp[prev, high].astype(bf16)
         self.own[:, pl.ds(pl.multiple_of(n * 512, 512), 512)] = tmp[p.x]
@@ -645,7 +381,7 @@
         snd[n, 5] = (snd[n, 5].astype(f32) + rcv[n, 2].astype(f32)).astype(bf16)
         self.sum_prev(n).start()
 
-    def run(self):
+    def run(self, launch=True):
         def body(i, _):
             @pl.when(i < 4)
             def _():
@@ -653,15 +389,32 @@
 
             @pl.when((i >= 1) & (i < 5))
             def _():
-                self.own_part(i - 1)
-
-            @pl.when(i >= 2)
-            def _():
-                self.pass_on(i - 2)
+                self.own_part(i - 1, launch)
+
+            if launch:
+
+                @pl.when(i >= 2)
+                def _():
+                    self.pass_on(i - 2)
 
             return 0
 
-        lax.fori_loop(0, 6, body, 0)
+        lax.fori_loop(0, 6 if launch else 5, body, 0)
+
+    def launch(self):
+        def body(n, _):
+            self.to_next(n).start()
+            self.to_prev(n).start()
+            return 0
+
+        lax.fori_loop(0, 4, body, 0)
+
+    def pass_all(self):
+        def body(n, _):
+            self.pass_on(n)
+            return 0
+
+        lax.fori_loop(0, 4, body, 0)
 
     def finish(self):
         def body(n, _):
@@ -701,28 +454,34 @@
         low, high = w.at[p.x, p.c, self.low], w.at[p.x, p.c, self.high]
         self.first = [self.send(low, self.to_next), self.send(high, self.to_prev)]
         self.second = [self.send(high, self.to_next), self.send(low, self.to_prev)]
-        self.paired = [self.send(w.at[p.x, p.c], self.sibling)]
+        tiles = (p.x, self.prev, self.nxt, self.far)
+        self.paired = [self.later(w.at[x, p.c], self.sibling) for x in tiles]
+        self.paired[0].start()
+        self.third = [
+            self.later(w.at[self.prev, p.c, self.low], self.to_next),
+            self.later(w.at[self.nxt, p.c, self.high], self.to_prev),
+        ]
+
+    def later(self, ref, device):
+        return self.links.prepare(ref, ref, device)
 
     def forward(self):
-        p, w = self.place, self.whole
-        self.first[0].wait_recv()
-        self.third = [self.send(w.at[self.prev, p.c, self.low], self.to_next)]
-        self.first[1].wait_recv()
-        self.third.append(self.send(w.at[self.nxt, p.c, self.high], self.to_prev))
-
-    def share(self):
-        p, w = self.place, self.whole
-        self.second[0].wait_recv()
-        self.paired.append(self.send(w.at[self.prev, p.c], self.sibling))
-        self.second[1].wait_recv()
-        self.paired.append(self.send(w.at[self.nxt, p.c], self.sibling))
+        for k in range(2):
+            self.first[k].wait_recv()
+            self.third[k].start()
+
+    def share_near(self):
+        for k in range(2):
+            self.second[k].wait_recv()
+            self.paired[1 + k].start()
+
+    def share_far(self):
         for copy in self.third:
             copy.wait_recv()
-        self.paired.append(self.send(w.at[self.far, p.c], self.sibling))
-
-    def done(self):
-        for copy in self.paired:
-            copy.wait_recv()
+        self.paired[3].start()
+
+    def ready(self, k):
+        self.paired[k].wait_recv()
 
 
 class BlockGather:
@@ -752,32 +511,205 @@
     return r * e - values * r**3 * jnp.mean(e * values, axis=-1, keepdims=True)
 
 
-def backward_kernel(
-    wq_in, wo_in, gu_in, d_in, xr_in, q_in, kv_in, mixed_in, resid_in, nm_in, cot_in, hid, bias_in,
-    result_o, grad_o, fin_gu, fin_d, fin_q, fin_o,
-    wq, wo, gu, d, nm, cot, act, gg, kv, bias, resid, hid_own, gres, own, low_own, res_own, gb,
+def block_kernel(
+    lengths, pk_q, pk_o, pk_gu, pk_d, hid, cot_in,
+    result_o, grad_o, fin_gu, fin_d, fin_q, fin_o, xr_o, qm_o,
+    wq, wo, gu, d, nm, cot, act, gg, kv, resid, hid_own, gres, own, low_own, res_own, gb,
     acc, last_kv, tail_out, tail_in, in_gu, in_d, in_q, in_o, in2_gu, in2_d, in2_q, in2_o,
-    send_c, snd, tmp, recv_c1, rcv1,
+    send_c, snd, tmp, recv_c, rcv,
     send_sems, recv_sems, local_sems, group_send, group_recv, ready,
 ):
     p = Place()
     links = Links(send_sems, recv_sems, local_sems)
     sibling = p.at(c=1 - p.c)
-    load_nm = links.local(nm_in, nm)
-    load_gu = links.local(gu_in, gu)
-    load_cot = links.local(cot_in, cot)
-    load_d = links.local(d_in, d)
-    load_resid = links.local(resid_in, resid)
-    load_wo = links.local(wo_in, wo)
-    load_kv = links.local(kv_in, kv)
-    load_bias = links.local(bias_in, bias)
-    load_wq = links.local(wq_in, wq)
-    load_hid = links.local(hid.at[pl.ds(p.q * OWNED, OWNED)], hid_own)
+    facing = p.at(x=3 - p.x)
+    hidg, xr = gb, nm
+
+    own_pair = pl.ds(2 * p.xh, 2)
+    own_hidden = links.local(hid, hidg.at[own_pair])
+    load_hid = links.local(hid.at[p.xl, p.c], hid_own)
+    own_cot = links.local(cot_in, cot.at[own_pair])
     greet(p)
-    for copy in (load_nm, load_gu, load_cot, load_d):
-        copy.wait()
-
-    def feed(t, _):
+
+    def cross(ref, whole):
+        return [links.send(ref.at[p.c, k], whole.at[2 * p.xh + p.c, k], facing) for k in range(2)]
+
+    def handed(whole, copies):
+        shared = []
+        for k in range(2):
+            copies[k].wait_recv()
+            part = whole.at[2 * (1 - p.xh) + p.c, k]
+            shared.append(links.send(part, part, sibling))
+        return shared
+
+    g_q = WeightGather(links, p, pk_q, wq, 384)
+    hidden_sent = cross(hid, hidg)
+    g_o = WeightGather(links, p, pk_o, wo, 128)
+    g_gu = WeightGather(links, p, pk_gu, gu, 768)
+    g_d = WeightGather(links, p, pk_d, d, 384)
+    g_q.start0()
+    g_o.start0()
+
+    def norm_rows(tile):
+        def body(i, _):
+            core, r = i // 4, pl.ds((i % 4) * 32, 32)
+            xr[tile, core, r] = unit_scale(hidg[tile, core, r].astype(f32)).astype(bf16)
+            return 0
+
+        lax.fori_loop(0, 8, body, 0)
+
+    own_hidden.wait()
+    norm_rows(2 * p.xh)
+    norm_rows(2 * p.xh + 1)
+    g_q.start1()
+    g_o.start1()
+    g_q.start2()
+    g_o.start2()
+    g_gu.start0()
+    g_d.start0()
+    shared = handed(hidg, hidden_sent)
+    cot_sent = cross(cot_in, cot)
+    norm_rows(2 * (1 - p.xh) + p.c)
+    for copy in shared:
+        copy.wait_recv()
+    norm_rows(2 * (1 - p.xh) + 1 - p.c)
+    xr_spill = links.local(xr, xr_o)
+    g_q.start3()
+    g_o.start3()
+    g_gu.start1()
+    g_d.start1()
+    g_q.done()
+
+    def project(t, _):
+        w = wq[...].reshape(2048, 768)
+        out = jnp.dot(xr[t].reshape(256, 2048), w, preferred_element_type=f32).astype(bf16)
+        gg[t, :, :, 0:256] = out[:, :256].reshape(2, OWNED, 256)
+        kv[t // 2, pl.ds((t % 2) * 256 + WINDOW, 256)] = out[:, 256:]
+        return 0
+
+    lax.fori_loop(0, 4, project, 0)
+
+    tails = []
+    last = jnp.where(p.z == 3, 1, 0)
+    for block in range(2):
+        to_y = p.y if block == 0 else (p.y + last) % 4
+        slot = last if block == 0 else 1 - last
+        tails.append(
+            links.send(
+                kv.at[block, pl.ds(BLOCK, WINDOW)],
+                kv.at[slot, pl.ds(0, WINDOW)],
+                p.at(y=to_y, z=(p.z + 1) % 4),
+            )
+        )
+    g_gu.start2()
+
+    end0 = lengths[0]
+    end1 = end0 + lengths[1]
+
+    def masked(scores, block, chunk):
+        start = (p.y * 8 + block * 4 + p.z) * BLOCK + chunk * 128
+        query = start + lax.broadcasted_iota(jnp.int32, (128, 192), 0)
+        key = start - WINDOW + lax.broadcasted_iota(jnp.int32, (128, 192), 1)
+        seen = (key <= query) & (key > query - WINDOW) & (key >= 0)
+        for end in (end0, end1):
+            seen = seen & ((key >= end) | (query < end))
+        return jnp.where(seen, scores, masked_score)
+
+    def probabilities(query, keys, block, chunk):
+        scores = lax.dot_general(query, keys, TURNED, preferred_element_type=f32) * SCALE
+        scores = masked(scores, block, chunk)
+        expo = jnp.exp(scores - jnp.max(scores, axis=-1, keepdims=True))
+        return expo / jnp.sum(expo, axis=-1, keepdims=True)
+
+    def attend(block, chunk, head):
+        x, core = block * 2 + chunk // 2, chunk % 2
+        r, lane = pl.multiple_of(chunk * 128, 128), pl.multiple_of(head * 128, 128)
+        query = gg[x, core, :, pl.ds(lane, 128)]
+        keys = kv[block, pl.ds(r, 192), pl.ds(lane, 128)]
+        values = kv[block, pl.ds(r, 192), pl.ds(lane + 256, 128)]
+        probs = probabilities(query, keys, block, chunk).astype(bf16)
+        out = jnp.dot(probs, values, preferred_element_type=f32)
+        gg[x, core, :, pl.ds(lane + 256, 128)] = out.astype(bf16)
+
+    def inner(i, _):
+        attend(i // 6, (i % 6) // 2 + 1, i % 2)
+        return 0
+
+    lax.fori_loop(0, 12, inner, 0)
+    for copy in tails:
+        copy.wait_recv()
+
+    def first_chunk(i, _):
+        attend(i // 2, 0, i % 2)
+        return 0
+
+    lax.fori_loop(0, 4, first_chunk, 0)
+    mixed = gg.at[:, :, :, pl.ds(256, 256)]
+    g_o.done()
+    xr_spill.wait()
+
+    def partial_of(left, right, width, start=0):
+        def partial(n, core):
+            return lax.dot_general(
+                left[:, core, :, start : start + width].reshape(512, width),
+                right[n].reshape(512, width),
+                TURNED,
+                preferred_element_type=f32,
+            )
+
+        return partial
+
+    def group_reduce(k, partial):
+        span = pl.ds(20 * k, 20)
+        return GroupReduce(
+            p, partial, (send_c, recv_c, tmp, snd, rcv, own), (group_send.at[span], group_recv.at[span])
+        )
+
+    r_branch = group_reduce(0, partial_of(gg, wo, 256, 256))
+    r_branch.run()
+    cot_shared = handed(cot, cot_sent)
+    g_d.start2()
+    g_gu.start3()
+    load_hid.wait()
+    r_branch.finish()
+
+    def resid_rows(i, _):
+        r = pl.ds(i * 16, 16)
+        total = hid_own[r].astype(f32) + own[r]
+        resid[r] = total
+        nm[p.x, p.c, r] = unit_scale(total).astype(bf16)
+        return 0
+
+    lax.fori_loop(0, OWNED // 16, resid_rows, 0)
+    g_nm = GroupGather(links, p, nm)
+    g_nm.start()
+    q_spill = links.local(gg.at[:, :, :, pl.ds(0, 512)], qm_o)
+    g_gu.done()
+    g_d.start3()
+    own_cot.wait()
+    for copy in cot_shared:
+        copy.wait_recv()
+    q_spill.wait()
+    g_nm.forward()
+    g_d.done()
+    g_nm.ready(0)
+
+    def feed(k, _):
+        @pl.when(k == 1)
+        def _():
+            g_nm.share_near()
+            g_nm.ready(1)
+
+        @pl.when(k == 2)
+        def _():
+            g_nm.ready(2)
+
+        @pl.when(k == 3)
+        def _():
+            g_nm.share_far()
+            g_nm.ready(3)
+
+        t = (p.x + jnp.where(k == 0, 0, jnp.where(k == 1, 3, k - 1))) % 4
         part = jnp.dot(nm[t].reshape(256, 2048), gu[...].reshape(2048, 1408), preferred_element_type=f32)
         back = jnp.dot(cot[t].reshape(256, 2048), d[...].reshape(2048, 768), preferred_element_type=f32)
         tail = part[:, 1280:]
@@ -803,22 +735,9 @@
 
     lax.fori_loop(0, 4, feed, 0)
 
-    def partial_of(left, right, width):
-        def partial(n, core):
-            return lax.dot_general(
-                left[:, core].reshape(512, width),
-                right[n].reshape(512, width),
-                TURNED,
-                preferred_element_type=f32,
-            )
-
-        return partial
-
-    def sems(k):
-        span = pl.ds(20 * k, 20)
-        return group_send.at[span], group_recv.at[span]
-
-    r_mlp = GroupReduce(p, partial_of(gg, gu, 1408), (send_c, recv_c1, tmp, snd, rcv1, own), sems(0))
+    r_branch.sent()
+    links.settle()
+    r_mlp = group_reduce(1, partial_of(gg, gu, 1408))
     r_mlp.run()
 
     def grads_into(out, left, right, width):
@@ -835,7 +754,11 @@
 
         lax.fori_loop(0, 8, body, 0)
 
-    load_resid.wait()
+    grads_into(gu, nm, gg, 1408)
+    w_gu = WeightReduce(links, p, gu, in_gu, in2_gu, fin_gu, 768)
+    w_gu.start0()
+    load_xr = links.local(xr_o, nm)
+    load_qm = links.local(qm_o, gg.at[:, :, :, pl.ds(0, 512)])
     r_mlp.finish()
 
     def grad_rows(i, _):
@@ -848,44 +771,21 @@
     lax.fori_loop(0, OWNED // 16, grad_rows, 0)
     g_branch = GroupGather(links, p, gb)
     g_branch.start()
-    grads_into(gu, nm, gg, 1408)
-    load_xr = links.local(xr_in, nm)
-    load_q = links.local(q_in, gg.at[:, :, :, pl.ds(0, 256)])
-    load_mixed = links.local(mixed_in, gg.at[:, :, :, pl.ds(256, 256)])
-    w_gu = WeightReduce(links, p, gu, in_gu, in2_gu, fin_gu, 768)
-    w_gu.start0()
+    r_mlp.sent()
+    g_branch.ready(0)
+
+    r_out = group_reduce(2, partial_of(act, d, 768))
+    r_out.run(launch=False)
     g_branch.forward()
-    r_mlp.sent()
-
-    r_out = GroupReduce(p, partial_of(act, d, 768), (send_c, recv_c1, tmp, snd, rcv1, own), sems(1))
-    g_branch.share()
-    g_branch.done()
-    r_out.run()
     grads_into(d, cot, act, 768)
     w_d = WeightReduce(links, p, d, in_d, in2_d, fin_d, 384)
+    w_gu.start1()
     w_d.start0()
-    r_out.finish()
-
-    def result_rows(i, _):
-        r = pl.ds(i * 16, 16)
-        res_own[r] = (resid[r] + own[r]).astype(bf16)
-        return 0
-
-    lax.fori_loop(0, OWNED // 16, result_rows, 0)
-    w_gu.start1()
-    for device in (sibling, p.at(x=(p.x + 1) % 4), p.at(x=(p.x + 3) % 4)):
-        pl.semaphore_signal(ready, inc=1, device_id=device, device_id_type=MESH)
-    b_out = BlockGather(links, p, res_own, result_o)
-
-    for copy in (load_wo, load_q, load_mixed, load_kv, load_bias):
-        copy.wait()
-
-    def grad_mixed(t, _):
+    g_branch.share_near()
+
+    def grad_mixed(t):
         out = jnp.dot(gb[t].reshape(256, 2048), wo[...].reshape(2048, 256), preferred_element_type=f32)
         gg[t, :, :, 512:768] = out.astype(bf16).reshape(2, OWNED, 256)
-        return 0
-
-    lax.fori_loop(0, 4, grad_mixed, 0)
 
     def attend_back(block, head):
         lane = pl.multiple_of(head * 128, 128)
@@ -898,10 +798,7 @@
             grad = gg[x, core, :, pl.ds(lane + 512, 128)]
             keys = kv[block, pl.ds(r, 192), pl.ds(lane, 128)]
             values = kv[block, pl.ds(r, 192), pl.ds(lane + 256, 128)]
-            scores = lax.dot_general(query, keys, TURNED, preferred_element_type=f32) * SCALE
-            scores = scores + bias[block * 4 + chunk].astype(f32)
-            expo = jnp.exp(scores - jnp.max(scores, axis=-1, keepdims=True))
-            probs = expo / jnp.sum(expo, axis=-1, keepdims=True)
+            probs = probabilities(query, keys, block, chunk)
             probs_low = probs.astype(bf16)
             grad_probs = lax.dot_general(grad, values, TURNED, preferred_element_type=f32)
             inner = jnp.sum(probs * grad_probs, axis=-1, keepdims=True)
@@ -930,42 +827,67 @@
 
             lax.fori_loop(0, 4, store, 0)
 
-    def all_heads(i, _):
-        attend_back(i // 2, i % 2)
+    load_qm.wait()
+    g_branch.ready(1)
+    g_branch.ready(2)
+
+    def half_block(i, _):
+        @pl.when(i == 2)
+        def _():
+            g_branch.share_far()
+            r_out.launch()
+            g_branch.ready(3)
+
+        block = jnp.where(i < 2, p.xh, 1 - p.xh)
+
+        @pl.when(i % 2 == 0)
+        def _():
+            grad_mixed(2 * block)
+            grad_mixed(2 * block + 1)
+
+        attend_back(block, i % 2)
         return 0
 
-    lax.fori_loop(0, 4, all_heads, 0)
+    lax.fori_loop(0, 4, half_block, 0)
     first = jnp.where(p.z == 0, 1, 0)
     tails = []
     for block in range(2):
         to_y = (p.y + 4 - first) % 4 if block == 0 else p.y
         slot = first if block == 0 else 1 - first
         tails.append(links.send(tail_out.at[block], tail_in.at[slot], p.at(y=to_y, z=(p.z + 3) % 4)))
+    r_out.pass_all()
     w_gu.start2()
+    grads_into(wo, gb, mixed, 256)
+    w_o = WeightReduce(links, p, wo, in_o, in2_o, fin_o, 128)
+    w_o.start0()
     w_d.start1()
-    r_out.sent()
-    b_out.share()
     for copy in tails:
         copy.wait_recv()
     for block in range(2):
         whole = last_kv[block] + tail_in[block].astype(f32)
         act[2 * block + 1, 1, pl.ds(64, 64), 256:] = whole.astype(bf16)
-
-    load_wq.wait()
-    r_attn = GroupReduce(p, partial_of(act, wq, 768), (send_c, recv_c1, tmp, snd, rcv1, own), sems(2))
+    r_out.finish()
+
+    def result_rows(i, _):
+        r = pl.ds(i * 16, 16)
+        res_own[r] = (resid[r] + own[r]).astype(bf16)
+        return 0
+
+    lax.fori_loop(0, OWNED // 16, result_rows, 0)
+    for device in (sibling, p.at(x=(p.x + 1) % 4), p.at(x=(p.x + 3) % 4)):
+        pl.semaphore_signal(ready, inc=1, device_id=device, device_id_type=MESH)
+    r_out.sent()
     pl.semaphore_wait(ready, 3)
+    r_attn = group_reduce(3, partial_of(act, wq, 768))
     r_attn.run()
+    b_out = BlockGather(links, p, res_own, result_o)
     load_xr.wait()
     grads_into(wq, nm, act, 768)
     w_q = WeightReduce(links, p, wq, in_q, in2_q, fin_q, 384)
     w_q.start0()
     w_gu.start3()
     w_d.start2()
-    mixed_part = gg.at[:, :, :, pl.ds(256, 256)]
-    grads_into(wo, gb, mixed_part, 256)
-    w_o = WeightReduce(links, p, wo, in_o, in2_o, fin_o, 128)
-    w_o.start0()
-    load_hid.wait()
+    w_o.start1()
     r_attn.finish()
 
     def input_rows(i, _):
@@ -978,27 +900,27 @@
     w_q.start1()
     w_gu.start4()
     w_d.start3()
-    w_o.start1()
+    w_o.start2()
+    b_out.share()
     w_q.start2()
-    w_o.start2()
     w_d.start4()
+    w_o.start3()
     w_q.start3()
-    w_o.start3()
+    w_o.start4()
     b_in.share()
     w_q.start4()
-    w_o.start4()
     for item in (b_out, b_in, w_gu, w_d, w_q, w_o):
         item.done()
     r_attn.sent()
     links.finish()
 
 
-def backward_call(wq, wo, gu, d, xr, q, kv, mixed, resid, nm, cot, hid, bias):
+def block_call(lengths, pk_q, pk_o, pk_gu, pk_d, hid, cot):
     sds = jax.ShapeDtypeStruct
     group = (4, 2, OWNED)
     vm = pltpu.VMEM
-    return pl.pallas_call(
-        backward_kernel,
+    outs = pl.pallas_call(
+        block_kernel,
         out_shape=(
             sds((BLOCK, 2048), bf16),
             sds((BLOCK, 2048), bf16),
@@ -1006,9 +928,11 @@
             sds((2, 64, 768), bf16),
             sds((2, 64, 768), bf16),
             sds((2, 64, 256), bf16),
+            sds(group + (2048,), bf16),
+            sds(group + (512,), bf16),
         ),
-        in_specs=[ANY] * 13,
-        out_specs=[ANY] * 6,
+        in_specs=[pl.BlockSpec(memory_space=pltpu.SMEM)] + [ANY] * 6,
+        out_specs=[ANY] * 8,
         scratch_shapes=[
             vm((4, 2, 4, 64, 768), bf16),
             vm((4, 2, 4, 64, 256), bf16),
@@ -1019,7 +943,6 @@
             vm(group + (768,), bf16),
             vm(group + (1408,), bf16),
             vm((2, BLOCK + WINDOW, 512), bf16),
-            vm((8, 128, 192), bf16),
             vm((OWNED, 2048), f32),
             vm((OWNED, 2048), bf16),
             vm((OWNED, 2048), f32),
@@ -1044,18 +967,43 @@
             vm((4, OWNED, 512), f32),
             vm((4, 4, OWNED, 512), bf16),
             vm((4, 6, 64, 512), bf16),
-            pltpu.SemaphoreType.DMA((130,)),
-            pltpu.SemaphoreType.DMA((130,)),
+            pltpu.SemaphoreType.DMA((220,)),
+            pltpu.SemaphoreType.DMA((220,)),
             pltpu.SemaphoreType.DMA((24,)),
-            pltpu.SemaphoreType.DMA((60,)),
-            pltpu.SemaphoreType.DMA((60,)),
+            pltpu.SemaphoreType.DMA((80,)),
+            pltpu.SemaphoreType.DMA((80,)),
             pltpu.SemaphoreType.REGULAR,
         ],
         compiler_params=pltpu.CompilerParams(
-            collective_id=1, has_side_effects=True, vmem_limit_bytes=60 * 2**20
+            collective_id=0, has_side_effects=True, vmem_limit_bytes=60 * 2**20
         ),
-        name="backward",
-    )(wq, wo, gu, d, xr, q, kv, mixed, resid, nm, cot, hid, bias)
+        name="block",
+    )(lengths, pk_q, pk_o, pk_gu, pk_d, hid.reshape(2, 2, OWNED, 2048), cot.reshape(2, 2, OWNED, 2048))
+    return outs[:6]
+
+
+def pack_ff(gate, up, down):
+    def tail(w):
+        return jnp.pad(w[:, 640:], ((0, 0), (0, 16)))
+
+    def one(k):
+        g, u, d = (w[:, k * 688 : (k + 1) * 688] for w in (gate, up, down))
+        return (
+            jnp.concatenate([g[:, :640], u[:, :640], tail(g), tail(u)], axis=1),
+            jnp.pad(d, ((0, 0), (0, 80))),
+        )
+
+    (gu0, d0), (gu1, d1) = one(0), one(1)
+    return jnp.stack([gu0, gu1]), jnp.stack([d0, d1])
+
+
+def pack_attn(query, key, value, out):
+    def one(k):
+        part = slice(k * 256, (k + 1) * 256)
+        return jnp.concatenate([query[:, part], key[:, part], value[:, part]], axis=1), out[:, part]
+
+    (q0, o0), (q1, o1) = one(0), one(1)
+    return jnp.stack([q0, q1]), jnp.stack([o0, o1])
 
 
 def per_device(
@@ -1072,7 +1020,6 @@
     lengths,
     cotangent,
 ):
-    xh = lax.axis_index("xh")
     gain_attn = norm_gain_attn.astype(f32)[:, None]
     gain_mlp = norm_gain_mlp.astype(f32)[:, None]
     scaled = lambda w, g: (w.astype(f32) * g).astype(bf16)
@@ -1080,22 +1027,8 @@
         scaled(w_query, gain_attn), scaled(w_key, gain_attn), scaled(w_value, gain_attn), w_out.T
     )
     pk_gu, pk_d = pack_ff(scaled(w_gate, gain_mlp), scaled(w_up, gain_mlp), w_down.T)
-    bias = attention_bias(lengths)
-    wq, wo, gu, d, xr, q, kv, mixed, resid, nm, cot = forward_call(
-        pk_q, pk_o, pk_gu, pk_d, hidden_in, cotangent, bias
-    )
-    group = (4, 2, OWNED)
-    result, input_grad, fin_gu, fin_d, fin_q, fin_o = backward_call(
-        wq, wo, gu, d,
-        xr.reshape(group + (2048,)),
-        q.reshape(group + (256,)),
-        kv,
-        mixed.reshape(group + (256,)),
-        resid,
-        nm,
-        cot.reshape(group + (2048,)),
-        hidden_in,
-        bias,
+    result, input_grad, fin_gu, fin_d, fin_q, fin_o = block_call(
+        lengths, pk_q, pk_o, pk_gu, pk_d, hidden_in, cotangent
     )
 
     def joined(fin, *spans):

time: 336 us -> 289 us (0.86)
  Pallas kernels: 298 us -> 257 us
  other arithmetic: 17.7 us -> 11.4 us
    pallas_call x2 -> x1, Pallas kernels: 298 us -> 257 us  [block_call(): pl.pallas_call(block_kernel, out_shape=(sds((BLOCK, 2048), bf16), sds((BL...]
    add x3 -> x0, other arithmetic: 4.09 us -> none  [the longest x1 2.01 us: attention_bias(): key = starts - WINDOW + jnp.arange(192, dtype=jnp.int32)[None, None, :]]
  transfers between devices with their start and end apart: 2 -> 2, of which waited for: 2 -> 2; matrix products, arithmetic and copies ran while one was open for 0% -> 1% of each run, Pallas kernels for 0% -> 0%
where the time goes in v4:
time: 289 us
  Pallas kernels  257 us (89%)
  local copies, waits for them, and re-layouts  11.8 us (4%)
  other arithmetic  11.4 us (4%)
  starting transfers between devices  7.27 us (3%)
    pallas_call x1, Pallas kernels, block_call(): pl.pallas_call(block_kernel, out_shape=(sds((BLOCK, 2048), bf16), sds((BL...  257 us
    ppermute x2, starting transfers between devices, flip(): return lax.ppermute(value, axis, [(0, 1), (1, 0)])  7.27 us
  transfers between devices with their start and end apart: 2, of which 2 were waited for; matrix products, arithmetic and copies ran while one was open for 1% of the time, Pallas kernels for 0%

profile of v4, /device:TPU:1, one launch (start us, length us, event | category | flops | bytes accessed | tf_op | source)
XLA Modules:
  0.0 288.8 jit_solution(17292536648256307187)
XLA Ops:
  0.7 0.7 convert_element_type.74
  1.4 1.1 fusion.1
  2.7 0.7 convert_element_type.67
  3.4 0.8 slice_bitcast_fusion.7
  4.2 1.0 slice.216
  5.1 1.0 fusion.4
  6.9 0.7 pad_maximum_fusion.2.pk_d
  7.7 0.7 pad_maximum_fusion.1.pk_q
  8.6 0.8 pad_maximum_fusion.pk_gu
  9.3 257.0 %block.1 = (bf16[512,2048]{1,0:T(8,128)(2,1)}, bf16[512,2048]{1,0:T(8,128)(2,1)}, bf16[2,64,1408]{2,1,0:T(8,128)(2,1)}, bf16[2,64,768]{2,1,0:T(8,128)(2,1)}, bf1...) custom-call(s32[3]{0:T(128)} %lengths.1, ...), custom_call_target="tpu_custom_call" | custom-call | tf_op jit(solution)/shard_map/block/pallas_call | solution.py:922
  266.4 1.1 slice_bitcast_fusion
  267.7 0.7 fusion.14
  268.4 1.0 slice_bitcast_fusion.5
  270.0 1.0 concatenate.41
  271.0 0.9 concatenate.40
  271.9 1.8 convert_multiply_fusion
  273.7 1.8 convert_multiply_fusion.6
  275.5 2.1 collective-permute-start
  277.7 0.8 convert_bitcast_fusion
  278.6 5.1 %collective-permute-start.1 = (f32[2,64]{1,0:T(2,128)S(1)}, f32[2,64]{1,0:T(2,128)S(1)}, u32[]{:S(2)}, u32[]{:S(2)}) collective-permute-start(f32[2,64]{1,0:T(2,128)S(1)} %fusion.11), channel_id=1, source_target_pairs={{0,1},{1,0},{2,3},{3,2},{4,5},{5,4},{6,7},{7,6},{8,9},{9,8},{10,11... | collective-permute-start | bytes 1544 | tf_op jit(solution)/shard_map/ppermute | solution.py:21
  283.7 0.7 convert_bitcast_fusion.1
  285.1 1.3 copy.25
  286.4 1.0 copy-done
  287.4 1.3 copy.26
  (54 shorter events, 2.7 us)
Async XLA Ops:
  0.6 6.2 %copy-start.12 = (pred[768]{0:T(1024)(128)(4,1)S(1)}, pred[768]{0:T(1024)(128)(4,1)}, u32[]{:S(2)}) copy-start(pred[768]{0:T(1024)(128)(4,1)} %constant.5.clone.1) | copy-start | bytes 2308
  0.7 6.2 %copy-start.7 = (bf16[1376,64]{0,1:T(8,128)(2,1)S(1)}, bf16[1376,64]{0,1:T(8,128)(2,1)}, u32[]{:S(2)}) copy-start(bf16[1376,64]{0,1:T(8,128)(2,1)} %param.21) | copy-start | bytes 528388
  1.4 7.0 %copy-start.10 = (f32[64]{0:T(128)}, f32[64]{0:T(128)S(1)}, u32[]{:S(2)}) copy-start(f32[64]{0:T(128)S(1)} %convert_element_type.74) | copy-start | bytes 772
  3.4 2.8 copy-start.11
  266.4 5.5 %copy-start.2 = (bf16[64,1376]{1,0:T(8,128)(2,1)S(1)}, bf16[64,1376]{1,0:T(8,128)(2,1)}, u32[]{:S(2)}) copy-start(bf16[64,1376]{1,0:T(8,128)(2,1)} %param.20) | copy-start | bytes 528388
  266.4 5.5 %copy-start.3 = (bf16[64,1376]{1,0:T(8,128)(2,1)S(1)}, bf16[64,1376]{1,0:T(8,128)(2,1)}, u32[]{:S(2)}) copy-start(bf16[64,1376]{1,0:T(8,128)(2,1)} %param.19) | copy-start | bytes 528388
  266.4 7.3 %copy-start.4 = (bf16[64,512]{1,0:T(8,128)(2,1)S(1)}, bf16[64,512]{1,0:T(8,128)(2,1)}, u32[]{:S(2)}) copy-start(bf16[64,512]{1,0:T(8,128)(2,1)} %param.14) | copy-start | bytes 196612
  266.4 7.3 %copy-start.5 = (bf16[64,512]{1,0:T(8,128)(2,1)S(1)}, bf16[64,512]{1,0:T(8,128)(2,1)}, u32[]{:S(2)}) copy-start(bf16[64,512]{1,0:T(8,128)(2,1)} %param.15) | copy-start | bytes 196612
  266.4 7.3 %copy-start.6 = (bf16[64,512]{1,0:T(8,128)(2,1)S(1)}, bf16[64,512]{1,0:T(8,128)(2,1)}, u32[]{:S(2)}) copy-start(bf16[64,512]{1,0:T(8,128)(2,1)} %param.16) | copy-start | bytes 196612
  267.7 10.0 %copy-start.8 = (bf16[2,64,768]{2,1,0:T(8,128)(2,1)S(1)}, bf16[2,64,768]{2,1,0:T(8,128)(2,1)}, u32[]{:S(2)}) copy-start(bf16[2,64,768]{2,1,0:T(8,128)(2,1)} %get-tuple-element.22) | copy-start | bytes 589828
  270.0 15.1 %copy-start.1 = (bf16[512,2048]{1,0:T(8,128)(2,1)S(1)}, bf16[512,2048]{1,0:T(8,128)(2,1)}, u32[]{:S(2)}) copy-start(bf16[512,2048]{1,0:T(8,128)(2,1)} %get-tuple-element.103) | copy-start | bytes 6291460
  271.9 6.6 %copy-start.9 = (bf16[2,64,256]{2,1,0:T(8,128)(2,1)S(1)}, bf16[2,64,256]{2,1,0:T(8,128)(2,1)}, u32[]{:S(2)}) copy-start(bf16[2,64,256]{2,1,0:T(8,128)(2,1)} %get-tuple-element.21) | copy-start | bytes 196612
  275.5 3.1 %collective-permute-start = (f32[2,64]{1,0:T(2,128)S(1)}, f32[2,64]{1,0:T(2,128)S(1)}, u32[]{:S(2)}, u32[]{:S(2)}) collective-permute-start(f32[2,64]{1,0:T(2,128)S(1)} %pad_maximum_fusion.7), channel_id=1, source_target_pairs={{0,2},{2,0},{1,3},{3,1},{4,6},{6,4},{5,7},{7,5},{8,10},{10,8},{9,1... | collective-permute-start | bytes 1544 | tf_op jit(solution)/shard_map/ppermute | solution.py:21
  278.6 5.9 %collective-permute-start.1 = (f32[2,64]{1,0:T(2,128)S(1)}, f32[2,64]{1,0:T(2,128)S(1)}, u32[]{:S(2)}, u32[]{:S(2)}) collective-permute-start(f32[2,64]{1,0:T(2,128)S(1)} %fusion.11), channel_id=1, source_target_pairs={{0,1},{1,0},{2,3},{3,2},{4,5},{5,4},{6,7},{7,6},{8,9},{9,8},{10,11... | collective-permute-start | bytes 1544 | tf_op jit(solution)/shard_map/ppermute | solution.py:21
  285.1 2.3 copy-start

commit v5 on v4

--- a/solution.py
+++ b/solution.py
@@ -9,6 +9,8 @@
 WINDOW = 64
 BLOCK = 512
 OWNED = 128
+PIECES = 4
+WIDE = 2048 // PIECES
 AXES = ("y", "xh", "z", "xl", "c")
 
 epsilon = 1e-05
@@ -72,12 +74,11 @@
         copy.start()
         return copy
 
-    def settle(self):
-        for copy in self.started:
+    def settle(self, copies=None):
+        copies = self.started if copies is None else copies
+        for copy in copies:
             copy.wait_send()
-        self.started = []
-
-    finish = settle
+        self.started = [copy for copy in self.started if not any(copy is other for other in copies)]
 
 
 class WeightGather:
@@ -324,38 +325,43 @@
         )
 
     def crossing(self, n):
-        return self.copy(self.send_c.at[n], self.recv_c.at[n], n, self.place.at(c=1 - self.place.c))
+        return self.copy(self.send_c.at[n % 2], self.recv_c.at[n], n, self.place.at(c=1 - self.place.c))
 
     def to_next(self, n):
         pair = pl.ds(0, 2)
         return self.copy(
-            self.snd.at[n, pair], self.rcv.at[n, pair], 4 + n, self.place.at(x=(self.place.x + 1) % 4)
+            self.snd.at[n, pair], self.rcv.at[n, pair], PIECES + n, self.place.at(x=(self.place.x + 1) % 4)
         )
 
     def to_prev(self, n):
         pair = pl.ds(2, 2)
         return self.copy(
-            self.snd.at[n, pair], self.rcv.at[n, pair], 8 + n, self.place.at(x=(self.place.x + 3) % 4)
+            self.snd.at[n, pair], self.rcv.at[n, pair], 2 * PIECES + n, self.place.at(x=(self.place.x + 3) % 4)
         )
 
     def sum_next(self, n):
         return self.copy(
-            self.snd.at[n, 4], self.rcv.at[n, 4], 12 + n, self.place.at(x=(self.place.x + 1) % 4)
+            self.snd.at[n, 4], self.rcv.at[n, 4], 3 * PIECES + n, self.place.at(x=(self.place.x + 1) % 4)
         )
 
     def sum_prev(self, n):
         return self.copy(
-            self.snd.at[n, 5], self.rcv.at[n, 5], 16 + n, self.place.at(x=(self.place.x + 3) % 4)
+            self.snd.at[n, 5], self.rcv.at[n, 5], 4 * PIECES + n, self.place.at(x=(self.place.x + 3) % 4)
         )
 
     def sibling_part(self, n):
         part = self.partial(n, 1 - self.place.c)
-        self.send_c[n] = part.astype(bf16).reshape(4, OWNED, 512)
+
+        @pl.when(n >= 2)
+        def _():
+            self.crossing(n - 2).wait_send()
+
+        self.send_c[n % 2] = part.astype(bf16).reshape(4, OWNED, WIDE)
         self.crossing(n).start()
 
     def own_part(self, n, launch):
         p, tmp, snd = self.place, self.tmp, self.snd
-        part = self.partial(n, p.c).reshape(4, OWNED, 512)
+        part = self.partial(n, p.c).reshape(4, OWNED, WIDE)
         self.crossing(n).wait_recv()
         tmp[...] = part + self.recv_c[n].astype(f32)
         far, nxt, prev = (p.x + 2) % 4, (p.x + 1) % 4, (p.x + 3) % 4
@@ -370,7 +376,7 @@
             self.to_prev(n).start()
         snd[n, 4] = tmp[nxt, low].astype(bf16)
         snd[n, 5] = tmp[prev, high].astype(bf16)
-        self.own[:, pl.ds(pl.multiple_of(n * 512, 512), 512)] = tmp[p.x]
+        self.own[:, pl.ds(pl.multiple_of(n * WIDE, WIDE), WIDE)] = tmp[p.x]
 
     def pass_on(self, n):
         snd, rcv = self.snd, self.rcv
@@ -381,25 +387,27 @@
         snd[n, 5] = (snd[n, 5].astype(f32) + rcv[n, 2].astype(f32)).astype(bf16)
         self.sum_prev(n).start()
 
-    def run(self, launch=True):
+    def run(self, launch=True, pass_on=True, hooks=()):
         def body(i, _):
-            @pl.when(i < 4)
+            @pl.when(i < PIECES)
             def _():
                 self.sibling_part(i)
 
-            @pl.when((i >= 1) & (i < 5))
+            @pl.when((i >= 1) & (i < PIECES + 1))
             def _():
                 self.own_part(i - 1, launch)
 
-            if launch:
+            if pass_on:
 
                 @pl.when(i >= 2)
                 def _():
                     self.pass_on(i - 2)
 
-            return 0
-
-        lax.fori_loop(0, 6 if launch else 5, body, 0)
+            for step, hook in hooks:
+                pl.when(i == step)(hook)
+            return 0
+
+        lax.fori_loop(0, PIECES + 2 if pass_on else PIECES + 1, body, 0)
 
     def launch(self):
         def body(n, _):
@@ -407,18 +415,18 @@
             self.to_prev(n).start()
             return 0
 
-        lax.fori_loop(0, 4, body, 0)
-
-    def pass_all(self):
+        lax.fori_loop(0, PIECES, body, 0)
+
+    def pass_range(self, start, stop):
         def body(n, _):
             self.pass_on(n)
             return 0
 
-        lax.fori_loop(0, 4, body, 0)
+        lax.fori_loop(start, stop, body, 0)
 
     def finish(self):
         def body(n, _):
-            lanes = pl.ds(pl.multiple_of(n * 512, 512), 512)
+            lanes = pl.ds(pl.multiple_of(n * WIDE, WIDE), WIDE)
             low, high = pl.ds(0, 64), pl.ds(64, 64)
             rcv, own = self.rcv, self.own
             self.sum_next(n).wait_recv()
@@ -427,15 +435,18 @@
             own[high, lanes] = own[high, lanes] + rcv[n, 1].astype(f32) + rcv[n, 5].astype(f32)
             return 0
 
-        lax.fori_loop(0, 4, body, 0)
+        lax.fori_loop(0, PIECES, body, 0)
 
     def sent(self):
         def body(n, _):
-            for copy in (self.crossing, self.to_next, self.to_prev, self.sum_next, self.sum_prev):
+            for copy in (self.to_next, self.to_prev, self.sum_next, self.sum_prev):
                 copy(n).wait_send()
             return 0
 
-        lax.fori_loop(0, 4, body, 0)
+        self.crossing(PIECES - 2).wait_send()
+        self.crossing(PIECES - 1).wait_send()
+
+        lax.fori_loop(0, PIECES, body, 0)
 
 
 class GroupGather:
@@ -480,29 +491,119 @@
             copy.wait_recv()
         self.paired[3].start()
 
+    def sent(self):
+        self.links.settle(self.first + self.second + self.third + self.paired)
+
     def ready(self, k):
         self.paired[k].wait_recv()
 
 
-class BlockGather:
-    def __init__(self, links, place, own, out):
+class BlockExchange:
+    def __init__(self, links, place, block, whole):
         p = place
-        self.links, self.place, self.out = links, place, out
-        self.sibling = p.at(c=1 - p.c)
-        mine = out.at[pl.ds(p.q * OWNED, OWNED)]
-        self.local = links.local(own, mine)
-        self.across = links.send(own, mine, p.at(x=p.xh * 2 + 1 - p.xl))
-        self.paired = [links.send(own, mine, self.sibling)]
+        self.place, self.links = p, links
+        beside = p.at(x=2 * p.xh + 1 - p.xl)
+        sibling = p.at(c=1 - p.c)
+        self.near, self.next = 3 - p.x, 2 * (1 - p.xh) + p.xl
+        halves = [pl.ds(0, 64), pl.ds(64, 64)]
+        self.cross = [links.send(block.at[p.xl, p.c, h], whole.at[p.x, p.c, h], p.at(x=3 - p.x)) for h in halves]
+        self.across = [
+            links.prepare(whole.at[self.near, p.c, h], whole.at[self.near, p.c, h], beside) for h in halves
+        ]
+        self.paired = [
+            links.prepare(whole.at[x, p.c], whole.at[x, p.c], sibling) for x in (self.near, self.next)
+        ]
+
+    def forward(self, k):
+        self.cross[k].wait_recv()
+        self.across[k].start()
 
     def share(self):
-        p = self.place
-        self.across.wait_recv()
-        theirs = self.out.at[pl.ds(((1 - p.xl) * 2 + p.c) * OWNED, OWNED)]
-        self.paired.append(self.links.send(theirs, theirs, self.sibling))
+        self.paired[0].start()
+
+    def share_next(self):
+        for copy in self.across:
+            copy.wait_recv()
+        self.paired[1].start()
+
+    def done(self, k):
+        self.paired[k].wait_recv()
+
+
+class BlockReduce(GroupReduce):
+    def __init__(self, place, partial, bufs, sems, extra=None):
+        self.place, self.partial, self.extra = place, partial, extra
+        self.send_c, self.recv_c, self.tmp, self.moving = bufs
+        self.send_sems, self.recv_sems = sems
+        self.facing, self.beside = place.at(x=3 - place.x), place.at(x=2 * place.xh + 1 - place.xl)
+
+    def part(self, which, n):
+        lanes = pl.ds(pl.multiple_of(n * WIDE, WIDE), WIDE)
+        return self.moving.at[pl.ds(2 * (which // 2), 2), which % 2, :, lanes]
+
+    def over(self, n):
+        return self.copy(self.part(0, n), self.part(1, n), PIECES + n, self.facing)
+
+    def across(self, n):
+        return self.copy(self.part(2, n), self.part(3, n), 2 * PIECES + n, self.beside)
+
+    def own_part(self, n, launch):
+        p, tmp = self.place, self.tmp
+        part = self.partial(n, p.c).reshape(4, OWNED, WIDE)
+        self.crossing(n).wait_recv()
+        tmp[...] = part + self.recv_c[n].astype(f32)
+        if self.extra is not None:
+            lanes = pl.ds(pl.multiple_of(n * WIDE, WIDE), WIDE)
+            tmp[p.x] += self.extra[:, lanes]
+        self.part(0, n)[...] = tmp[pl.ds(2 * (1 - p.xh), 2)].astype(bf16)
+        if launch:
+            self.over(n).start()
+        self.part(2, n)[...] = tmp[pl.ds(2 * p.xh, 2)].astype(bf16)
+
+    def pass_on(self, n):
+        self.over(n).wait_recv()
+        mine = self.part(2, n)
+        mine[...] = (mine[...].astype(f32) + self.part(1, n)[...].astype(f32)).astype(bf16)
+        self.across(n).start()
+
+    def launch(self):
+        def body(n, _):
+            self.over(n).start()
+            return 0
+
+        lax.fori_loop(0, PIECES, body, 0)
+
+    def finish(self):
+        def body(n, _):
+            self.across(n).wait_recv()
+            return 0
+
+        lax.fori_loop(0, PIECES, body, 0)
+
+    def total(self, tile, rows):
+        return self.moving[2 + tile, 0, rows].astype(f32) + self.moving[2 + tile, 1, rows].astype(f32)
+
+    def crossed(self):
+        self.crossing(PIECES - 2).wait_send()
+        self.crossing(PIECES - 1).wait_send()
+
+    def sent(self):
+        def body(n, _):
+            self.over(n).wait_send()
+            self.across(n).wait_send()
+            return 0
+
+        lax.fori_loop(0, PIECES, body, 0)
+
+
+class BlockOut:
+    def __init__(self, links, place, rows, out):
+        mine = out.at[:, place.c]
+        self.local = links.local(rows, mine)
+        self.paired = links.send(rows, mine, place.at(c=1 - place.c))
 
     def done(self):
-        for copy in self.paired:
-            copy.wait_recv()
+        self.paired.wait_recv()
         self.local.wait()
 
 
@@ -514,7 +615,7 @@
 def block_kernel(
     lengths, pk_q, pk_o, pk_gu, pk_d, hid, cot_in,
     result_o, grad_o, fin_gu, fin_d, fin_q, fin_o, xr_o, qm_o,
-    wq, wo, gu, d, nm, cot, act, gg, kv, resid, hid_own, gres, own, low_own, res_own, gb,
+    wq, wo, gu, d, nm, cot, act, gg, kv, resid, hid_pair, own, gb,
     acc, last_kv, tail_out, tail_in, in_gu, in_d, in_q, in_o, in2_gu, in2_d, in2_q, in2_o,
     send_c, snd, tmp, recv_c, rcv,
     send_sems, recv_sems, local_sems, group_send, group_recv, ready,
@@ -522,72 +623,77 @@
     p = Place()
     links = Links(send_sems, recv_sems, local_sems)
     sibling = p.at(c=1 - p.c)
-    facing = p.at(x=3 - p.x)
+    facing, beside = p.at(x=3 - p.x), p.at(x=2 * p.xh + 1 - p.xl)
+
+    def signal(semaphore, devices):
+        for device in devices:
+            pl.semaphore_signal(semaphore, inc=1, device_id=device, device_id_type=MESH)
+
     hidg, xr = gb, nm
 
     own_pair = pl.ds(2 * p.xh, 2)
     own_hidden = links.local(hid, hidg.at[own_pair])
-    load_hid = links.local(hid.at[p.xl, p.c], hid_own)
+    load_hid = links.local(hid.at[:, p.c], hid_pair)
     own_cot = links.local(cot_in, cot.at[own_pair])
     greet(p)
-
-    def cross(ref, whole):
-        return [links.send(ref.at[p.c, k], whole.at[2 * p.xh + p.c, k], facing) for k in range(2)]
-
-    def handed(whole, copies):
-        shared = []
-        for k in range(2):
-            copies[k].wait_recv()
-            part = whole.at[2 * (1 - p.xh) + p.c, k]
-            shared.append(links.send(part, part, sibling))
-        return shared
-
     g_q = WeightGather(links, p, pk_q, wq, 384)
-    hidden_sent = cross(hid, hidg)
     g_o = WeightGather(links, p, pk_o, wo, 128)
+    e_hid = BlockExchange(links, p, hid, hidg)
+    g_q.start0()
+    g_o.start0()
+    def norm_rows(tile, core):
+        def body(i, _):
+            r = pl.ds(i * 32, 32)
+            xr[tile, core, r] = unit_scale(hidg[tile, core, r].astype(f32)).astype(bf16)
+            return 0
+
+        lax.fori_loop(0, 4, body, 0)
+
+    def norm_own(i, _):
+        norm_rows(2 * p.xh + i // 2, i % 2)
+        return 0
+
+    own_hidden.wait()
+    lax.fori_loop(0, 4, norm_own, 0)
+    g_q.start1()
+    g_o.start1()
+    e_hid.forward(0)
+    g_q.start2()
     g_gu = WeightGather(links, p, pk_gu, gu, 768)
     g_d = WeightGather(links, p, pk_d, d, 384)
-    g_q.start0()
-    g_o.start0()
-
-    def norm_rows(tile):
-        def body(i, _):
-            core, r = i // 4, pl.ds((i % 4) * 32, 32)
-            xr[tile, core, r] = unit_scale(hidg[tile, core, r].astype(f32)).astype(bf16)
-            return 0
-
-        lax.fori_loop(0, 8, body, 0)
-
-    own_hidden.wait()
-    norm_rows(2 * p.xh)
-    norm_rows(2 * p.xh + 1)
-    g_q.start1()
-    g_o.start1()
-    g_q.start2()
+    e_hid.forward(1)
+    e_hid.share()
+    e_cot = BlockExchange(links, p, cot_in, cot)
+    norm_rows(e_hid.near, p.c)
+    g_q.start3()
     g_o.start2()
     g_gu.start0()
     g_d.start0()
-    shared = handed(hidg, hidden_sent)
-    cot_sent = cross(cot_in, cot)
-    norm_rows(2 * (1 - p.xh) + p.c)
-    for copy in shared:
-        copy.wait_recv()
-    norm_rows(2 * (1 - p.xh) + 1 - p.c)
-    xr_spill = links.local(xr, xr_o)
-    g_q.start3()
-    g_o.start3()
-    g_gu.start1()
-    g_d.start1()
+    e_hid.done(0)
+    norm_rows(e_hid.near, 1 - p.c)
     g_q.done()
 
-    def project(t, _):
+    def project(t):
         w = wq[...].reshape(2048, 768)
         out = jnp.dot(xr[t].reshape(256, 2048), w, preferred_element_type=f32).astype(bf16)
         gg[t, :, :, 0:256] = out[:, :256].reshape(2, OWNED, 256)
         kv[t // 2, pl.ds((t % 2) * 256 + WINDOW, 256)] = out[:, 256:]
+
+    def project_three(i, _):
+        project(jnp.where(i < 2, 2 * p.xh + i, e_hid.near))
         return 0
 
-    lax.fori_loop(0, 4, project, 0)
+    lax.fori_loop(0, 3, project_three, 0)
+    g_o.start3()
+    e_hid.share_next()
+    norm_rows(e_hid.next, p.c)
+    g_gu.start1()
+    g_d.start1()
+    e_cot.forward(0)
+    e_hid.done(1)
+    norm_rows(e_hid.next, 1 - p.c)
+    xr_spill = links.local(xr, xr_o)
+    project(e_hid.next)
 
     tails = []
     last = jnp.where(p.z == 3, 1, 0)
@@ -601,8 +707,6 @@
                 p.at(y=to_y, z=(p.z + 1) % 4),
             )
         )
-    g_gu.start2()
-
     end0 = lengths[0]
     end1 = end0 + lengths[1]
 
@@ -621,29 +725,36 @@
         expo = jnp.exp(scores - jnp.max(scores, axis=-1, keepdims=True))
         return expo / jnp.sum(expo, axis=-1, keepdims=True)
 
-    def attend(block, chunk, head):
+    def attend(block, chunk):
         x, core = block * 2 + chunk // 2, chunk % 2
-        r, lane = pl.multiple_of(chunk * 128, 128), pl.multiple_of(head * 128, 128)
-        query = gg[x, core, :, pl.ds(lane, 128)]
-        keys = kv[block, pl.ds(r, 192), pl.ds(lane, 128)]
-        values = kv[block, pl.ds(r, 192), pl.ds(lane + 256, 128)]
-        probs = probabilities(query, keys, block, chunk).astype(bf16)
-        out = jnp.dot(probs, values, preferred_element_type=f32)
-        gg[x, core, :, pl.ds(lane + 256, 128)] = out.astype(bf16)
+        r = pl.multiple_of(chunk * 128, 128)
+        for head in range(2):
+            lane = head * 128
+            query = gg[x, core, :, lane : lane + 128]
+            keys = kv[block, pl.ds(r, 192), lane : lane + 128]
+            values = kv[block, pl.ds(r, 192), lane + 256 : lane + 384]
+            probs = probabilities(query, keys, block, chunk).astype(bf16)
+            out = jnp.dot(probs, values, preferred_element_type=f32)
+            gg[x, core, :, lane + 256 : lane + 384] = out.astype(bf16)
 
     def inner(i, _):
-        attend(i // 6, (i % 6) // 2 + 1, i % 2)
+        attend(i // 3, i % 3 + 1)
         return 0
 
-    lax.fori_loop(0, 12, inner, 0)
+    e_cot.forward(1)
+    e_cot.share()
+    g_gu.start2()
+    g_d.start2()
+    lax.fori_loop(0, 6, inner, 0)
+    e_cot.share_next()
     for copy in tails:
         copy.wait_recv()
 
     def first_chunk(i, _):
-        attend(i // 2, 0, i % 2)
+        attend(i, 0)
         return 0
 
-    lax.fori_loop(0, 4, first_chunk, 0)
+    lax.fori_loop(0, 2, first_chunk, 0)
     mixed = gg.at[:, :, :, pl.ds(256, 256)]
     g_o.done()
     xr_spill.wait()
@@ -652,7 +763,7 @@
         def partial(n, core):
             return lax.dot_general(
                 left[:, core, :, start : start + width].reshape(512, width),
-                right[n].reshape(512, width),
+                right[n].reshape(WIDE, width),
                 TURNED,
                 preferred_element_type=f32,
             )
@@ -660,22 +771,22 @@
         return partial
 
     def group_reduce(k, partial):
-        span = pl.ds(20 * k, 20)
+        span = pl.ds(5 * PIECES * k, 5 * PIECES)
         return GroupReduce(
             p, partial, (send_c, recv_c, tmp, snd, rcv, own), (group_send.at[span], group_recv.at[span])
         )
 
     r_branch = group_reduce(0, partial_of(gg, wo, 256, 256))
-    r_branch.run()
-    cot_shared = handed(cot, cot_sent)
-    g_d.start2()
+    r_branch.run(pass_on=False)
+    r_branch.pass_range(0, PIECES)
     g_gu.start3()
+    g_d.start3()
     load_hid.wait()
     r_branch.finish()
 
     def resid_rows(i, _):
         r = pl.ds(i * 16, 16)
-        total = hid_own[r].astype(f32) + own[r]
+        total = hid_pair[p.xl, r].astype(f32) + own[r]
         resid[r] = total
         nm[p.x, p.c, r] = unit_scale(total).astype(bf16)
         return 0
@@ -685,18 +796,17 @@
     g_nm.start()
     q_spill = links.local(gg.at[:, :, :, pl.ds(0, 512)], qm_o)
     g_gu.done()
-    g_d.start3()
     own_cot.wait()
-    for copy in cot_shared:
-        copy.wait_recv()
+    for k in range(2):
+        e_cot.done(k)
     q_spill.wait()
-    g_nm.forward()
     g_d.done()
     g_nm.ready(0)
 
     def feed(k, _):
         @pl.when(k == 1)
         def _():
+            g_nm.forward()
             g_nm.share_near()
             g_nm.ready(1)
 
@@ -738,9 +848,9 @@
     r_branch.sent()
     links.settle()
     r_mlp = group_reduce(1, partial_of(gg, gu, 1408))
-    r_mlp.run()
-
-    def grads_into(out, left, right, width):
+    r_mlp.run(pass_on=False)
+
+    def grads_into(out, left, right, width, reduce=None):
         def body(n, _):
             lanes = pl.ds(pl.multiple_of(n * 256, 256), 256)
             part = lax.dot_general(
@@ -750,21 +860,26 @@
                 preferred_element_type=f32,
             )
             out[n // 2, n % 2] = part.astype(bf16).reshape(4, 64, width)
+            if reduce is not None:
+
+                @pl.when(n % 2 == 0)
+                def _():
+                    reduce.pass_on(n // 2)
+
             return 0
 
         lax.fori_loop(0, 8, body, 0)
 
-    grads_into(gu, nm, gg, 1408)
+    grads_into(gu, nm, gg, 1408, r_mlp)
     w_gu = WeightReduce(links, p, gu, in_gu, in2_gu, fin_gu, 768)
     w_gu.start0()
-    load_xr = links.local(xr_o, nm)
+    signal(ready.at[0], (facing, beside))
     load_qm = links.local(qm_o, gg.at[:, :, :, pl.ds(0, 512)])
     r_mlp.finish()
 
     def grad_rows(i, _):
         r = pl.ds(i * 16, 16)
         grad = cot[p.x, p.c, r].astype(f32) + norm_back(own[r], resid[r])
-        gres[r] = grad
         gb[p.x, p.c, r] = grad.astype(bf16)
         return 0
 
@@ -774,12 +889,18 @@
     r_mlp.sent()
     g_branch.ready(0)
 
-    r_out = group_reduce(2, partial_of(act, d, 768))
-    r_out.run(launch=False)
+    def block_reduce(k, partial, moving, extra=None):
+        span = pl.ds(5 * PIECES * k, 5 * PIECES)
+        sems = (group_send.at[span], group_recv.at[span])
+        return BlockReduce(p, partial, (send_c, recv_c, tmp, moving), sems, extra)
+
+    r_out = block_reduce(2, partial_of(act, d, 768), nm, resid)
+    r_out.run(launch=False, pass_on=False)
     g_branch.forward()
+    w_gu.start1()
     grads_into(d, cot, act, 768)
+    signal(ready.at[1], (facing, beside, sibling))
     w_d = WeightReduce(links, p, d, in_d, in2_d, fin_d, 384)
-    w_gu.start1()
     w_d.start0()
     g_branch.share_near()
 
@@ -787,132 +908,134 @@
         out = jnp.dot(gb[t].reshape(256, 2048), wo[...].reshape(2048, 256), preferred_element_type=f32)
         gg[t, :, :, 512:768] = out.astype(bf16).reshape(2, OWNED, 256)
 
-    def attend_back(block, head):
-        lane = pl.multiple_of(head * 128, 128)
+    first = jnp.where(p.z == 0, 1, 0)
+    tails = []
+
+    def attend_back(block):
         acc[...] = jnp.zeros_like(acc)
 
         def chunk_body(chunk, _):
             x, core = block * 2 + chunk // 2, chunk % 2
             r = pl.multiple_of(chunk * 128, 128)
-            query = gg[x, core, :, pl.ds(lane, 128)]
-            grad = gg[x, core, :, pl.ds(lane + 512, 128)]
-            keys = kv[block, pl.ds(r, 192), pl.ds(lane, 128)]
-            values = kv[block, pl.ds(r, 192), pl.ds(lane + 256, 128)]
-            probs = probabilities(query, keys, block, chunk)
-            probs_low = probs.astype(bf16)
-            grad_probs = lax.dot_general(grad, values, TURNED, preferred_element_type=f32)
-            inner = jnp.sum(probs * grad_probs, axis=-1, keepdims=True)
-            grad_scores = (probs * (grad_probs - inner)).astype(bf16)
-            grad_query = jnp.dot(grad_scores, keys, preferred_element_type=f32) * SCALE
-            act[x, core, :, pl.ds(lane, 128)] = grad_query.astype(bf16)
             rows = pl.ds(r, 192)
-            grad_keys = lax.dot_general(grad_scores, query, LEFT_TURNED, preferred_element_type=f32)
-            acc[0, rows] = acc[0, rows] + grad_keys * SCALE
-            acc[1, rows] = acc[1, rows] + lax.dot_general(
-                probs_low, grad, LEFT_TURNED, preferred_element_type=f32
-            )
-            return 0
-
-        lax.fori_loop(0, 4, chunk_body, 0)
-        for k in range(2):
-            lanes = pl.ds(pl.multiple_of(lane + 256 * k, 128), 128)
-            tail_out[block, :, lanes] = acc[k, pl.ds(0, WINDOW)].astype(bf16)
-            last_kv[block, :, lanes] = acc[k, pl.ds(BLOCK, WINDOW)]
-
-            def store(i, _):
-                x, core = block * 2 + i // 2, i % 2
-                out = pl.ds(pl.multiple_of(lane + 256 + 256 * k, 128), 128)
-                act[x, core, :, out] = acc[k, pl.ds(WINDOW + i * 128, 128)].astype(bf16)
-                return 0
-
-            lax.fori_loop(0, 4, store, 0)
-
+            for head in range(2):
+                lane = head * 128
+                query = gg[x, core, :, lane : lane + 128]
+                grad = gg[x, core, :, lane + 512 : lane + 640]
+                keys = kv[block, rows, lane : lane + 128]
+                values = kv[block, rows, lane + 256 : lane + 384]
+                probs = probabilities(query, keys, block, chunk)
+                probs_low = probs.astype(bf16)
+                grad_probs = lax.dot_general(grad, values, TURNED, preferred_element_type=f32)
+                inner = jnp.sum(probs * grad_probs, axis=-1, keepdims=True)
+                grad_scores = (probs * (grad_probs - inner)).astype(bf16)
+                grad_query = jnp.dot(grad_scores, keys, preferred_element_type=f32) * SCALE
+                act[x, core, :, lane : lane + 128] = grad_query.astype(bf16)
+                grad_keys = lax.dot_general(grad_scores, query, LEFT_TURNED, preferred_element_type=f32)
+                grad_values = lax.dot_general(probs_low, grad, LEFT_TURNED, preferred_element_type=f32)
+                acc[rows, lane : lane + 128] += grad_keys * SCALE
+                acc[rows, lane + 256 : lane + 384] += grad_values
+            return 0
+
+        chunk_body(0, 0)
+        tail_out[block] = acc[0:WINDOW].astype(bf16)
+        to_y = jnp.where(block == 0, (p.y + 4 - first) % 4, p.y)
+        slot = jnp.where(block == 0, first, 1 - first)
+        tails.append(links.send(tail_out.at[block], tail_in.at[slot], p.at(y=to_y, z=(p.z + 3) % 4)))
+        lax.fori_loop(1, 4, chunk_body, 0)
+        last_kv[block] = acc[BLOCK:]
+
+        def store(i, _):
+            r = pl.ds(pl.multiple_of(WINDOW + i * 128, 64), 128)
+            act[block * 2 + i // 2, i % 2, :, 256:] = acc[r].astype(bf16)
+            return 0
+
+        lax.fori_loop(0, 4, store, 0)
+
+    pl.semaphore_wait(ready.at[0], 2)
+    r_out.launch()
     load_qm.wait()
     g_branch.ready(1)
     g_branch.ready(2)
 
-    def half_block(i, _):
-        @pl.when(i == 2)
-        def _():
-            g_branch.share_far()
-            r_out.launch()
-            g_branch.ready(3)
-
-        block = jnp.where(i < 2, p.xh, 1 - p.xh)
-
-        @pl.when(i % 2 == 0)
-        def _():
-            grad_mixed(2 * block)
-            grad_mixed(2 * block + 1)
-
-        attend_back(block, i % 2)
-        return 0
-
-    lax.fori_loop(0, 4, half_block, 0)
-    first = jnp.where(p.z == 0, 1, 0)
-    tails = []
-    for block in range(2):
-        to_y = (p.y + 4 - first) % 4 if block == 0 else p.y
-        slot = first if block == 0 else 1 - first
-        tails.append(links.send(tail_out.at[block], tail_in.at[slot], p.at(y=to_y, z=(p.z + 3) % 4)))
-    r_out.pass_all()
+    grad_mixed(2 * p.xh)
+    grad_mixed(2 * p.xh + 1)
+
+    attend_back(p.xh)
+    g_branch.share_far()
+    r_out.pass_range(0, 1)
     w_gu.start2()
+    g_branch.ready(3)
+    grad_mixed(2 * (1 - p.xh))
+    grad_mixed(2 * (1 - p.xh) + 1)
+    attend_back(1 - p.xh)
+    r_out.pass_range(1, 2)
+    w_gu.start3()
     grads_into(wo, gb, mixed, 256)
-    w_o = WeightReduce(links, p, wo, in_o, in2_o, fin_o, 128)
-    w_o.start0()
-    w_d.start1()
+    own[...] = gb[2 * p.xh, p.c].astype(f32)
+    resid[...] = gb[2 * p.xh + 1, p.c].astype(f32)
+    g_branch.sent()
+    load_xr = links.local(xr_o, gb)
     for copy in tails:
         copy.wait_recv()
     for block in range(2):
         whole = last_kv[block] + tail_in[block].astype(f32)
         act[2 * block + 1, 1, pl.ds(64, 64), 256:] = whole.astype(bf16)
-    r_out.finish()
-
-    def result_rows(i, _):
-        r = pl.ds(i * 16, 16)
-        res_own[r] = (resid[r] + own[r]).astype(bf16)
-        return 0
-
-    lax.fori_loop(0, OWNED // 16, result_rows, 0)
-    for device in (sibling, p.at(x=(p.x + 1) % 4), p.at(x=(p.x + 3) % 4)):
-        pl.semaphore_signal(ready, inc=1, device_id=device, device_id_type=MESH)
-    r_out.sent()
-    pl.semaphore_wait(ready, 3)
-    r_attn = group_reduce(3, partial_of(act, wq, 768))
-    r_attn.run()
-    b_out = BlockGather(links, p, res_own, result_o)
+    w_d.start1()
+    w_o = WeightReduce(links, p, wo, in_o, in2_o, fin_o, 128)
+    w_o.start0()
+    w_gu.start4()
+    r_out.pass_range(2, 3)
+    r_out.crossed()
+    pl.semaphore_wait(ready.at[1], 3)
+    r_attn = block_reduce(3, partial_of(act, wq, 768), cot)
+    r_attn.run(pass_on=False)
+    r_out.pass_range(3, 4)
+    w_d.start2()
+    w_o.start1()
     load_xr.wait()
-    grads_into(wq, nm, act, 768)
+    grads_into(wq, gb, act, 768)
+    w_d.start3()
     w_q = WeightReduce(links, p, wq, in_q, in2_q, fin_q, 384)
     w_q.start0()
-    w_gu.start3()
-    w_d.start2()
-    w_o.start1()
+    r_attn.pass_range(0, 1)
+    w_o.start2()
+    r_out.finish()
+    r_out.sent()
+
+    def result_rows(i, _):
+        tile, r = i // 8, pl.ds((i % 8) * 16, 16)
+        nm[2 + tile, 0, r] = r_out.total(tile, r).astype(bf16)
+        return 0
+
+    lax.fori_loop(0, 16, result_rows, 0)
+    b_out = BlockOut(links, p, nm.at[pl.ds(2, 2), 0], result_o)
+    w_d.start4()
+    r_attn.pass_range(1, 2)
+    w_q.start1()
+    w_o.start3()
+    r_attn.pass_range(2, 3)
+    w_q.start2()
+    w_o.start4()
+    r_attn.pass_range(3, 4)
+    w_q.start3()
+    w_q.start4()
     r_attn.finish()
 
     def input_rows(i, _):
-        r = pl.ds(i * 16, 16)
-        low_own[r] = (gres[r] + norm_back(own[r], hid_own[r].astype(f32))).astype(bf16)
+        tile, r = i // 8, pl.ds((i % 8) * 16, 16)
+        values = hid_pair[tile, r].astype(f32)
+        base = jnp.where(tile == 0, own[r], resid[r])
+        hid_pair[tile, r] = (base + norm_back(r_attn.total(tile, r), values)).astype(bf16)
         return 0
 
-    lax.fori_loop(0, OWNED // 16, input_rows, 0)
-    b_in = BlockGather(links, p, low_own, grad_o)
-    w_q.start1()
-    w_gu.start4()
-    w_d.start3()
-    w_o.start2()
-    b_out.share()
-    w_q.start2()
-    w_d.start4()
-    w_o.start3()
-    w_q.start3()
-    w_o.start4()
-    b_in.share()
-    w_q.start4()
+    lax.fori_loop(0, 16, input_rows, 0)
+    b_in = BlockOut(links, p, hid_pair, grad_o)
     for item in (b_out, b_in, w_gu, w_d, w_q, w_o):
         item.done()
+    r_attn.crossed()
     r_attn.sent()
-    links.finish()
+    links.settle()
 
 
 def block_call(lengths, pk_q, pk_o, pk_gu, pk_d, hid, cot):
@@ -922,8 +1045,8 @@
     outs = pl.pallas_call(
         block_kernel,
         out_shape=(
-            sds((BLOCK, 2048), bf16),
-            sds((BLOCK, 2048), bf16),
+            sds((2, 2, OWNED, 2048), bf16),
+            sds((2, 2, OWNED, 2048), bf16),
             sds((2, 64, 1408), bf16),
             sds((2, 64, 768), bf16),
             sds((2, 64, 768), bf16),
@@ -944,13 +1067,10 @@
             vm(group + (1408,), bf16),
             vm((2, BLOCK + WINDOW, 512), bf16),
             vm((OWNED, 2048), f32),
-            vm((OWNED, 2048), bf16),
+            vm((2, OWNED, 2048), bf16),
             vm((OWNED, 2048), f32),
-            vm((OWNED, 2048), f32),
-            vm((OWNED, 2048), bf16),
-            vm((OWNED, 2048), bf16),
             vm(group + (2048,), bf16),
-            vm((2, BLOCK + WINDOW, 128), f32),
+            vm((BLOCK + WINDOW, 512), f32),
             vm((2, WINDOW, 512), f32),
             vm((2, WINDOW, 512), bf16),
             vm((2, WINDOW, 512), bf16),
@@ -962,24 +1082,24 @@
             vm((6, 64, 768), bf16),
             vm((6, 64, 768), bf16),
             vm((6, 64, 256), bf16),
-            vm((4, 4, OWNED, 512), bf16),
-            vm((4, 6, 64, 512), bf16),
-            vm((4, OWNED, 512), f32),
-            vm((4, 4, OWNED, 512), bf16),
-            vm((4, 6, 64, 512), bf16),
+            vm((2, 4, OWNED, WIDE), bf16),
+            vm((PIECES, 6, 64, WIDE), bf16),
+            vm((4, OWNED, WIDE), f32),
+            vm((PIECES, 4, OWNED, WIDE), bf16),
+            vm((PIECES, 6, 64, WIDE), bf16),
             pltpu.SemaphoreType.DMA((220,)),
             pltpu.SemaphoreType.DMA((220,)),
             pltpu.SemaphoreType.DMA((24,)),
-            pltpu.SemaphoreType.DMA((80,)),
-            pltpu.SemaphoreType.DMA((80,)),
-            pltpu.SemaphoreType.REGULAR,
+            pltpu.SemaphoreType.DMA((20 * PIECES,)),
+            pltpu.SemaphoreType.DMA((20 * PIECES,)),
+            pltpu.SemaphoreType.REGULAR((2,)),
         ],
         compiler_params=pltpu.CompilerParams(
             collective_id=0, has_side_effects=True, vmem_limit_bytes=60 * 2**20
         ),
         name="block",
     )(lengths, pk_q, pk_o, pk_gu, pk_d, hid.reshape(2, 2, OWNED, 2048), cot.reshape(2, 2, OWNED, 2048))
-    return outs[:6]
+    return tuple(out.reshape(BLOCK, 2048) for out in outs[:2]) + tuple(outs[2:6])
 
 
 def pack_ff(gate, up, down):

time: 289 us -> 247 us (0.85)
  Pallas kernels: 257 us -> 219 us
  starting transfers between devices: 7.27 us -> 2.7 us
    pallas_call x1, Pallas kernels: 257 us -> 219 us  [block_call(): pl.pallas_call(block_kernel, out_shape=(sds((2, 2, OWNED, 2048), bf16), s...]
    ppermute x2, starting transfers between devices: 7.27 us -> 2.7 us  [flip(): return lax.ppermute(value, axis, [(0, 1), (1, 0)])]
where the time goes in v5:
time: 247 us; the launch traced here: 246 us
  Pallas kernels  219 us (89%)
  local copies, waits for them, and re-layouts  11.8 us (5%)
  other arithmetic  11.4 us (5%)
  starting transfers between devices  2.7 us (1%)
    pallas_call x1, Pallas kernels, block_call(): pl.pallas_call(block_kernel, out_shape=(sds((2, 2, OWNED, 2048), bf16), s...  219 us
  transfers between devices with their start and end apart: 2, of which 2 were waited for; matrix products, arithmetic and copies ran while one was open for 1% of the time, Pallas kernels for 0%

profile of v5, /device:TPU:1, one launch (start us, length us, event | category | flops | bytes accessed | tf_op | source)
XLA Modules:
  0.0 246.3 jit_solution(11885496096252910526)
XLA Ops:
  0.7 0.7 convert_element_type.74
  1.4 1.1 fusion.1
  2.7 0.7 convert_element_type.67
  3.4 0.8 slice_bitcast_fusion.7
  4.2 1.0 slice.216
  5.1 1.0 fusion.4
  6.9 0.7 pad_maximum_fusion.2.pk_d
  7.7 0.7 pad_maximum_fusion.1.pk_q
  8.6 0.8 pad_maximum_fusion.pk_gu
  9.3 219.1 %block.1 = (bf16[2,2,128,2048]{3,2,1,0:T(8,128)(2,1)}, bf16[2,2,128,2048]{3,2,1,0:T(8,128)(2,1)}, bf16[2,64,1408]{2,1,0:T(8,128)(2,1)}, bf16[2,64,768]{2,1,0:T(8...) custom-call(s32[3]{0:T(128)} %lengths.1, ...), custom_call_target="tpu_custom_call" | custom-call | tf_op jit(solution)/shard_map/block/pallas_call | solution.py:1045
  228.5 1.1 slice_bitcast_fusion
  229.8 0.7 fusion.14
  230.5 1.0 slice_bitcast_fusion.5
  232.1 1.0 concatenate.41
  233.1 0.9 concatenate.40
  234.0 1.8 convert_multiply_fusion
  235.8 1.8 convert_multiply_fusion.6
  237.6 1.7 collective-permute-start
  239.3 0.8 convert_bitcast_fusion
  240.3 1.0 collective-permute-start.1
  241.3 0.7 convert_bitcast_fusion.1
  242.6 1.3 copy.25
  243.9 1.0 copy-done
  245.0 1.3 copy.26
  (54 shorter events, 2.7 us)
Async XLA Ops:
  0.6 6.2 %copy-start.12 = (pred[768]{0:T(1024)(128)(4,1)S(1)}, pred[768]{0:T(1024)(128)(4,1)}, u32[]{:S(2)}) copy-start(pred[768]{0:T(1024)(128)(4,1)} %constant.5.clone.1) | copy-start | bytes 2308
  0.7 6.2 %copy-start.7 = (bf16[1376,64]{0,1:T(8,128)(2,1)S(1)}, bf16[1376,64]{0,1:T(8,128)(2,1)}, u32[]{:S(2)}) copy-start(bf16[1376,64]{0,1:T(8,128)(2,1)} %param.21) | copy-start | bytes 528388
  1.4 7.0 %copy-start.10 = (f32[64]{0:T(128)}, f32[64]{0:T(128)S(1)}, u32[]{:S(2)}) copy-start(f32[64]{0:T(128)S(1)} %convert_element_type.74) | copy-start | bytes 772
  3.4 2.8 %copy-start.11 = (f32[64]{0:T(128)}, f32[64]{0:T(128)S(1)}, u32[]{:S(2)}) copy-start(f32[64]{0:T(128)S(1)} %convert_element_type.67) | copy-start | bytes 772
  228.5 5.5 %copy-start.2 = (bf16[64,1376]{1,0:T(8,128)(2,1)S(1)}, bf16[64,1376]{1,0:T(8,128)(2,1)}, u32[]{:S(2)}) copy-start(bf16[64,1376]{1,0:T(8,128)(2,1)} %param.20) | copy-start | bytes 528388
  228.5 5.5 %copy-start.3 = (bf16[64,1376]{1,0:T(8,128)(2,1)S(1)}, bf16[64,1376]{1,0:T(8,128)(2,1)}, u32[]{:S(2)}) copy-start(bf16[64,1376]{1,0:T(8,128)(2,1)} %param.19) | copy-start | bytes 528388
  228.5 7.3 %copy-start.4 = (bf16[64,512]{1,0:T(8,128)(2,1)S(1)}, bf16[64,512]{1,0:T(8,128)(2,1)}, u32[]{:S(2)}) copy-start(bf16[64,512]{1,0:T(8,128)(2,1)} %param.14) | copy-start | bytes 196612
  228.5 7.3 %copy-start.5 = (bf16[64,512]{1,0:T(8,128)(2,1)S(1)}, bf16[64,512]{1,0:T(8,128)(2,1)}, u32[]{:S(2)}) copy-start(bf16[64,512]{1,0:T(8,128)(2,1)} %param.15) | copy-start | bytes 196612
  228.5 7.3 %copy-start.6 = (bf16[64,512]{1,0:T(8,128)(2,1)S(1)}, bf16[64,512]{1,0:T(8,128)(2,1)}, u32[]{:S(2)}) copy-start(bf16[64,512]{1,0:T(8,128)(2,1)} %param.16) | copy-start | bytes 196612
  229.8 9.5 %copy-start.8 = (bf16[2,64,768]{2,1,0:T(8,128)(2,1)S(1)}, bf16[2,64,768]{2,1,0:T(8,128)(2,1)}, u32[]{:S(2)}) copy-start(bf16[2,64,768]{2,1,0:T(8,128)(2,1)} %get-tuple-element.22) | copy-start | bytes 589828
  232.1 10.5 %copy-start.1 = (bf16[2,2,128,2048]{3,2,1,0:T(8,128)(2,1)S(1)}, bf16[2,2,128,2048]{3,2,1,0:T(8,128)(2,1)}, u32[]{:S(2)}) copy-start(bf16[2,2,128,2048]{3,2,1,0:T(8,128)(2,1)} %get-tuple-element.17) | copy-start | bytes 6291460
  234.0 6.2 %copy-start.9 = (bf16[2,64,256]{2,1,0:T(8,128)(2,1)S(1)}, bf16[2,64,256]{2,1,0:T(8,128)(2,1)}, u32[]{:S(2)}) copy-start(bf16[2,64,256]{2,1,0:T(8,128)(2,1)} %get-tuple-element.21) | copy-start | bytes 196612
  237.6 2.7 %collective-permute-start = (f32[2,64]{1,0:T(2,128)S(1)}, f32[2,64]{1,0:T(2,128)S(1)}, u32[]{:S(2)}, u32[]{:S(2)}) collective-permute-start(f32[2,64]{1,0:T(2,128)S(1)} %pad_maximum_fusion.7), channel_id=1, source_target_pairs={{0,2},{2,0},{1,3},{3,1},{4,6},{6,4},{5,7},{7,5},{8,10},{10,8},{9,1... | collective-permute-start | bytes 1544 | tf_op jit(solution)/shard_map/ppermute | solution.py:23
  240.3 1.8 collective-permute-start.1
  242.6 2.3 copy-start

commit v6 on v5

--- a/solution.py
+++ b/solution.py
@@ -17,10 +17,6 @@
 masked_score = -1e30
 f32 = jnp.float32
 bf16 = jnp.bfloat16
-
-
-def flip(value, axis):
-    return lax.ppermute(value, axis, [(0, 1), (1, 0)])
 
 
 MESH = pl.DeviceIdType.MESH
@@ -87,9 +83,9 @@
         cols = whole.shape[-1]
         self.parts = (pl.ds(0, cut), pl.ds(cut, cols - cut))
         self.swap = links.send(
-            pack.at[1 - place.xh], whole.at[place.y, place.xh, place.z], place.at(x=(place.x + 2) % 4)
+            pack(1 - place.xh), whole.at[place.y, place.xh, place.z], place.at(x=(place.x + 2) % 4)
         )
-        self.mine = links.local(pack.at[place.xh], whole.at[place.y, place.xh, place.z])
+        self.mine = links.local(pack(place.xh), whole.at[place.y, place.xh, place.z])
 
     def send(self, ref, device):
         return self.links.send(ref, ref, device)
@@ -171,6 +167,7 @@
         p.at(x=(p.x + 3) % 4),
         p.at(x=(p.x + 2) % 4),
         p.at(c=1 - p.c),
+        p.at(x=2 * p.xh + 1 - p.xl, c=1 - p.c),
     )
     for device in partners:
         pl.semaphore_signal(barrier, inc=1, device_id=device, device_id_type=MESH)
@@ -183,7 +180,7 @@
     def _():
         pl.semaphore_signal(barrier, inc=1, device_id=p.at(y=(p.y + 3) % 4, z=0 * p.z + 3), device_id_type=MESH)
 
-    pl.semaphore_wait(barrier, 8 + jnp.where((p.z == 3) | (p.z == 0), 1, 0))
+    pl.semaphore_wait(barrier, 9 + jnp.where((p.z == 3) | (p.z == 0), 1, 0))
 
 
 def unit_scale(values):
@@ -612,11 +609,120 @@
     return r * e - values * r**3 * jnp.mean(e * values, axis=-1, keepdims=True)
 
 
+def column(gain):
+    row = gain[...].astype(f32).reshape(1, 64)
+    places = [lax.broadcasted_iota(jnp.int32, (64, 64), k) for k in range(2)]
+    return jnp.sum(jnp.where(places[0] == places[1], row, 0.0), axis=1, keepdims=True)
+
+
+def pack_attn(gain, query, key, value, pack):
+    for i, ref in enumerate((query, key, value)):
+        scaled = (ref[...].astype(f32) * gain).astype(bf16)
+        for k in range(2):
+            pack(k)[:, 256 * i : 256 * i + 256] = scaled[:, 256 * k : 256 * k + 256]
+
+
+def pack_out(out, pack):
+    for k in range(2):
+        pack(k)[...] = out[:, 256 * k : 256 * k + 256]
+
+
+def pack_ff(gain, gate, up, down, pack_gu, pack_d):
+    zeros = jnp.zeros((64, 16), f32)
+    for k in range(2):
+        start = 688 * k
+        tails = []
+        for i, ref in enumerate((gate, up)):
+            part = ref[:, start : start + 640].astype(f32) * gain
+            pack_gu(k)[:, 640 * i : 640 * i + 640] = part.astype(bf16)
+            tails += [ref[:, start + 640 : start + 688].astype(f32) * gain, zeros]
+        pack_gu(k)[:, 1280:] = jnp.concatenate(tails, axis=1).astype(bf16)
+        part = down[:, start : start + 688].astype(f32)
+        pack_d(k)[...] = jnp.concatenate([part, jnp.zeros((64, 80), f32)], axis=1).astype(bf16)
+
+
+def row_dots(weight, grads):
+    return jnp.sum(weight.astype(f32) * grads.astype(f32), axis=1, keepdims=True)
+
+
+def final_kernel(
+    result_in, input_in, fin_gu, fin_d, fin_q, fin_o, sums, gain_attn, gain_mlp,
+    result, input_grad, g_attn, query, key, value, out, g_mlp, gate, up, down,
+    hold, sems,
+):
+    loads = [pltpu.make_async_copy(ref, hold.at[k], sems.at[k]) for k, ref in enumerate((result_in, input_in))]
+    for copy in loads:
+        copy.start()
+    attn, mlp = column(gain_attn), column(gain_mlp)
+    for i, ref in enumerate((query, key, value)):
+        for k in range(2):
+            ref[:, 256 * k : 256 * k + 256] = fin_q[k, :, 256 * i : 256 * i + 256].astype(f32) * attn
+    for k in range(2):
+        out[:, 256 * k : 256 * k + 256] = fin_o[k].astype(f32)
+        down[:, 688 * k : 688 * k + 688] = fin_d[k, :, :688].astype(f32)
+        tail = fin_gu[k, :, 1280:].astype(f32) * mlp
+        for i, ref in enumerate((gate, up)):
+            ref[:, 688 * k : 688 * k + 640] = fin_gu[k, :, 640 * i : 640 * i + 640].astype(f32) * mlp
+            ref[:, 688 * k + 640 : 688 * k + 688] = tail[:, 64 * i : 64 * i + 48]
+    turned = sums[...].T
+    g_attn[...] = turned[0:1]
+    g_mlp[...] = turned[1:2]
+    stores = [pltpu.make_async_copy(hold.at[k], ref, sems.at[2 + k]) for k, ref in enumerate((result, input_grad))]
+    for k in range(2):
+        loads[k].wait()
+        stores[k].start()
+    for copy in stores:
+        copy.wait()
+
+
+def final_call(result, input_grad, fin_gu, fin_d, fin_q, fin_o, sums, gain_attn, gain_mlp):
+    sds = jax.ShapeDtypeStruct
+    vmem = pl.BlockSpec(memory_space=pltpu.VMEM)
+    whole = (2, 2, OWNED, 2048)
+    outs = pl.pallas_call(
+        final_kernel,
+        out_shape=(
+            sds(whole, bf16),
+            sds(whole, bf16),
+            sds((1, 64), f32),
+            sds((64, 512), f32),
+            sds((64, 512), f32),
+            sds((64, 512), f32),
+            sds((64, 512), f32),
+            sds((1, 64), f32),
+            sds((64, 1376), f32),
+            sds((64, 1376), f32),
+            sds((64, 1376), f32),
+        ),
+        in_specs=[ANY] * 2 + [vmem] * 7,
+        out_specs=[ANY] * 2 + [vmem] * 9,
+        scratch_shapes=[pltpu.VMEM((2,) + whole, bf16), pltpu.SemaphoreType.DMA((4,))],
+        compiler_params=pltpu.CompilerParams(vmem_limit_bytes=62 * 2**20),
+        name="final",
+    )(result, input_grad, fin_gu, fin_d, fin_q, fin_o, sums, gain_attn, gain_mlp)
+    result, input_grad, g_attn, query, key, value, out, g_mlp, gate, up, down = outs
+    return (
+        result.reshape(BLOCK, 2048),
+        input_grad.reshape(BLOCK, 2048),
+        g_attn.reshape(64),
+        query,
+        key,
+        value,
+        out.T,
+        g_mlp.reshape(64),
+        gate,
+        up,
+        down.T,
+    )
+
+
 def block_kernel(
-    lengths, pk_q, pk_o, pk_gu, pk_d, hid, cot_in,
-    result_o, grad_o, fin_gu, fin_d, fin_q, fin_o, xr_o, qm_o,
+    lengths, gain_attn, gain_mlp, w_query, w_key, w_value, w_out, w_gate, w_up, w_down, hid, cot_in,
+    result_o, grad_o, fin_gu_o, fin_d_o, fin_q_o, fin_o_o, sums_o, xr_o, qm_o,
+    raw_g, raw_u, raw_d,
+    fin_gu, fin_d, fin_q, fin_o, sums, sums_in,
     wq, wo, gu, d, nm, cot, act, gg, kv, resid, hid_pair, own, gb,
-    acc, last_kv, tail_out, tail_in, in_gu, in_d, in_q, in_o, in2_gu, in2_d, in2_q, in2_o,
+    last_kv, tail_out, tail_in, in_gu, in_d, in_q, in_o, in2_gu, in2_d, in2_q, in2_o,
     send_c, snd, tmp, recv_c, rcv,
     send_sems, recv_sems, local_sems, group_send, group_recv, ready,
 ):
@@ -635,10 +741,24 @@
     own_hidden = links.local(hid, hidg.at[own_pair])
     load_hid = links.local(hid.at[:, p.c], hid_pair)
     own_cot = links.local(cot_in, cot.at[own_pair])
+    raw_q, raw_k, raw_v, raw_o = (snd.at[0, k] for k in range(4))
+    half = lambda k: pl.ds(64 * k, 64)
+    pk_q, pk_d = (lambda k: act.at[0, 0, half(k)]), (lambda k: act.at[0, 1, half(k)])
+    pk_o, pk_gu = (lambda k: act.at[1, 0, half(k), pl.ds(0, 256)]), (lambda k: gg.at[0, 0, half(k)])
+    raws = ((w_query, raw_q), (w_key, raw_k), (w_value, raw_v), (w_out, raw_o), (w_gate, raw_g), (w_up, raw_u), (w_down, raw_d))
+    loads = [links.local(ref, raw) for ref, raw in raws]
     greet(p)
+    scale_attn, scale_mlp = column(gain_attn), column(gain_mlp)
+    for copy in loads[:4]:
+        copy.wait()
+    pack_attn(scale_attn, raw_q, raw_k, raw_v, pk_q)
+    pack_out(raw_o, pk_o)
     g_q = WeightGather(links, p, pk_q, wq, 384)
     g_o = WeightGather(links, p, pk_o, wo, 128)
     e_hid = BlockExchange(links, p, hid, hidg)
+    for copy in loads[4:]:
+        copy.wait()
+    pack_ff(scale_mlp, raw_g, raw_u, raw_d, pk_gu, pk_d)
     g_q.start0()
     g_o.start0()
     def norm_rows(tile, core):
@@ -673,6 +793,8 @@
     norm_rows(e_hid.near, 1 - p.c)
     g_q.done()
 
+    links.settle([g_q.swap, g_o.swap, g_gu.swap, g_d.swap])
+
     def project(t):
         w = wq[...].reshape(2048, 768)
         out = jnp.dot(xr[t].reshape(256, 2048), w, preferred_element_type=f32).astype(bf16)
@@ -773,13 +895,14 @@
     def group_reduce(k, partial):
         span = pl.ds(5 * PIECES * k, 5 * PIECES)
         return GroupReduce(
-            p, partial, (send_c, recv_c, tmp, snd, rcv, own), (group_send.at[span], group_recv.at[span])
+            p, partial, (send_c, recv_c, tmp.at[pl.ds(0, 4)], snd, rcv, own), (group_send.at[span], group_recv.at[span])
         )
 
     r_branch = group_reduce(0, partial_of(gg, wo, 256, 256))
     r_branch.run(pass_on=False)
-    r_branch.pass_range(0, PIECES)
+    r_branch.pass_range(0, 3)
     g_gu.start3()
+    r_branch.pass_range(3, 4)
     g_d.start3()
     load_hid.wait()
     r_branch.finish()
@@ -892,7 +1015,7 @@
     def block_reduce(k, partial, moving, extra=None):
         span = pl.ds(5 * PIECES * k, 5 * PIECES)
         sems = (group_send.at[span], group_recv.at[span])
-        return BlockReduce(p, partial, (send_c, recv_c, tmp, moving), sems, extra)
+        return BlockReduce(p, partial, (send_c, recv_c, tmp.at[pl.ds(0, 4)], moving), sems, extra)
 
     r_out = block_reduce(2, partial_of(act, d, 768), nm, resid)
     r_out.run(launch=False, pass_on=False)
@@ -912,7 +1035,7 @@
     tails = []
 
     def attend_back(block):
-        acc[...] = jnp.zeros_like(acc)
+        tmp[...] = jnp.zeros_like(tmp)
 
         def chunk_body(chunk, _):
             x, core = block * 2 + chunk // 2, chunk % 2
@@ -933,21 +1056,23 @@
                 act[x, core, :, lane : lane + 128] = grad_query.astype(bf16)
                 grad_keys = lax.dot_general(grad_scores, query, LEFT_TURNED, preferred_element_type=f32)
                 grad_values = lax.dot_general(probs_low, grad, LEFT_TURNED, preferred_element_type=f32)
-                acc[rows, lane : lane + 128] += grad_keys * SCALE
-                acc[rows, lane + 256 : lane + 384] += grad_values
+                for start, value in ((lane, grad_keys * SCALE), (lane + 256, grad_values)):
+                    tmp[chunk, :, start : start + 128] += value[:128]
+                    tmp[chunk + 1, 0:64, start : start + 128] += value[128:]
             return 0
 
         chunk_body(0, 0)
-        tail_out[block] = acc[0:WINDOW].astype(bf16)
+        tail_out[block] = tmp[0, 0:WINDOW].astype(bf16)
         to_y = jnp.where(block == 0, (p.y + 4 - first) % 4, p.y)
         slot = jnp.where(block == 0, first, 1 - first)
         tails.append(links.send(tail_out.at[block], tail_in.at[slot], p.at(y=to_y, z=(p.z + 3) % 4)))
         lax.fori_loop(1, 4, chunk_body, 0)
-        last_kv[block] = acc[BLOCK:]
+        last_kv[block] = tmp[4, 0:WINDOW]
 
         def store(i, _):
-            r = pl.ds(pl.multiple_of(WINDOW + i * 128, 64), 128)
-            act[block * 2 + i // 2, i % 2, :, 256:] = acc[r].astype(bf16)
+            x, core = block * 2 + i // 2, i % 2
+            act[x, core, 0:64, 256:] = tmp[i, WINDOW:].astype(bf16)
+            act[x, core, 64:128, 256:] = tmp[i + 1, 0:WINDOW].astype(bf16)
             return 0
 
         lax.fori_loop(0, 4, store, 0)
@@ -988,6 +1113,7 @@
     r_out.pass_range(2, 3)
     r_out.crossed()
     pl.semaphore_wait(ready.at[1], 3)
+    again = [links.local(ref, raw) for ref, raw in raws[:3]]
     r_attn = block_reduce(3, partial_of(act, wq, 768), cot)
     r_attn.run(pass_on=False)
     r_out.pass_range(3, 4)
@@ -998,7 +1124,7 @@
     w_d.start3()
     w_q = WeightReduce(links, p, wq, in_q, in2_q, fin_q, 384)
     w_q.start0()
-    r_attn.pass_range(0, 1)
+    r_attn.pass_range(0, 2)
     w_o.start2()
     r_out.finish()
     r_out.sent()
@@ -1011,17 +1137,38 @@
     lax.fori_loop(0, 16, result_rows, 0)
     b_out = BlockOut(links, p, nm.at[pl.ds(2, 2), 0], result_o)
     w_d.start4()
-    r_attn.pass_range(1, 2)
     w_q.start1()
+    r_attn.pass_range(2, 3)
     w_o.start3()
-    r_attn.pass_range(2, 3)
+    r_attn.pass_range(3, 4)
     w_q.start2()
     w_o.start4()
-    r_attn.pass_range(3, 4)
     w_q.start3()
     w_q.start4()
     r_attn.finish()
 
+    for item in (w_gu, w_d, w_q, w_o):
+        item.done()
+
+    part_attn, part_mlp = jnp.zeros((64, 1), f32), jnp.zeros((64, 1), f32)
+    for copy in again:
+        copy.wait()
+    for k in range(2):
+        for i, raw in enumerate((raw_q, raw_k, raw_v)):
+            part_attn += row_dots(raw[:, 256 * k : 256 * k + 256], fin_q[k, :, 256 * i : 256 * i + 256])
+        for i, raw in enumerate((raw_g, raw_u)):
+            start = 688 * k
+            part_mlp += row_dots(raw[:, start : start + 640], fin_gu[k, :, 640 * i : 640 * i + 640])
+            tail = slice(1280 + 64 * i, 1328 + 64 * i)
+            part_mlp += row_dots(raw[:, start + 640 : start + 688], fin_gu[k, :, tail])
+    lane = lax.broadcasted_iota(jnp.int32, (64, 128), 1)
+    sums[...] = jnp.where(lane == 0, part_attn, jnp.where(lane == 1, part_mlp, 0.0))
+    others = (sibling, beside, p.at(x=2 * p.xh + 1 - p.xl, c=1 - p.c))
+    shared = [links.send(sums, sums_in.at[k], device) for k, device in enumerate(others)]
+    stored = [
+        links.local(fin, out)
+        for fin, out in ((fin_gu, fin_gu_o), (fin_d, fin_d_o), (fin_q, fin_q_o), (fin_o, fin_o_o))
+    ]
     def input_rows(i, _):
         tile, r = i // 8, pl.ds((i % 8) * 16, 16)
         values = hid_pair[tile, r].astype(f32)
@@ -1031,14 +1178,21 @@
 
     lax.fori_loop(0, 16, input_rows, 0)
     b_in = BlockOut(links, p, hid_pair, grad_o)
-    for item in (b_out, b_in, w_gu, w_d, w_q, w_o):
-        item.done()
+    for copy in shared:
+        copy.wait_recv()
+    links.settle(shared)
+    sums[...] = (sums[...] + sums_in[0]) + (sums_in[1] + sums_in[2])
+    stored.append(links.local(sums, sums_o))
+    for copy in stored:
+        copy.wait()
+    b_out.done()
+    b_in.done()
     r_attn.crossed()
     r_attn.sent()
     links.settle()
 
 
-def block_call(lengths, pk_q, pk_o, pk_gu, pk_d, hid, cot):
+def block_call(lengths, gain_attn, gain_mlp, weights, hid, cot):
     sds = jax.ShapeDtypeStruct
     group = (4, 2, OWNED)
     vm = pltpu.VMEM
@@ -1051,12 +1205,22 @@
             sds((2, 64, 768), bf16),
             sds((2, 64, 768), bf16),
             sds((2, 64, 256), bf16),
+            sds((64, 128), f32),
             sds(group + (2048,), bf16),
             sds(group + (512,), bf16),
         ),
-        in_specs=[pl.BlockSpec(memory_space=pltpu.SMEM)] + [ANY] * 6,
-        out_specs=[ANY] * 8,
+        in_specs=[pl.BlockSpec(memory_space=pltpu.SMEM)] + [pl.BlockSpec(memory_space=pltpu.VMEM)] * 2 + [ANY] * 9,
+        out_specs=[ANY] * 9,
         scratch_shapes=[
+            vm((64, 1376), bf16),
+            vm((64, 1376), bf16),
+            vm((64, 1376), bf16),
+            vm((2, 64, 1408), bf16),
+            vm((2, 64, 768), bf16),
+            vm((2, 64, 768), bf16),
+            vm((2, 64, 256), bf16),
+            vm((64, 128), f32),
+            vm((3, 64, 128), f32),
             vm((4, 2, 4, 64, 768), bf16),
             vm((4, 2, 4, 64, 256), bf16),
             vm((4, 2, 4, 64, 1408), bf16),
@@ -1070,7 +1234,6 @@
             vm((2, OWNED, 2048), bf16),
             vm((OWNED, 2048), f32),
             vm(group + (2048,), bf16),
-            vm((BLOCK + WINDOW, 512), f32),
             vm((2, WINDOW, 512), f32),
             vm((2, WINDOW, 512), bf16),
             vm((2, WINDOW, 512), bf16),
@@ -1084,12 +1247,12 @@
             vm((6, 64, 256), bf16),
             vm((2, 4, OWNED, WIDE), bf16),
             vm((PIECES, 6, 64, WIDE), bf16),
-            vm((4, OWNED, WIDE), f32),
+            vm((5, OWNED, WIDE), f32),
             vm((PIECES, 4, OWNED, WIDE), bf16),
             vm((PIECES, 6, 64, WIDE), bf16),
             pltpu.SemaphoreType.DMA((220,)),
             pltpu.SemaphoreType.DMA((220,)),
-            pltpu.SemaphoreType.DMA((24,)),
+            pltpu.SemaphoreType.DMA((32,)),
             pltpu.SemaphoreType.DMA((20 * PIECES,)),
             pltpu.SemaphoreType.DMA((20 * PIECES,)),
             pltpu.SemaphoreType.REGULAR((2,)),
@@ -1098,32 +1261,8 @@
             collective_id=0, has_side_effects=True, vmem_limit_bytes=60 * 2**20
         ),
         name="block",
-    )(lengths, pk_q, pk_o, pk_gu, pk_d, hid.reshape(2, 2, OWNED, 2048), cot.reshape(2, 2, OWNED, 2048))
-    return tuple(out.reshape(BLOCK, 2048) for out in outs[:2]) + tuple(outs[2:6])
-
-
-def pack_ff(gate, up, down):
-    def tail(w):
-        return jnp.pad(w[:, 640:], ((0, 0), (0, 16)))
-
-    def one(k):
-        g, u, d = (w[:, k * 688 : (k + 1) * 688] for w in (gate, up, down))
-        return (
-            jnp.concatenate([g[:, :640], u[:, :640], tail(g), tail(u)], axis=1),
-            jnp.pad(d, ((0, 0), (0, 80))),
-        )
-
-    (gu0, d0), (gu1, d1) = one(0), one(1)
-    return jnp.stack([gu0, gu1]), jnp.stack([d0, d1])
-
-
-def pack_attn(query, key, value, out):
-    def one(k):
-        part = slice(k * 256, (k + 1) * 256)
-        return jnp.concatenate([query[:, part], key[:, part], value[:, part]], axis=1), out[:, part]
-
-    (q0, o0), (q1, o1) = one(0), one(1)
-    return jnp.stack([q0, q1]), jnp.stack([o0, o1])
+    )(lengths, gain_attn, gain_mlp, *weights, hid.reshape(2, 2, OWNED, 2048), cot.reshape(2, 2, OWNED, 2048))
+    return outs[:7]
 
 
 def per_device(
@@ -1140,45 +1279,15 @@
     lengths,
     cotangent,
 ):
-    gain_attn = norm_gain_attn.astype(f32)[:, None]
-    gain_mlp = norm_gain_mlp.astype(f32)[:, None]
-    scaled = lambda w, g: (w.astype(f32) * g).astype(bf16)
-    pk_q, pk_o = pack_attn(
-        scaled(w_query, gain_attn), scaled(w_key, gain_attn), scaled(w_value, gain_attn), w_out.T
+    outs = block_call(
+        lengths,
+        norm_gain_attn,
+        norm_gain_mlp,
+        (w_query, w_key, w_value, w_out.T, w_gate, w_up, w_down.T),
+        hidden_in,
+        cotangent,
     )
-    pk_gu, pk_d = pack_ff(scaled(w_gate, gain_mlp), scaled(w_up, gain_mlp), w_down.T)
-    result, input_grad, fin_gu, fin_d, fin_q, fin_o = block_call(
-        lengths, pk_q, pk_o, pk_gu, pk_d, hidden_in, cotangent
-    )
-
-    def joined(fin, *spans):
-        return jnp.concatenate([fin[k][:, s] for k in range(2) for s in spans], axis=1).astype(f32)
-
-    dq, dk, dv = (joined(fin_q, slice(256 * i, 256 * i + 256)) for i in range(3))
-    dg = joined(fin_gu, slice(0, 640), slice(1280, 1328))
-    du = joined(fin_gu, slice(640, 1280), slice(1344, 1392))
-
-    def dots(pairs):
-        return sum(jnp.sum(w.astype(f32) * g, axis=1) for w, g in pairs)
-
-    grads_gain = jnp.stack(
-        [dots([(w_query, dq), (w_key, dk), (w_value, dv)]), dots([(w_gate, dg), (w_up, du)])]
-    )
-    grads_gain = grads_gain + flip(grads_gain, "xl")
-    grads_gain = grads_gain + flip(grads_gain, "c")
-    return (
-        result,
-        input_grad,
-        grads_gain[0],
-        dq * gain_attn,
-        dk * gain_attn,
-        dv * gain_attn,
-        joined(fin_o, slice(0, 256)).T,
-        grads_gain[1],
-        dg * gain_mlp,
-        du * gain_mlp,
-        joined(fin_d, slice(0, 688)).T,
-    )
+    return final_call(*outs, norm_gain_attn, norm_gain_mlp)
 
 
 def solution(mesh):

time: 247 us -> 231 us (0.935)
  local copies, waits for them, and re-layouts: 11.8 us -> 0 us
  other arithmetic: 11.4 us -> 0 us
  Pallas kernels: 219 us -> 230 us
  starting transfers between devices: 2.7 us -> 0 us
    pallas_call x0 -> x1, Pallas kernels: none -> 6.06 us  [final_call(): pl.pallas_call(final_kernel, out_shape=(sds(whole, bf16), sds(whole, bf16...]
    pallas_call x1, Pallas kernels: 219 us -> 224 us  [block_call(): pl.pallas_call(block_kernel, out_shape=(sds((2, 2, OWNED, 2048), bf16), s...]
    unnamed x28 -> x0, local copies, waits for them, and re-layouts: 3.73 us -> none
    mul x2 -> x0, other arithmetic: 3.53 us -> none  [the longest x1 1.78 us: per_device(): du * gain_mlp]
    convert_element_type x4 -> x0, other arithmetic: 3.5 us -> none  [the longest x2 2.14 us: per_device(): scaled = lambda w, g: (w.astype(f32) * g).astype(bf16)]
    another operation x8 -> x0, other arithmetic: 2.86 us -> none  [the longest x3 1.5 us: pack_ff(): return (jnp.stack([gu0, gu1]), jnp.stack([d0, d1]))]
    ppermute x2 -> x0, starting transfers between devices: 2.7 us -> none  [flip(): return lax.ppermute(value, axis, [(0, 1), (1, 0)])]
    slice x11 -> x0, local copies, waits for them, and re-layouts: 2.62 us -> none  [the longest x6 1.42 us: joined(): fin[k][:, s]]
  transfers between devices with their start and end apart: 2 -> 0, of which waited for: 2 -> 0; matrix products, arithmetic and copies ran while one was open for 1% -> 0% of each run, Pallas kernels for 0% -> 0%
where the time goes in v6:
time: 231 us
  Pallas kernels  230 us (100%)
    pallas_call x1, Pallas kernels, block_call(): pl.pallas_call(block_kernel, out_shape=(sds((2, 2, OWNED, 2048), bf16), s...  224 us
    pallas_call x1, Pallas kernels, final_call(): pl.pallas_call(final_kernel, out_shape=(sds(whole, bf16), sds(whole, bf16...  6.06 us

profile of v6, /device:TPU:1, one launch (start us, length us, event | category | flops | bytes accessed | tf_op | source)
XLA Modules:
  0.0 230.7 jit_solution(3963243837087826975)
XLA Ops:
  0.6 223.9 %block.1 = (bf16[2,2,128,2048]{3,2,1,0:T(8,128)(2,1)}, bf16[2,2,128,2048]{3,2,1,0:T(8,128)(2,1)}, bf16[2,64,1408]{2,1,0:T(8,128)(2,1)}, bf16[2,64,768]{2,1,0:T(8...) custom-call(s32[3]{0:T(128)} %lengths.1, ...), custom_call_target="tpu_custom_call" | custom-call | tf_op jit(solution)/shard_map/block/pallas_call | solution.py:1199
  224.5 6.1 %final.1 = (bf16[2,2,128,2048]{3,2,1,0:T(8,128)(2,1)}, bf16[2,2,128,2048]{3,2,1,0:T(8,128)(2,1)}, f32[1,64]{1,0:T(1,128)}, f32[64,512]{1,0:T(8,128)}, f32[64,512...) custom-call(bf16[2,2,128,2048]{3,2,1,0:T(8,128)(2,1)} %get-tuple-ele, ...), custom_call_target="tpu_custom_call" | custom-call | tf_op jit(solution)/shard_map/final/pallas_call | solution.py:682

commit v7 on v6

--- a/solution.py
+++ b/solution.py
@@ -78,8 +78,8 @@
 
 
 class WeightGather:
-    def __init__(self, links, place, pack, whole, cut):
-        self.links, self.place, self.whole = links, place, whole
+    def __init__(self, links, place, pack, whole, cut, direct=False):
+        self.links, self.place, self.whole, self.direct = links, place, whole, direct
         cols = whole.shape[-1]
         self.parts = (pl.ds(0, cut), pl.ds(cut, cols - cut))
         self.swap = links.send(
@@ -117,8 +117,15 @@
             (w.at[p.y, :, p.z, :, first], "z"),
             (w.at[p.y, :, p.z, :, second], "y"),
         )
+        if self.direct:
+            self.got += [
+                self.send(w.at[p.y, :, p.z, :, first], p.at(z=(p.z + 2) % 4)),
+                self.send(w.at[p.y, :, p.z, :, second], p.at(y=(p.y + 2) % 4)),
+            ]
 
     def start1(self):
+        if self.direct:
+            return
         p, w = self.place, self.whole
         first, second = self.parts
         self.wait()
@@ -167,6 +174,8 @@
         p.at(x=(p.x + 3) % 4),
         p.at(x=(p.x + 2) % 4),
         p.at(c=1 - p.c),
+        p.at(y=(p.y + 2) % 4),
+        p.at(z=(p.z + 2) % 4),
         p.at(x=2 * p.xh + 1 - p.xl, c=1 - p.c),
     )
     for device in partners:
@@ -180,7 +189,7 @@
     def _():
         pl.semaphore_signal(barrier, inc=1, device_id=p.at(y=(p.y + 3) % 4, z=0 * p.z + 3), device_id_type=MESH)
 
-    pl.semaphore_wait(barrier, 9 + jnp.where((p.z == 3) | (p.z == 0), 1, 0))
+    pl.semaphore_wait(barrier, 11 + jnp.where((p.z == 3) | (p.z == 0), 1, 0))
 
 
 def unit_scale(values):
@@ -190,6 +199,7 @@
 class WeightReduce:
     def __init__(self, links, place, total, first_in, second_in, out, cut):
         self.links, self.place, self.total, self.out = links, place, total, out
+        self.copies = []
         self.one, self.two = first_in, second_in
         cols = total.shape[-1]
         self.cols = cols
@@ -200,9 +210,14 @@
         self.next_y, self.prev_y = p.at(y=self.yn), p.at(y=self.yp)
         self.next_z, self.prev_z = p.at(z=self.zn), p.at(z=self.zp)
 
+    def send(self, src, dst, device):
+        copy = self.links.send(src, dst, device)
+        self.copies.append(copy)
+        return copy
+
     def start0(self):
         a, b = self.parts
-        t, one, send = self.total, self.one, self.links.send
+        t, one, send = self.total, self.one, self.send
         self.far = [
             send(t.at[self.yf, 0, :, :, a], one.at[0, :, :, a], self.next_y),
             send(t.at[:, 0, self.zf, :, b], one.at[0, :, :, b], self.next_z),
@@ -229,7 +244,7 @@
 
     def start1(self):
         a, b = self.parts
-        t, one, send = self.total, self.one, self.links.send
+        t, one, send = self.total, self.one, self.send
         yn, yp, zn, zp = self.yn, self.yp, self.zn, self.zp
         self.sums = []
         self.far[0].wait_recv()
@@ -247,7 +262,7 @@
 
     def start2(self):
         a, b = self.parts
-        t, one, two, send = self.total, self.one, self.two, self.links.send
+        t, one, two, send = self.total, self.one, self.two, self.send
         p = self.place
         for copy in self.near + self.sums:
             copy.wait_recv()
@@ -255,18 +270,15 @@
         self.add(lambda i: t.at[p.y, 1, i, :, a], [lambda i: one.at[1, i, :, a], lambda i: one.at[5, i, :, a]], 4)
         self.add(lambda i: t.at[i, 0, p.z, :, b], [lambda i: one.at[3, i, :, b], lambda i: one.at[4, i, :, b]], 4)
         self.add(lambda i: t.at[i, 1, p.z, :, b], [lambda i: one.at[1, i, :, b], lambda i: one.at[5, i, :, b]], 4)
-        self.far = [
-            send(t.at[p.y, 0, self.zf, :, a], two.at[0, :, a], self.next_z),
-            send(t.at[self.yf, 0, p.z, :, b], two.at[0, :, b], self.next_y),
-            send(t.at[p.y, 1, self.zf, :, a], two.at[2, :, a], self.prev_z),
-            send(t.at[self.yf, 1, p.z, :, b], two.at[2, :, b], self.prev_y),
-        ]
-        self.near = [
-            send(t.at[p.y, 1, self.zn, :, a], two.at[1, :, a], self.next_z),
-            send(t.at[self.yn, 1, p.z, :, b], two.at[1, :, b], self.next_y),
-            send(t.at[p.y, 0, self.zp, :, a], two.at[3, :, a], self.prev_z),
-            send(t.at[self.yp, 0, p.z, :, b], two.at[3, :, b], self.prev_y),
-        ]
+        sends = (
+            (t.at[p.y, :, self.zn, :, a], 0, a, self.next_z),
+            (t.at[self.yn, :, p.z, :, b], 0, b, self.next_y),
+            (t.at[p.y, :, self.zp, :, a], 2, a, self.prev_z),
+            (t.at[self.yp, :, p.z, :, b], 2, b, self.prev_y),
+            (t.at[p.y, :, self.zf, :, a], 4, a, p.at(z=self.zf)),
+            (t.at[self.yf, :, p.z, :, b], 4, b, p.at(y=self.yf)),
+        )
+        self.sums = [send(src, two.at[pl.ds(slot, 2), :, lanes], device) for src, slot, lanes, device in sends]
 
     def plus(self, target, *sources):
         value = target[...].astype(f32)
@@ -275,30 +287,16 @@
         target[...] = value.astype(bf16)
 
     def start3(self):
-        a, b = self.parts
-        t, two, send = self.total, self.two, self.links.send
-        p = self.place
-        yn, yp, zn, zp = self.yn, self.yp, self.zn, self.zp
-        self.sums = []
-        for k, ref, lanes, slot, other, device in (
-            (0, t.at[p.y, 0, zn, :, a], a, 0, 4, self.next_z),
-            (1, t.at[yn, 0, p.z, :, b], b, 0, 4, self.next_y),
-            (2, t.at[p.y, 1, zp, :, a], a, 2, 5, self.prev_z),
-            (3, t.at[yp, 1, p.z, :, b], b, 2, 5, self.prev_y),
-        ):
-            self.far[k].wait_recv()
-            self.plus(ref, two.at[slot, :, lanes])
-            self.sums.append(send(ref, two.at[other, :, lanes], device))
-
-    def start4(self):
-        t, two, out = self.total, self.two, self.out
-        p = self.place
-        for copy in self.near + self.sums:
+        p, two = self.place, self.two
+        for copy in self.sums:
             copy.wait_recv()
-        self.plus(t.at[p.y, 0, p.z], two.at[3], two.at[4])
-        self.plus(t.at[p.y, 1, p.z], two.at[1], two.at[5])
-        self.swap = self.links.send(t.at[p.y, 1 - p.xh, p.z], out.at[p.xh], p.at(x=(p.x + 2) % 4))
-        self.mine = self.links.local(t.at[p.y, p.xh, p.z], out.at[p.xh])
+        for half in range(2):
+            self.plus(two.at[half], two.at[2 + half], two.at[4 + half], self.total.at[p.y, half, p.z])
+        self.swap = self.links.send(two.at[1 - p.xh], self.out.at[p.xh], p.at(x=(p.x + 2) % 4))
+        self.mine = self.links.local(two.at[p.xh], self.out.at[p.xh])
+
+    def sent(self):
+        self.links.settle(self.copies)
 
     def done(self):
         self.swap.wait_recv()
@@ -650,10 +648,21 @@
     result, input_grad, g_attn, query, key, value, out, g_mlp, gate, up, down,
     hold, sems,
 ):
-    loads = [pltpu.make_async_copy(ref, hold.at[k], sems.at[k]) for k, ref in enumerate((result_in, input_in))]
+    parts = [(k, i, j) for i in range(2) for j in range(2) for k in range(2)]
+    inputs, outputs = (result_in, input_in), (result, input_grad)
+    loads = [
+        pltpu.make_async_copy(inputs[k].at[i, j], hold.at[k, i, j], sems.at[n]) for n, (k, i, j) in enumerate(parts)
+    ]
+    stores = [
+        pltpu.make_async_copy(hold.at[k, i, j], outputs[k].at[i, j], sems.at[8 + n])
+        for n, (k, i, j) in enumerate(parts)
+    ]
     for copy in loads:
         copy.start()
     attn, mlp = column(gain_attn), column(gain_mlp)
+    for load, store in zip(loads, stores):
+        load.wait()
+        store.start()
     for i, ref in enumerate((query, key, value)):
         for k in range(2):
             ref[:, 256 * k : 256 * k + 256] = fin_q[k, :, 256 * i : 256 * i + 256].astype(f32) * attn
@@ -667,10 +676,6 @@
     turned = sums[...].T
     g_attn[...] = turned[0:1]
     g_mlp[...] = turned[1:2]
-    stores = [pltpu.make_async_copy(hold.at[k], ref, sems.at[2 + k]) for k, ref in enumerate((result, input_grad))]
-    for k in range(2):
-        loads[k].wait()
-        stores[k].start()
     for copy in stores:
         copy.wait()
 
@@ -696,7 +701,7 @@
         ),
         in_specs=[ANY] * 2 + [vmem] * 7,
         out_specs=[ANY] * 2 + [vmem] * 9,
-        scratch_shapes=[pltpu.VMEM((2,) + whole, bf16), pltpu.SemaphoreType.DMA((4,))],
+        scratch_shapes=[pltpu.VMEM((2,) + whole, bf16), pltpu.SemaphoreType.DMA((16,))],
         compiler_params=pltpu.CompilerParams(vmem_limit_bytes=62 * 2**20),
         name="final",
     )(result, input_grad, fin_gu, fin_d, fin_q, fin_o, sums, gain_attn, gain_mlp)
@@ -753,8 +758,8 @@
         copy.wait()
     pack_attn(scale_attn, raw_q, raw_k, raw_v, pk_q)
     pack_out(raw_o, pk_o)
-    g_q = WeightGather(links, p, pk_q, wq, 384)
-    g_o = WeightGather(links, p, pk_o, wo, 128)
+    g_q = WeightGather(links, p, pk_q, wq, 384, direct=True)
+    g_o = WeightGather(links, p, pk_o, wo, 128, direct=True)
     e_hid = BlockExchange(links, p, hid, hidg)
     for copy in loads[4:]:
         copy.wait()
@@ -775,10 +780,8 @@
 
     own_hidden.wait()
     lax.fori_loop(0, 4, norm_own, 0)
-    g_q.start1()
-    g_o.start1()
+    g_q.start2()
     e_hid.forward(0)
-    g_q.start2()
     g_gu = WeightGather(links, p, pk_gu, gu, 768)
     g_d = WeightGather(links, p, pk_d, d, 384)
     e_hid.forward(1)
@@ -809,8 +812,6 @@
     g_o.start3()
     e_hid.share_next()
     norm_rows(e_hid.next, p.c)
-    g_gu.start1()
-    g_d.start1()
     e_cot.forward(0)
     e_hid.done(1)
     norm_rows(e_hid.next, 1 - p.c)
@@ -865,9 +866,10 @@
 
     e_cot.forward(1)
     e_cot.share()
-    g_gu.start2()
+    g_gu.start1()
+    g_d.start1()
+    lax.fori_loop(0, 6, inner, 0)
     g_d.start2()
-    lax.fori_loop(0, 6, inner, 0)
     e_cot.share_next()
     for copy in tails:
         copy.wait_recv()
@@ -878,6 +880,7 @@
 
     lax.fori_loop(0, 2, first_chunk, 0)
     mixed = gg.at[:, :, :, pl.ds(256, 256)]
+    g_gu.start2()
     g_o.done()
     xr_spill.wait()
 
@@ -901,9 +904,8 @@
     r_branch = group_reduce(0, partial_of(gg, wo, 256, 256))
     r_branch.run(pass_on=False)
     r_branch.pass_range(0, 3)
-    g_gu.start3()
+    g_d.start3()
     r_branch.pass_range(3, 4)
-    g_d.start3()
     load_hid.wait()
     r_branch.finish()
 
@@ -917,19 +919,27 @@
     lax.fori_loop(0, OWNED // 16, resid_rows, 0)
     g_nm = GroupGather(links, p, nm)
     g_nm.start()
+    g_gu.start3()
     q_spill = links.local(gg.at[:, :, :, pl.ds(0, 512)], qm_o)
-    g_gu.done()
     own_cot.wait()
     for k in range(2):
         e_cot.done(k)
+    g_d.done()
+
+    def grad_activated(t, _):
+        out = jnp.dot(cot[t].reshape(256, 2048), d[...].reshape(2048, 768), preferred_element_type=f32)
+        act[t] = out.astype(bf16).reshape(2, OWNED, 768)
+        return 0
+
+    lax.fori_loop(0, 4, grad_activated, 0)
     q_spill.wait()
-    g_d.done()
+    g_nm.forward()
+    g_gu.done()
     g_nm.ready(0)
 
     def feed(k, _):
         @pl.when(k == 1)
         def _():
-            g_nm.forward()
             g_nm.share_near()
             g_nm.ready(1)
 
@@ -944,7 +954,7 @@
 
         t = (p.x + jnp.where(k == 0, 0, jnp.where(k == 1, 3, k - 1))) % 4
         part = jnp.dot(nm[t].reshape(256, 2048), gu[...].reshape(2048, 1408), preferred_element_type=f32)
-        back = jnp.dot(cot[t].reshape(256, 2048), d[...].reshape(2048, 768), preferred_element_type=f32)
+        back = act[t].reshape(256, 768).astype(f32)
         tail = part[:, 1280:]
         flipped = pltpu.roll(tail, 64, 1)
         lane = lax.broadcasted_iota(jnp.int32, (256, 128), 1)
@@ -1095,7 +1105,6 @@
     grad_mixed(2 * (1 - p.xh) + 1)
     attend_back(1 - p.xh)
     r_out.pass_range(1, 2)
-    w_gu.start3()
     grads_into(wo, gb, mixed, 256)
     own[...] = gb[2 * p.xh, p.c].astype(f32)
     resid[...] = gb[2 * p.xh + 1, p.c].astype(f32)
@@ -1109,7 +1118,7 @@
     w_d.start1()
     w_o = WeightReduce(links, p, wo, in_o, in2_o, fin_o, 128)
     w_o.start0()
-    w_gu.start4()
+    w_gu.start3()
     r_out.pass_range(2, 3)
     r_out.crossed()
     pl.semaphore_wait(ready.at[1], 3)
@@ -1121,7 +1130,6 @@
     w_o.start1()
     load_xr.wait()
     grads_into(wq, gb, act, 768)
-    w_d.start3()
     w_q = WeightReduce(links, p, wq, in_q, in2_q, fin_q, 384)
     w_q.start0()
     r_attn.pass_range(0, 2)
@@ -1136,15 +1144,13 @@
 
     lax.fori_loop(0, 16, result_rows, 0)
     b_out = BlockOut(links, p, nm.at[pl.ds(2, 2), 0], result_o)
-    w_d.start4()
+    w_d.start3()
     w_q.start1()
     r_attn.pass_range(2, 3)
     w_o.start3()
+    w_q.start2()
     r_attn.pass_range(3, 4)
-    w_q.start2()
-    w_o.start4()
     w_q.start3()
-    w_q.start4()
     r_attn.finish()
 
     for item in (w_gu, w_d, w_q, w_o):

time: 231 us -> 226 us (0.978)
  Pallas kernels: 230 us -> 225 us
    pallas_call x1, Pallas kernels: 224 us -> 219 us  [block_call(): pl.pallas_call(block_kernel, out_shape=(sds((2, 2, OWNED, 2048), bf16), s...]
where the time goes in v7:
time: 226 us
  Pallas kernels  225 us (100%)
    pallas_call x1, Pallas kernels, block_call(): pl.pallas_call(block_kernel, out_shape=(sds((2, 2, OWNED, 2048), bf16), s...  219 us
    pallas_call x1, Pallas kernels, final_call(): pl.pallas_call(final_kernel, out_shape=(sds(whole, bf16), sds(whole, bf16...  6 us

profile of v7, /device:TPU:1, one launch (start us, length us, event | category | flops | bytes accessed | tf_op | source)
XLA Modules:
  0.0 225.8 jit_solution(651081878104935122)
XLA Ops:
  0.6 219.0 %block.1 = (bf16[2,2,128,2048]{3,2,1,0:T(8,128)(2,1)}, bf16[2,2,128,2048]{3,2,1,0:T(8,128)(2,1)}, bf16[2,64,1408]{2,1,0:T(8,128)(2,1)}, bf16[2,64,768]{2,1,0:T(8...) custom-call(s32[3]{0:T(128)} %lengths.1, ...), custom_call_target="tpu_custom_call" | custom-call | tf_op jit(solution)/shard_map/block/pallas_call | solution.py:1205
  219.7 6.0 %final.1 = (bf16[2,2,128,2048]{3,2,1,0:T(8,128)(2,1)}, bf16[2,2,128,2048]{3,2,1,0:T(8,128)(2,1)}, f32[1,64]{1,0:T(1,128)}, f32[64,512]{1,0:T(8,128)}, f32[64,512...) custom-call(bf16[2,2,128,2048]{3,2,1,0:T(8,128)(2,1)} %get-tuple-ele, ...), custom_call_target="tpu_custom_call" | custom-call | tf_op jit(solution)/shard_map/final/pallas_call | solution.py:687

commit v8 on v7

--- a/solution.py
+++ b/solution.py
@@ -86,6 +86,20 @@
             pack(1 - place.xh), whole.at[place.y, place.xh, place.z], place.at(x=(place.x + 2) % 4)
         )
         self.mine = links.local(pack(place.xh), whole.at[place.y, place.xh, place.z])
+        if direct:
+            self.got = self.spread(pack(place.xh), place.xh)
+            self.early = list(self.got)
+
+    def spread(self, ref, half):
+        p, w = self.place, self.whole
+        devices = [
+            (p.at(z=(p.z + k) % 4), p.at(y=(p.y + k) % 4)) for k in (1, 3, 2)
+        ]
+        copies = []
+        for along_z, along_y in devices:
+            for lanes, device in zip(self.parts, (along_z, along_y)):
+                copies.append(self.links.send(ref.at[:, lanes], w.at[p.y, half, p.z, :, lanes], device))
+        return copies
 
     def send(self, ref, device):
         return self.links.send(ref, ref, device)
@@ -113,15 +127,13 @@
         first, second = self.parts
         self.swap.wait_recv()
         self.mine.wait()
+        if self.direct:
+            self.got += self.spread(w.at[p.y, 1 - p.xh, p.z], 1 - p.xh)
+            return
         self.near(
             (w.at[p.y, :, p.z, :, first], "z"),
             (w.at[p.y, :, p.z, :, second], "y"),
         )
-        if self.direct:
-            self.got += [
-                self.send(w.at[p.y, :, p.z, :, first], p.at(z=(p.z + 2) % 4)),
-                self.send(w.at[p.y, :, p.z, :, second], p.at(y=(p.y + 2) % 4)),
-            ]
 
     def start1(self):
         if self.direct:
@@ -644,12 +656,14 @@
 
 
 def final_kernel(
-    result_in, input_in, fin_gu, fin_d, fin_q, fin_o, sums, gain_attn, gain_mlp,
-    result, input_grad, g_attn, query, key, value, out, g_mlp, gate, up, down,
-    hold, sems,
+    result_in, input_in, fin_gu_in, fin_d_in, fin_q_in, fin_o_in, sums_in, gain_attn, gain_mlp,
+    result, input_grad, g_attn_out, query_out, key_out, value_out, out_out, g_mlp_out, gate_out, up_out, down_out,
+    hold, fin_gu, fin_d, fin_q, fin_o, sums, g_attn, query, key, value, out, g_mlp, gate, up, down, sems, small_sems,
 ):
     parts = [(k, i, j) for i in range(2) for j in range(2) for k in range(2)]
     inputs, outputs = (result_in, input_in), (result, input_grad)
+    small = ((fin_q_in, fin_q), (fin_o_in, fin_o), (fin_d_in, fin_d), (fin_gu_in, fin_gu), (sums_in, sums))
+    fetched = [pltpu.make_async_copy(ref, here, small_sems.at[n]) for n, (ref, here) in enumerate(small)]
     loads = [
         pltpu.make_async_copy(inputs[k].at[i, j], hold.at[k, i, j], sems.at[n]) for n, (k, i, j) in enumerate(parts)
     ]
@@ -657,51 +671,79 @@
         pltpu.make_async_copy(hold.at[k, i, j], outputs[k].at[i, j], sems.at[8 + n])
         for n, (k, i, j) in enumerate(parts)
     ]
-    for copy in loads:
+    finished = [
+        pltpu.make_async_copy(here, ref, small_sems.at[5 + n])
+        for n, (here, ref) in enumerate(
+            (
+                (query, query_out),
+                (key, key_out),
+                (value, value_out),
+                (out, out_out),
+                (down, down_out),
+                (gate, gate_out),
+                (up, up_out),
+                (g_attn, g_attn_out),
+                (g_mlp, g_mlp_out),
+            )
+        )
+    ]
+    for copy in fetched + loads:
         copy.start()
     attn, mlp = column(gain_attn), column(gain_mlp)
-    for load, store in zip(loads, stores):
-        load.wait()
-        store.start()
+
+    def hand_over(start):
+        for n in (start, start + 1):
+            loads[n].wait()
+            stores[n].start()
+
+    fetched[0].wait()
     for i, ref in enumerate((query, key, value)):
         for k in range(2):
             ref[:, 256 * k : 256 * k + 256] = fin_q[k, :, 256 * i : 256 * i + 256].astype(f32) * attn
+        finished[i].start()
+    fetched[1].wait()
     for k in range(2):
         out[:, 256 * k : 256 * k + 256] = fin_o[k].astype(f32)
+    finished[3].start()
+    hand_over(0)
+    fetched[2].wait()
+    for k in range(2):
         down[:, 688 * k : 688 * k + 688] = fin_d[k, :, :688].astype(f32)
-        tail = fin_gu[k, :, 1280:].astype(f32) * mlp
-        for i, ref in enumerate((gate, up)):
+    finished[4].start()
+    hand_over(2)
+    fetched[3].wait()
+    for i, ref in enumerate((gate, up)):
+        for k in range(2):
             ref[:, 688 * k : 688 * k + 640] = fin_gu[k, :, 640 * i : 640 * i + 640].astype(f32) * mlp
+            tail = fin_gu[k, :, 1280:].astype(f32) * mlp
             ref[:, 688 * k + 640 : 688 * k + 688] = tail[:, 64 * i : 64 * i + 48]
+        finished[5 + i].start()
+    hand_over(4)
+    fetched[4].wait()
     turned = sums[...].T
     g_attn[...] = turned[0:1]
     g_mlp[...] = turned[1:2]
-    for copy in stores:
+    for copy in finished[7:]:
+        copy.start()
+    hand_over(6)
+    for copy in stores + finished:
         copy.wait()
 
 
 def final_call(result, input_grad, fin_gu, fin_d, fin_q, fin_o, sums, gain_attn, gain_mlp):
-    sds = jax.ShapeDtypeStruct
+    sds, vm = jax.ShapeDtypeStruct, pltpu.VMEM
     vmem = pl.BlockSpec(memory_space=pltpu.VMEM)
     whole = (2, 2, OWNED, 2048)
+    grads = ((1, 64), (64, 512), (64, 512), (64, 512), (64, 512), (1, 64), (64, 1376), (64, 1376), (64, 1376))
     outs = pl.pallas_call(
         final_kernel,
-        out_shape=(
-            sds(whole, bf16),
-            sds(whole, bf16),
-            sds((1, 64), f32),
-            sds((64, 512), f32),
-            sds((64, 512), f32),
-            sds((64, 512), f32),
-            sds((64, 512), f32),
-            sds((1, 64), f32),
-            sds((64, 1376), f32),
-            sds((64, 1376), f32),
-            sds((64, 1376), f32),
-        ),
-        in_specs=[ANY] * 2 + [vmem] * 7,
-        out_specs=[ANY] * 2 + [vmem] * 9,
-        scratch_shapes=[pltpu.VMEM((2,) + whole, bf16), pltpu.SemaphoreType.DMA((16,))],
+        out_shape=(sds(whole, bf16), sds(whole, bf16)) + tuple(sds(shape, f32) for shape in grads),
+        in_specs=[ANY] * 7 + [vmem] * 2,
+        out_specs=[ANY] * 11,
+        scratch_shapes=[vm((2,) + whole, bf16)]
+        + [vm(ref.shape, ref.dtype) for ref in (fin_gu, fin_d, fin_q, fin_o, sums)]
+        + [vm(shape, f32) for shape in grads]
+        + [pltpu.SemaphoreType.DMA((16,)), pltpu.SemaphoreType.DMA((14,))],
         compiler_params=pltpu.CompilerParams(vmem_limit_bytes=62 * 2**20),
         name="final",
     )(result, input_grad, fin_gu, fin_d, fin_q, fin_o, sums, gain_attn, gain_mlp)
@@ -796,7 +838,7 @@
     norm_rows(e_hid.near, 1 - p.c)
     g_q.done()
 
-    links.settle([g_q.swap, g_o.swap, g_gu.swap, g_d.swap])
+    links.settle([g_q.swap, g_o.swap, g_gu.swap, g_d.swap] + g_q.early + g_o.early)
 
     def project(t):
         w = wq[...].reshape(2048, 768)
@@ -861,16 +903,16 @@
             gg[x, core, :, lane + 256 : lane + 384] = out.astype(bf16)
 
     def inner(i, _):
-        attend(i // 3, i % 3 + 1)
+        for chunk in range(1, 4):
+            attend(i, chunk)
         return 0
 
     e_cot.forward(1)
     e_cot.share()
     g_gu.start1()
     g_d.start1()
-    lax.fori_loop(0, 6, inner, 0)
+    lax.fori_loop(0, 2, inner, 0)
     g_d.start2()
-    e_cot.share_next()
     for copy in tails:
         copy.wait_recv()
 
@@ -903,6 +945,7 @@
 
     r_branch = group_reduce(0, partial_of(gg, wo, 256, 256))
     r_branch.run(pass_on=False)
+    e_cot.share_next()
     r_branch.pass_range(0, 3)
     g_d.start3()
     r_branch.pass_range(3, 4)

time: 226 us -> 226 us (level)
  no operation moved by 1% of the time
where the time goes in v8:
time: 226 us
  Pallas kernels  225 us (100%)
    pallas_call x1, Pallas kernels, block_call(): pl.pallas_call(block_kernel, out_shape=(sds((2, 2, OWNED, 2048), bf16), s...  220 us
    pallas_call x1, Pallas kernels, final_call(): pl.pallas_call(final_kernel, out_shape=(sds(whole, bf16), sds(whole, bf16...  5.18 us

profile of v8, /device:TPU:1, one launch (start us, length us, event | category | flops | bytes accessed | tf_op | source)
XLA Modules:
  0.0 225.6 jit_solution(5927211412374249496)
XLA Ops:
  0.6 219.6 %block.1 = (bf16[2,2,128,2048]{3,2,1,0:T(8,128)(2,1)}, bf16[2,2,128,2048]{3,2,1,0:T(8,128)(2,1)}, bf16[2,64,1408]{2,1,0:T(8,128)(2,1)}, bf16[2,64,768]{2,1,0:T(8...) custom-call(s32[3]{0:T(128)} %lengths.1, ...), custom_call_target="tpu_custom_call" | custom-call | tf_op jit(solution)/shard_map/block/pallas_call | solution.py:1248
  220.2 5.2 %final.1 = (bf16[2,2,128,2048]{3,2,1,0:T(8,128)(2,1)}, bf16[2,2,128,2048]{3,2,1,0:T(8,128)(2,1)}, f32[1,64]{1,0:T(1,128)}, f32[64,512]{1,0:T(8,128)}, f32[64,512...) custom-call(bf16[2,2,128,2048]{3,2,1,0:T(8,128)(2,1)} %get-tuple-ele, ...), custom_call_target="tpu_custom_call" | custom-call | tf_op jit(solution)/shard_map/final/pallas_call | solution.py:738
